TPU v7x, 32 devices: a whole 2x2x4 slice. The times are simulated.
32 devices in a mesh: dp: 8 (over y, x, core), ctx: 4 (over z).
Axes of the slice: x: 2, y: 2, z: 4, core: 2. Of those that a mesh axis runs over, the one named last changes fastest.
Arguments:
- tokens_in: bfloat16 [8, 2048, 1280], P('dp', 'ctx'), may hold values from -6 to 6
- block_ids: int32 [8, 2048], P('dp'), may hold values from 0 to 15, never falling along the last dimension, each value on 1 to 256 neighbouring positions
- w_qkv: bfloat16 [1280, 3840], P('dp'), may hold values from -0.15625 to 0.15625
- w_out: bfloat16 [1280, 1280], P('dp'), may hold values from -1.25 to 1.25
- w_in: bfloat16 [1280, 1280], P('dp'), may hold values from -0.15625 to 0.15625
- w_down: bfloat16 [1280, 1280], P('dp'), may hold values from -0.15625 to 0.15625
- gain_attn: bfloat16 [1280], replicated, may hold values from 0.5 to 1.5
- gain_mlp: bfloat16 [1280], replicated, may hold values from 0.5 to 1.5
- bias_in: bfloat16 [1280], replicated, may hold values from -3 to 3
- bias_down: bfloat16 [1280], replicated, may hold values from -2 to 2
- query_scale: bfloat16 [80], replicated, may hold values from 0 to 1.5
- cotangent: bfloat16 [8, 2048, 1280], P('dp', 'ctx'), may hold values from -6 to 6
Outputs:
- output: bfloat16 [8, 2048, 1280], P('dp', 'ctx')
- grad_tokens: float32 [8, 2048, 1280], P('dp', 'ctx')
- grad_w_qkv: float32 [1280, 3840], P('dp')
- grad_w_out: float32 [1280, 1280], P('dp')
- grad_w_in: float32 [1280, 1280], P('dp')
- grad_w_down: float32 [1280, 1280], P('dp')
- grad_gain_attn: float32 [1280], replicated
- grad_gain_mlp: float32 [1280], replicated
- grad_bias_in: float32 [1280], replicated
- grad_bias_down: float32 [1280], replicated
- grad_query_scale: float32 [80], replicated
Inputs may be any that keep to these rules, and one draw needn't show every extreme that they name: `block_ids`: each sequence's block numbers never fall along positions, start at 0, take every value up to 15, and each block spans 1 to 256 positions.
All inputs are finite; a program needn't handle non-finite values.
Results may differ from a plain program's by a relative error of at most 0.02.
Values may be sent and summed in bfloat16 or wider, within the bound.
No kernel may reach another device: no remote copies, remote signals or barrier semaphores. Data moves between devices by JAX's collectives and lax.ppermute only.
A program may use at most 256 MiB of HBM per device.

v0:
```python
import functools
import math

import jax
import jax.numpy as jnp
import numpy as np
from jax import lax
from jax.experimental import pallas as pl
from jax.experimental.pallas import tpu as pltpu
from jax.sharding import PartitionSpec as P

EPSILON = 1e-06
SOFT_FACTOR = 1.442695041
LOG2E = 1.4426950408889634
MASKED = -1e30
HEADS_AT_ONCE = 4
COST = 1.0
AXES = ("dp", "ctx")
BF = jnp.bfloat16
F32 = jnp.float32


def nn(a, b):
    return lax.dot_general(a, b, (((1,), (0,)), ((), ())), preferred_element_type=F32)


def nt(a, b):
    return lax.dot_general(a, b, (((1,), (1,)), ((), ())), preferred_element_type=F32)


def tile_counts(ids_ref, stretch, tile, tiles):
    low = ids_ref[stretch * tile]
    high = ids_ref[stretch * tile + tile - 1]
    full = jnp.int32(0)
    need = jnp.int32(0)
    for t in range(tiles):
        full += (ids_ref[t * tile + tile - 1] <= low).astype(jnp.int32)
        need += (ids_ref[t * tile] <= high).astype(jnp.int32)
    return full, need


def project_kernel(part, query_slots, n, core_ref, gain_ref, scale_ref, *refs):
    x_refs, w_refs = refs[:n], refs[n : n + 3]
    qt_ref, kt_ref, vt_ref, xt_ref, wt, xs = refs[n + 3 :]
    i = pl.program_id(0)

    @pl.when(i == 0)
    def _():
        for j, ref in enumerate(w_refs):
            wt[j * part : (j + 1) * part, :] = ref[...].T

    for s in range(n):

        @pl.when(i == s)
        def _(s=s):
            xs[...] = x_refs[s][...]

    x = xs[...].astype(F32)
    inverse = lax.rsqrt(jnp.mean(x * x, -1, keepdims=True) + EPSILON)
    xt_ref[...] = (x * inverse * gain_ref[...]).astype(BF).T
    kt_ref[...] = nn(wt[part : 2 * part, :], xt_ref[...]).astype(BF)
    vt_ref[...] = nn(wt[2 * part :, :], xt_ref[...]).astype(BF)

    @pl.when(i < query_slots)
    def _():
        qt_ref[...] = (nn(wt[:part, :], xt_ref[...]) * scale_ref[...]).astype(BF)


def project(slots, w_full, core, gain, scale):
    n = len(slots)
    rows, width = slots[0].shape
    part = width // 2
    query_slots = 2
    once = pl.Buffered(1)
    return pl.pallas_call(
        functools.partial(project_kernel, part, query_slots, n),
        grid_spec=pltpu.PrefetchScalarGridSpec(
            num_scalar_prefetch=1,
            grid=(n,),
            in_specs=[
                pl.BlockSpec((1, width), lambda i, c: (0, 0)),
                pl.BlockSpec((part, 1), lambda i, c: (0, 0)),
                *[pl.BlockSpec((rows, width), lambda i, c: (0, 0), pipeline_mode=once)] * n,
                *[
                    pl.BlockSpec(
                        (width, part), lambda i, c, j=j: (0, 2 * j + c[0]), pipeline_mode=once
                    )
                    for j in range(3)
                ],
            ],
            out_specs=[
                pl.BlockSpec((part, rows), lambda i, c: (0, jnp.minimum(i, query_slots - 1))),
                pl.BlockSpec((part, rows), lambda i, c: (0, i)),
                pl.BlockSpec((part, rows), lambda i, c: (0, i)),
                pl.BlockSpec((width, rows), lambda i, c: (0, i)),
            ],
            scratch_shapes=[pltpu.VMEM((3 * part, width), BF), pltpu.VMEM((rows, width), BF)],
        ),
        out_shape=[
            jax.ShapeDtypeStruct((part, query_slots * rows), BF),
            jax.ShapeDtypeStruct((part, n * rows), BF),
            jax.ShapeDtypeStruct((part, n * rows), BF),
            jax.ShapeDtypeStruct((width, n * rows), BF),
        ],
        compiler_params=pltpu.CompilerParams(vmem_limit_bytes=60 << 20),
        cost_estimate=pl.CostEstimate(
            flops=int(COST * 2 * width * part * rows * (2 * n + query_slots)),
            bytes_accessed=1 << 16,
            transcendentals=0,
        ),
        name="project",
    )(core, gain, scale, *slots, *[w_full] * 3)


def mlp_kernel(
    part, core_ref, near_ref, far_ref, w_ref, x_ref, cot_ref, gain_ref, bin_ref, bdown_ref, out_ref, keep_ref, give_ref,
    gmid_ref, ht_ref, nt_ref, gpre_ref, gml_ref, gain_out, bin_out, bdown_out, middle, normed,
    hidden, slope, g_ref,
):
    width = x_ref.shape[1]
    step = width // 5
    chunks = [slice(c * step, (c + 1) * step) for c in range(5)]
    down, inner, outer = 0, width, 2 * width
    core = core_ref[0]
    near_rows = pl.ds(pl.multiple_of(core * part, part), part)
    far_rows = pl.ds(pl.multiple_of((1 - core) * part, part), part)

    @pl.when(pl.program_id(0) == 0)
    def _():
        for ref in (gain_out, bin_out, bdown_out):
            ref[...] = jnp.zeros(ref.shape, F32)

    near, far = near_ref[...].T, far_ref[...].T
    for cols in chunks:
        at = slice(outer + cols.start, outer + cols.stop)
        middle[:, cols] = (
            x_ref[:, cols].astype(F32) + nn(near, w_ref[near_rows, at]) + nn(far, w_ref[far_rows, at])
        )
    mid = middle[...]
    inverse = lax.rsqrt(jnp.mean(mid * mid, -1, keepdims=True) + EPSILON)
    normed[...] = (mid * inverse * gain_ref[...]).astype(BF)
    nt_ref[...] = normed[...].T
    for cols in chunks:
        at = slice(inner + cols.start, inner + cols.stop)
        pre = nn(normed[...], w_ref[:, at]) + bin_ref[:, cols]
        sigma = 1.0 / (1.0 + jnp.exp(-pre))
        hidden[:, cols] = (pre * sigma).astype(BF)
        slope[:, cols] = sigma * (1.0 + pre * (1.0 - sigma))
    ht_ref[...] = hidden[...].T
    for cols in chunks:
        at = slice(down + cols.start, down + cols.stop)
        out_ref[:, cols] = (
            middle[:, cols] + nn(hidden[...], w_ref[:, at]) + bdown_ref[:, cols]
        ).astype(BF)
    for cols in chunks:
        gpre_ref[:, cols] = (
            nt(cot_ref[...], w_ref[cols, down : down + width]) * slope[:, cols]
        ).astype(BF)
    for cols in chunks:
        g_ref[:, cols] = nt(gpre_ref[...], w_ref[cols, inner : inner + width])
    bin_out[...] += jnp.sum(gpre_ref[...].astype(F32), 0, keepdims=True)
    cot = cot_ref[...].astype(F32)
    bdown_out[...] += jnp.sum(cot, 0, keepdims=True)
    turned = middle[...] * inverse
    gn = g_ref[...] * turned
    gain_out[...] += jnp.sum(gn, 0, keepdims=True)
    mean = jnp.mean(gn * gain_ref[...], -1, keepdims=True)
    gmid = cot + inverse * (g_ref[...] * gain_ref[...] - turned * mean)
    gmid_ref[...] = gmid
    gml_ref[...] = gmid.astype(BF)
    low = gml_ref[...]
    keep_ref[...] = nt(w_ref[near_rows, outer : outer + width], low).astype(BF)
    give_ref[...] = nt(w_ref[far_rows, outer : outer + width], low).astype(BF)


def mlp(near, far, weights, x, cot, core, gain, bias_in, bias_down):
    part, rows = far.shape
    width = x.shape[1]
    tile = 256
    once = pl.Buffered(1)
    row = pl.BlockSpec((tile, width), lambda i, c: (i, 0))
    feature = pl.BlockSpec((part, tile), lambda i, c: (0, i))
    wide = pl.BlockSpec((width, tile), lambda i, c: (0, i))
    vector = pl.BlockSpec((1, width), lambda i, c: (0, 0))
    return pl.pallas_call(
        functools.partial(mlp_kernel, part),
        grid_spec=pltpu.PrefetchScalarGridSpec(
            num_scalar_prefetch=1,
            grid=(rows // tile,),
            in_specs=[
                feature,
                feature,
                pl.BlockSpec(weights.shape, lambda i, c: (0, 0), pipeline_mode=once),
                row, row, vector, vector, vector,
            ],
            out_specs=[
                row, feature, feature, row, wide, wide, row, row, vector, vector, vector
            ],
            scratch_shapes=[
                pltpu.VMEM((tile, width), F32),
                pltpu.VMEM((tile, width), BF),
                pltpu.VMEM((tile, width), BF),
                pltpu.VMEM((tile, width), F32),
                pltpu.VMEM((tile, width), F32),
            ],
        ),
        out_shape=[
            jax.ShapeDtypeStruct((rows, width), BF),
            jax.ShapeDtypeStruct((part, rows), BF),
            jax.ShapeDtypeStruct((part, rows), BF),
            jax.ShapeDtypeStruct((rows, width), F32),
            jax.ShapeDtypeStruct((width, rows), BF),
            jax.ShapeDtypeStruct((width, rows), BF),
            jax.ShapeDtypeStruct((rows, width), BF),
            jax.ShapeDtypeStruct((rows, width), BF),
            jax.ShapeDtypeStruct((1, width), F32),
            jax.ShapeDtypeStruct((1, width), F32),
            jax.ShapeDtypeStruct((1, width), F32),
        ],
        compiler_params=pltpu.CompilerParams(vmem_limit_bytes=60 << 20),
        cost_estimate=pl.CostEstimate(
            flops=int(COST * 12 * rows * width * width), bytes_accessed=1 << 16, transcendentals=0
        ),
        name="mlp",
    )(core, near, far, weights, x, cot, gain, bias_in, bias_down)


def mlp_weight_kernel(
    core_ref, near_ref, far_ref, ht_ref, nt_ref, cot_ref, gpre_ref, gml_ref, out_ref
):
    which, part_at = pl.program_id(0), pl.program_id(1)

    @pl.when(which == 0)
    def _():
        out_ref[...] = nn(ht_ref[...], cot_ref[...]).astype(BF)

    @pl.when(which == 1)
    def _():
        out_ref[...] = nn(nt_ref[...], gpre_ref[...]).astype(BF)

    @pl.when((which == 2) & (part_at == core_ref[0]))
    def _():
        out_ref[...] = nn(near_ref[...], gml_ref[...]).astype(BF)

    @pl.when((which == 2) & (part_at != core_ref[0]))
    def _():
        out_ref[...] = nn(far_ref[...], gml_ref[...]).astype(BF)


def mlp_weights(near, far, ht, nrt, cot, gpre, gml, core):
    part, rows = far.shape
    width = cot.shape[1]
    once = pl.Buffered(1)

    def whole(shape):
        return pl.BlockSpec(shape, lambda j, r, c: (0,) * len(shape), pipeline_mode=once)

    return pl.pallas_call(
        mlp_weight_kernel,
        grid_spec=pltpu.PrefetchScalarGridSpec(
            num_scalar_prefetch=1,
            grid=(3, 2),
            in_specs=[
                whole((part, rows)),
                whole((part, rows)),
                pl.BlockSpec((part, rows), lambda j, r, c: (jnp.where(j == 0, r, 1), 0)),
                pl.BlockSpec((part, rows), lambda j, r, c: (jnp.where(j == 1, r, j // 2), 0)),
                whole((rows, width)),
                whole((rows, width)),
                whole((rows, width)),
            ],
            out_specs=pl.BlockSpec((part, width), lambda j, r, c: (r, j)),
        ),
        out_shape=jax.ShapeDtypeStruct((width, 3 * width), BF),
        compiler_params=pltpu.CompilerParams(vmem_limit_bytes=60 << 20),
        cost_estimate=pl.CostEstimate(
            flops=6 * rows * width * width, bytes_accessed=20 << 20, transcendentals=0
        ),
        name="mlp_weights",
    )(core, near, far, ht, nrt, cot, gpre, gml)


def load_keys(ref, place_ref, hd, tile, group, knat, kt=None):
    tiles = ref.shape[1] // tile
    for b in range(tiles):
        stretch = place_ref[tiles + b]
        piece = ref[:, b * tile : (b + 1) * tile]
        if kt is not None:
            kt[stretch] = piece
        if knat is not None:
            for h in range(group):
                knat[h, stretch] = piece[h * hd : (h + 1) * hd, :].T


def forward_kernel(
    hd, tile, ids_ref, place_ref, row_ref, col_ref, qt_ref, kt_ref, vt_ref, near_ref, far_ref,
    lse_ref, knat, vt, acc, m_ref, l_ref,
):
    group = qt_ref.shape[0] // hd
    tiles = vt.shape[0]
    load_keys(kt_ref, place_ref, hd, tile, group, knat)
    load_keys(vt_ref, place_ref, hd, tile, group, None, vt)
    per_half = near_ref.shape[1] // tile

    def one_tile(qi, carry):
        stretch = place_ref[tiles + qi]
        full, need = tile_counts(ids_ref, stretch, tile, tiles)
        qcol = pl.ds(pl.multiple_of(qi * tile, tile), tile)
        qpos = pl.ds(pl.multiple_of(stretch * tile, tile), tile)
        m_ref[...] = jnp.full(m_ref.shape, MASKED, F32)
        l_ref[...] = jnp.zeros(l_ref.shape, F32)
        acc[...] = jnp.zeros(acc.shape, F32)

        def step(ts, masked):
            if masked:
                allowed = [
                    col_ref[pl.ds(pl.multiple_of(t * tile, tile), tile), :] <= row_ref[:, qpos]
                    for t in ts
                ]
            scores = [
                [nn(knat[h, t], qt_ref[h * hd : (h + 1) * hd, qcol]) for t in ts]
                for h in range(group)
            ]
            for h in range(group):
                s = scores[h]
                if masked:
                    s = [jnp.where(ok, one, MASKED) for ok, one in zip(allowed, s)]
                old = m_ref[h]
                new = old
                for one in s:
                    new = jnp.maximum(new, jnp.max(one, 0, keepdims=True))
                p = [jnp.exp2(one - new) for one in s]
                alpha = jnp.exp2(old - new)
                total = l_ref[h] * alpha
                for one in p:
                    total = total + jnp.sum(one, 0, keepdims=True)
                l_ref[h] = total
                m_ref[h] = new
                out = acc[h] * alpha
                for t, one in zip(ts, p):
                    out = out + nn(vt[t, h * hd : (h + 1) * hd, :], one.astype(BF))
                acc[h] = out

        def full_step(i, c):
            step([2 * i, 2 * i + 1], False)
            return c

        def mask_step(i, c):
            step([2 * i, 2 * i + 1], True)
            return c

        lax.fori_loop(0, full // 2, full_step, 0)
        lax.fori_loop(full // 2, (need + 1) // 2, mask_step, 0)
        inner = pl.ds(pl.multiple_of((qi % per_half) * tile, tile), tile)
        for half, ref in enumerate((near_ref, far_ref)):

            @pl.when(qi // per_half == half)
            def _(ref=ref):
                for h in range(group):
                    ref[h * hd : (h + 1) * hd, inner] = (acc[h] / l_ref[h]).astype(BF)

        for h in range(group):
            lse_ref[h, :, qcol] = m_ref[h] + jnp.log2(l_ref[h])
        return carry

    lax.fori_loop(0, qt_ref.shape[1] // tile, one_tile, 0)


def backward_kernel(hd, tile, base, count, first, last, *refs):
    ids_ref, place_ref, row_ref, col_ref, qt_ref, kt_ref, vt_ref = refs[:7]
    near_ref, far_ref, onear_ref, ofar_ref, lse_ref = refs[7:12]
    if last:
        before_ref, scale_ref, dqt_ref, dkt_ref, dvt_ref, gs_ref = refs[12:18]
        knat, vnat, kt, dq, dk, dv, delta, dot = refs[18:]
    else:
        dqt_ref, dkt_ref, dvt_ref = refs[12:15]
        knat, vnat, kt, dq, dk, dv, delta, dot = refs[15:]
    tiles = kt_ref.shape[1] // tile
    group = qt_ref.shape[0] // hd

    def block_of(i):
        return pl.multiple_of(place_ref[place_ref[base + i]] * tile, tile)

    for i in range(count):
        cols = pl.ds(block_of(i), tile)
        kt[i] = kt_ref[:, cols]
        for h in range(group):
            hs = slice(h * hd, (h + 1) * hd)
            knat[h, i] = kt_ref[hs, cols].T
            vnat[h, i] = vt_ref[hs, cols].T
    per_half = near_ref.shape[1] // tile
    for half, (ref, o_ref) in enumerate(((near_ref, onear_ref), (far_ref, ofar_ref))):
        for b in range(per_half):
            cols = slice(b * tile, (b + 1) * tile)
            dot[half * per_half + b] = ref[:, cols]
            product = ref[:, cols].astype(F32) * o_ref[:, cols].astype(F32)
            for h in range(group):
                delta[half * per_half + b, h] = jnp.sum(
                    product[h * hd : (h + 1) * hd], 0, keepdims=True
                )
    dk[...] = jnp.zeros(dk.shape, F32)
    dv[...] = jnp.zeros(dv.shape, F32)
    if last:
        gs_ref[...] = jnp.zeros(gs_ref.shape, F32)

    def one_tile(qi, carry):
        stretch = place_ref[tiles + qi]
        low = ids_ref[stretch * tile]
        high = ids_ref[stretch * tile + tile - 1]
        full = jnp.int32(0)
        need = jnp.int32(0)
        for i in range(count):
            t = place_ref[base + i]
            full += (ids_ref[t * tile + tile - 1] <= low).astype(jnp.int32)
            need += (ids_ref[t * tile] <= high).astype(jnp.int32)
        qcol = pl.ds(pl.multiple_of(qi * tile, tile), tile)
        qpos = pl.ds(pl.multiple_of(stretch * tile, tile), tile)
        dq[...] = before_ref[:, qcol] if last else jnp.zeros(dq.shape, F32)

        def step(ts, masked):
            if masked:
                allowed = [
                    col_ref[pl.ds(pl.multiple_of(place_ref[base + t] * tile, tile), tile), :]
                    <= row_ref[:, qpos]
                    for t in ts
                ]

            def scores(h, t):
                hs = slice(h * hd, (h + 1) * hd)
                return nn(knat[h, t], qt_ref[hs, qcol]), nn(vnat[h, t], dot[qi, hs, :])

            order = [(h, i) for h in range(group) for i in range(len(ts))]
            ahead = scores(0, ts[0])
            for j, (h, i) in enumerate(order):
                hs = slice(h * hd, (h + 1) * hd)
                t = ts[i]
                s, dp = ahead
                if j + 1 < len(order):
                    ahead = scores(order[j + 1][0], ts[order[j + 1][1]])
                if masked:
                    s = jnp.where(allowed[i], s, MASKED)
                p = jnp.exp2(s - lse_ref[h, :, qcol])
                ds = (p * (dp - delta[qi, h])).astype(BF)
                dv[t, hs, :] += nt(dot[qi, hs, :], p.astype(BF))
                dk[t, hs, :] += nt(qt_ref[hs, qcol], ds)
                dq[hs, :] += nn(kt[t, hs, :], ds)

        def full_step(i, c):
            step([2 * i, 2 * i + 1], False)
            return c

        def mask_step(i, c):
            step([2 * i, 2 * i + 1], True)
            return c

        lax.fori_loop(0, full // 2, full_step, 0)
        lax.fori_loop(full // 2, (need + 1) // 2, mask_step, 0)
        if last:
            gs_ref[...] += jnp.sum(dq[...] * qt_ref[:, qcol].astype(F32), 1, keepdims=True)
            dqt_ref[:, qcol] = (dq[...] * scale_ref[...]).astype(BF)
        else:
            dqt_ref[:, qcol] = dq[...]
        return carry

    lax.fori_loop(0, qt_ref.shape[1] // tile, one_tile, 0)
    for i in range(count):
        cols = pl.ds(pl.multiple_of(block_of(i) - first * tile, tile), tile)
        dkt_ref[:, cols] = (dk[i] * (1.0 / LOG2E)).astype(BF)
        dvt_ref[:, cols] = dv[i].astype(BF)


def attention_specs(nq, nk, hd, group, at):
    size = group * hd
    return (
        [
            pl.BlockSpec(memory_space=pltpu.SMEM),
            pl.BlockSpec(memory_space=pltpu.SMEM),
            pl.BlockSpec((1, nk), lambda i: (0, 0)),
            pl.BlockSpec((nk, 1), lambda i: (0, 0)),
            pl.BlockSpec((size, nq), lambda i: (i + at, 0)),
            pl.BlockSpec((size, nk), lambda i: (i + at, 0)),
            pl.BlockSpec((size, nk), lambda i: (i + at, 0)),
        ],
        pl.BlockSpec((size, nq // 2), lambda i: (i + at, 0)),
        pl.BlockSpec((group, 1, nq), lambda i: (i + at, 0, 0)),
    )


def attention_forward(ids, col, place, qt, kt, vt, hd, tile):
    heads = qt.shape[0] // hd
    nq, nk = qt.shape[1], kt.shape[1]
    group = HEADS_AT_ONCE
    common, halves, rows = attention_specs(nq, nk, hd, group, 0)
    pairs = heads * nq * nk * 0.6
    return pl.pallas_call(
        functools.partial(forward_kernel, hd, tile),
        grid=(heads // group,),
        in_specs=common,
        out_specs=[halves, halves, rows],
        out_shape=[
            jax.ShapeDtypeStruct((heads * hd, nq // 2), BF),
            jax.ShapeDtypeStruct((heads * hd, nq // 2), BF),
            jax.ShapeDtypeStruct((heads, 1, nq), F32),
        ],
        scratch_shapes=[
            pltpu.VMEM((group, nk // tile, tile, hd), BF),
            pltpu.VMEM((nk // tile, group * hd, tile), BF),
            pltpu.VMEM((group, hd, tile), F32),
            pltpu.VMEM((group, 1, tile), F32),
            pltpu.VMEM((group, 1, tile), F32),
        ],
        compiler_params=pltpu.CompilerParams(vmem_limit_bytes=60 << 20),
        cost_estimate=pl.CostEstimate(
            flops=int(COST * pairs * 1024), bytes_accessed=1 << 16, transcendentals=int(COST * pairs)
        ),
        name="attention_forward",
    )(ids, place, ids.reshape(1, -1), col, qt, kt, vt)


def attention_backward(
    ids, col, place, qt, kt, vt, near, far, onear, ofar, lse, hd, tile, before=None, scale=None
):
    heads = qt.shape[0] // hd
    nq, nk = qt.shape[1], kt.shape[1]
    group = HEADS_AT_ONCE
    size = group * hd
    last = before is not None
    early = nq // tile
    tiles = nk // tile
    count, first = (early, 0) if last else (tiles - early, early)
    base = 2 * tiles + (0 if last else early)
    common, halves, rows = attention_specs(nq, nk, hd, group, 0)
    wide = pl.BlockSpec((size, nq), lambda i: (i, 0))
    keys = pl.BlockSpec((size, count * tile), lambda i: (i, 0))
    one = pl.BlockSpec((size, 1), lambda i: (i, 0))
    pairs = heads * nq * count * tile * 0.6
    return pl.pallas_call(
        functools.partial(backward_kernel, hd, tile, base, count, first, last),
        grid=(heads // group,),
        in_specs=[*common, halves, halves, halves, halves, rows, *([wide, one] if last else [])],
        out_specs=[wide, keys, keys, *([one] if last else [])],
        out_shape=[
            jax.ShapeDtypeStruct((heads * hd, nq), BF if last else F32),
            jax.ShapeDtypeStruct((heads * hd, count * tile), BF),
            jax.ShapeDtypeStruct((heads * hd, count * tile), BF),
            *([jax.ShapeDtypeStruct((heads * hd, 1), F32)] if last else []),
        ],
        scratch_shapes=[
            pltpu.VMEM((group, count, tile, hd), BF),
            pltpu.VMEM((group, count, tile, hd), BF),
            pltpu.VMEM((count, size, tile), BF),
            pltpu.VMEM((size, tile), F32),
            pltpu.VMEM((count, size, tile), F32),
            pltpu.VMEM((count, size, tile), F32),
            pltpu.VMEM((nq // tile, group, 1, tile), F32),
            pltpu.VMEM((nq // tile, size, tile), BF),
        ],
        compiler_params=pltpu.CompilerParams(vmem_limit_bytes=60 << 20),
        cost_estimate=pl.CostEstimate(
            flops=int(pairs * 2560), bytes_accessed=16 << 20, transcendentals=int(pairs)
        ),
        name="attention_backward",
    )(
        ids, place, ids.reshape(1, -1), col, qt, kt, vt, near, far, onear, ofar, lse,
        *([before, scale] if last else []),
    )


def weight_kernel(size, nq, at_ref, xt_ref, dqt_ref, dka_ref, dva_ref, dkb_ref, dvb_ref, *out_refs):
    for m, ref in enumerate(out_refs):

        @pl.when(pl.program_id(0) == m)
        def _(ref=ref):
            early = jnp.concatenate([dka_ref[...], dva_ref[...]], 0)
            late = jnp.concatenate([dkb_ref[...], dvb_ref[...]], 0)
            ref[:, : 2 * size] = (nt(xt_ref[:, :nq], early) + nt(xt_ref[:, nq:], late)).astype(BF)
            ref[:, 2 * size :] = nt(xt_ref[:, :nq], dqt_ref[...]).astype(BF)


def weight_gradient(xt, dqt, early, late, at, pieces, which):
    width, nk = xt.shape
    part, nq = dqt.shape
    size = part // 2
    rows = width // pieces
    once = pl.Buffered(1)

    def heads(cols):
        return pl.BlockSpec((size, cols), lambda i, a: (which, 0), pipeline_mode=once)

    return pl.pallas_call(
        functools.partial(weight_kernel, size, nq),
        grid_spec=pltpu.PrefetchScalarGridSpec(
            num_scalar_prefetch=1,
            grid=(pieces,),
            in_specs=[
                pl.BlockSpec((rows, nk), lambda i, a: (a[i], 0)),
                heads(nq), heads(nq), heads(nq), heads(nk - nq), heads(nk - nq),
            ],
            out_specs=[pl.BlockSpec((rows, 3 * size), lambda i, a: (0, 0))] * pieces,
        ),
        out_shape=[jax.ShapeDtypeStruct((rows, 3 * size), BF)] * pieces,
        compiler_params=pltpu.CompilerParams(vmem_limit_bytes=60 << 20),
        cost_estimate=pl.CostEstimate(
            flops=2 * width * size * (2 * nk + nq), bytes_accessed=12 << 20, transcendentals=0
        ),
        name="weight_gradient",
    )(at, xt, dqt, *early, *late)


def dx_kernel(part, queries, n, core_ref, *refs):
    dk_ref, dv_ref, wk_ref, wv_ref, gain_ref = refs[:5]
    x_refs = refs[5 : 5 + n]
    rest = refs[5 + n :]
    if queries:
        dq_ref, wq_ref = rest[:2]
        rest = rest[2:]
    dx_ref, gg_ref, g_ref, xs = rest
    i = pl.program_id(0)
    width = dx_ref.shape[1]
    tile = dx_ref.shape[0]
    step = width // 5
    dk = dk_ref[...].T
    dv = dv_ref[...].T
    if queries:
        dq = dq_ref[...].T
    for c in range(5):
        cols = slice(c * step, (c + 1) * step)
        g = nt(dk, wk_ref[cols, :]) + nt(dv, wv_ref[cols, :])
        if queries:
            g = g + nt(dq, wq_ref[cols, :])
        g_ref[:, cols] = g

    @pl.when(i == 0)
    def _():
        gg_ref[...] = jnp.zeros(gg_ref.shape, F32)

    per_slot = x_refs[0].shape[0] // tile
    for s in range(n):

        @pl.when(i // per_slot == s)
        def _(s=s):
            xs[...] = x_refs[s][pl.ds(pl.multiple_of((i % per_slot) * tile, tile), tile), :]

    x = xs[...].astype(F32)
    inverse = lax.rsqrt(jnp.mean(x * x, -1, keepdims=True) + EPSILON)
    normed = x * inverse
    g = g_ref[...]
    gn = g * normed
    gg_ref[...] += jnp.sum(gn, 0, keepdims=True)
    scaled = g * gain_ref[...]
    mean = jnp.mean(gn * gain_ref[...], -1, keepdims=True)
    dx_ref[...] = (inverse * (scaled - normed * mean)).astype(BF)


def input_gradient(dkvs, dqs, w_full, slots, core, gain):
    part = dkvs[0].shape[0]
    n = len(slots)
    rows, width = slots[0].shape
    tile = 256
    once = pl.Buffered(1)
    dkv = pl.BlockSpec((part, tile), lambda i, c: (0, i))

    def weight(j):
        return pl.BlockSpec(
            (width, part), lambda i, c, j=j: (0, 2 * j + c[0]), pipeline_mode=once
        )

    specs = [
        dkv, dkv, weight(1), weight(2), pl.BlockSpec((1, width), lambda i, c: (0, 0)),
        *[pl.BlockSpec((rows, width), lambda i, c: (0, 0), pipeline_mode=once)] * n,
    ]
    operands = [*dkvs, w_full, w_full, gain, *slots]
    if dqs:
        specs += [dkv, weight(0)]
        operands += [*dqs, w_full]
    return pl.pallas_call(
        functools.partial(dx_kernel, part, bool(dqs), n),
        grid_spec=pltpu.PrefetchScalarGridSpec(
            num_scalar_prefetch=1,
            grid=(n * rows // tile,),
            in_specs=specs,
            out_specs=[
                pl.BlockSpec((tile, width), lambda i, c: (i, 0)),
                pl.BlockSpec((1, width), lambda i, c: (0, 0)),
            ],
            scratch_shapes=[pltpu.VMEM((tile, width), F32), pltpu.VMEM((tile, width), BF)],
        ),
        out_shape=[
            jax.ShapeDtypeStruct((n * rows, width), BF),
            jax.ShapeDtypeStruct((1, width), F32),
        ],
        compiler_params=pltpu.CompilerParams(vmem_limit_bytes=60 << 20),
        cost_estimate=pl.CostEstimate(
            flops=int(COST * 2 * width * n * rows * part * (3 if dqs else 2)),
            bytes_accessed=1 << 16,
            transcendentals=0,
        ),
        name="input_gradient",
    )(core, *operands)


class Plan:
    def __init__(self, dp, ctx):
        self.dp, self.ctx = dp, ctx
        self.half = ctx // 2

    def index(self, pair, core, z):
        return (pair * 2 + core) * self.ctx + z

    def perm(self, to):
        out = []
        for d in range(self.dp):
            for z in range(self.ctx):
                got = to(d // 2, d % 2, z)
                if got is not None:
                    out.append((self.index(d // 2, d % 2, z), self.index(*got)))
        return out

    def home(self, core, z):
        return core == z // self.half

    def turned(self, z, k):
        first = z // self.half * self.half
        return first + (z - first + k) % self.half

    def core_swap(self):
        return self.perm(lambda p, c, z: (p, 1 - c, z))

    def pair_swap(self, mask):
        return self.perm(lambda p, c, z: (p ^ mask, c, z))

    def line_swap(self, mask):
        return self.perm(lambda p, c, z: (p, c, z ^ mask))

    def line_in(self, s):
        last = self.ctx - 1
        to = {s: s + 1, last - s: last - s - 1}
        return self.perm(lambda p, c, z: (p, c, to[z]) if z in to else None)

    def line_out(self, s):
        last = self.ctx - 1
        to = {s + 1: s, last - s - 1: last - s}
        return self.perm(lambda p, c, z: (p, c, to[z]) if z in to else None)

    def line_middle(self):
        to = {self.half - 1: self.half, self.half: self.half - 1}
        return self.perm(lambda p, c, z: (p, c, to[z]) if z in to else None)

    def mirror(self):
        return self.perm(
            lambda p, c, z: None if self.home(c, z) else (p, 1 - c, self.ctx - 1 - z)
        )

    def mirror_or_turn(self, k):
        return self.perm(
            lambda p, c, z: (p, c, self.turned(z, k))
            if self.home(c, z)
            else (p, 1 - c, self.ctx - 1 - z)
        )

    def turn(self, k, away_only):
        return self.perm(
            lambda p, c, z: None
            if away_only and self.home(c, z)
            else (p, c, self.turned(z, k))
        )

    def shard(self, core, z, k, mine):
        chip = self.turned(z, -k)
        at_home = self.home(core, z) if mine else not self.home(core, z)
        return chip if at_home else self.ctx - 1 - chip

    def places(self):
        table = np.zeros((self.dp, self.ctx, 6 * self.ctx), np.int32)
        for d in range(self.dp):
            for z in range(self.ctx):
                slots = [
                    self.shard(d % 2, z, k, mine) for k in range(self.half) for mine in (True, False)
                ]
                stretches = [s for shard in slots for s in (shard, 2 * self.ctx - 1 - shard)]
                for block, stretch in enumerate(stretches):
                    table[d, z, stretch] = block
                    table[d, z, 2 * self.ctx + block] = stretch
                table[d, z, 4 * self.ctx :] = sorted(stretches[:4]) + sorted(stretches[4:])
        return table.reshape(self.dp * self.ctx, 6 * self.ctx)


def send(value, pairs):
    return lax.ppermute(value, AXES, pairs)


def tie(*values):
    return lax.optimization_barrier(values)


def line_inward(value, plan, kind):
    total = value.astype(F32)
    for s in range(plan.half - 2):
        total = total + send(total.astype(kind), plan.line_in(s)).astype(F32)
    if plan.half == 1:
        return total, jnp.zeros_like(total, kind)
    return total, send(total.astype(kind), plan.line_in(plan.half - 2))


def line_across(held, came, plan, kind):
    sent = (held + came.astype(F32)).astype(kind)
    return sent, send(sent, plan.line_middle())


def line_joined(sent, came):
    return (sent.astype(F32) + came.astype(F32)).astype(sent.dtype)


def line_outward(total, plan, z):
    for s in reversed(range(plan.half - 1)):
        back = send(total, plan.line_out(s))
        total = jnp.where((z == s) | (z == plan.ctx - 1 - s), back, total)
    return total


def body(
    tokens_in, block_ids, w_qkv, w_out, w_in, w_down, gain_attn, gain_mlp, bias_in, bias_down,
    query_scale, cotangent,
):
    n = lax.axis_size("ctx")
    plan = Plan(lax.axis_size("dp"), n)
    half = plan.half
    z = lax.axis_index("ctx")
    core = lax.axis_index("dp") % 2
    pair = lax.axis_index("dp") // 2
    pairs = plan.dp // 2
    home = core == z // half
    rows = tokens_in.shape[1]
    width = tokens_in.shape[2]
    hd = query_scale.shape[0]
    heads = width // hd
    part = width // 2
    tile = rows // 2
    wrows = w_qkv.shape[0]
    core_swap = plan.core_swap()

    own = tokens_in[0]
    first = send(own, plan.mirror_or_turn(1))
    token0 = jnp.where(home, own, first)
    second = send(token0, plan.turn(1, True))
    mine = [token0, jnp.where(home, first, second)]
    for k in range(2, half):
        mine.append(send(token0, plan.turn(k, False)))
    theirs = [send(m, core_swap) for m in mine]
    slots = [a for both in zip(mine, theirs) for a in both]

    full_qkv = lax.all_gather(w_qkv, "dp", axis=0, tiled=True)
    at = jnp.stack([pair ^ mask for mask in range(pairs)]).astype(jnp.int32)
    core_at = core.astype(jnp.int32).reshape(1)

    ids = jnp.where(home, block_ids[0], send(block_ids[0], core_swap))
    place = lax.dynamic_index_in_dim(
        jnp.asarray(plan.places()), lax.axis_index("dp") * n + z, 0, False
    )
    col = ids.reshape(-1, 1)

    gain_one = gain_attn.astype(F32)
    gain_two = gain_mlp.astype(F32)
    scale_exp = jnp.exp(query_scale.astype(F32))
    scale_dim = SOFT_FACTOR / math.sqrt(hd) * jnp.log1p(scale_exp)
    scale_vec = jnp.tile(scale_dim, heads // 2)[:, None]
    weights = lax.all_gather(
        jnp.concatenate([w_down, w_in, w_out], 1), "dp", axis=0, tiled=True
    )
    qt, kt, vt, xt = project(
        slots, full_qkv, core_at, gain_one.reshape(1, -1), scale_vec * LOG2E
    )
    grad_low = send(tie(cotangent[0], slots[-1])[0], plan.mirror())
    onear, ofar, lse = attention_forward(ids, col, place, qt, kt, vt, hd, tile)
    onear, ofar, grad_low = tie(onear, ofar, grad_low)
    grad_low = jnp.where(home, cotangent[0], grad_low)
    o_got = send(ofar, core_swap)

    (
        output, to_keep, to_give, grad_middle, hidden_t, normed_t, grad_pre, grad_mid_low,
        grad_gain_two, grad_bin, grad_bdown,
    ) = mlp(
        onear, o_got, weights, token0, grad_low, core_at, gain_two.reshape(1, -1),
        bias_in.astype(F32).reshape(1, -1), bias_down.astype(F32).reshape(1, -1),
    )
    far = send(to_give, core_swap)
    away_output = send(output, plan.mirror())
    joined = mlp_weights(onear, o_got, hidden_t, normed_t, grad_low, grad_pre, grad_mid_low, core_at)
    early_qt, joined, far = tie(qt, joined, far)
    scattered = lax.psum_scatter(joined, "dp", scatter_dimension=0, tiled=True)

    def backward(queries, **rest):
        return attention_backward(
            ids, col, place, queries, kt, vt, to_keep, far, onear, ofar, lse, hd, tile, **rest
        )

    def to_owners(grads):
        return [send(grads[m], plan.pair_swap(m)) for m in range(1, pairs)]

    def add_up(grads, came):
        total = grads[0].astype(F32)
        for one in came:
            total = total + one.astype(F32)
        return total

    gain_row = gain_one.reshape(1, -1)
    dq_part, *late_kv = backward(early_qt)
    late_dx, gain_late = input_gradient(late_kv, (), full_qkv, slots[2:], core_at, gain_row)
    late_dx, dq_part, away_output = tie(late_dx, dq_part, away_output)
    output = jnp.where(home, output, away_output)
    late_got = [
        send(late_dx[(2 * k + 1) * rows : (2 * k + 2) * rows], core_swap) for k in range(half - 1)
    ]
    dq_part, *late_got = tie(dq_part, *late_got)
    turned = []
    for k in range(half - 1):
        mine = late_dx[2 * k * rows : (2 * k + 1) * rows].astype(F32)
        turned.append(
            send((mine + late_got[k].astype(F32)).astype(BF), plan.turn(-k - 1, False))
        )
    dqt, dk_early, dv_early, gs = backward(qt, before=dq_part, scale=scale_vec)
    dqt, dk_early, dv_early, scattered, *turned = tie(
        dqt, dk_early, dv_early, scattered, *turned
    )
    held_o, line_o = line_inward(scattered, plan, BF)
    early_kv = (dk_early, dv_early)
    grads_a = weight_gradient(xt, dqt, early_kv, late_kv, at, pairs, 0)
    later_dq, *grads_a = tie(dqt, *grads_a)
    came_a = to_owners(grads_a)
    grads_b = weight_gradient(xt, later_dq, early_kv, late_kv, at, pairs, 1)
    last_dq, line_o, *rest = tie(dqt, line_o, *came_a, *grads_b)
    came_a, grads_b = rest[: pairs - 1], rest[pairs - 1 :]
    held_o, line_o = line_across(held_o, line_o, plan, BF)
    came_b = to_owners(grads_b)
    held_a, line_a = line_inward(add_up(grads_a, came_a), plan, BF)
    dx, gain_early = input_gradient(
        early_kv, (last_dq,), full_qkv, slots[:2], core_at, gain_row
    )
    dx, gain_early, line_o, line_a, *came_b = tie(dx, gain_early, line_o, line_a, *came_b)
    got = send(dx[rows:], core_swap)
    others = line_outward(line_joined(held_o, line_o), plan, z)
    held_b, line_b = line_inward(add_up(grads_b, came_b), plan, BF)
    held_a, line_a = line_across(held_a, line_a, plan, BF)
    total = dx[:rows].astype(F32) + got.astype(F32) + grad_middle
    for one in turned:
        total = total + one.astype(F32)
    last = send(total.astype(BF), plan.mirror())

    scale_slope = SOFT_FACTOR / math.sqrt(hd) * scale_exp / (1.0 + scale_exp)
    grad_scale = jnp.sum(gs.reshape(heads // 2, hd), 0)
    grad_scale = grad_scale * scale_slope / (scale_dim * LOG2E)
    small = jnp.concatenate(
        [
            *(v.reshape(-1) for v in (gain_late + gain_early, grad_gain_two, grad_bin, grad_bdown)),
            grad_scale,
        ]
    )
    small_size = small.shape[0]
    small = jnp.pad(small, (0, -small_size % 1024)).reshape(-1, 128)
    small = small + send(small, core_swap)
    mask = 1
    while mask < pairs:
        small = small + send(small, plan.pair_swap(mask))
        mask *= 2
    line_b, line_a, small = tie(line_b, line_a, small)
    held_b, line_b = line_across(held_b, line_b, plan, BF)
    line_a = line_outward(line_joined(held_a, line_a), plan, z)

    def owned_rows(value):
        keep = lax.dynamic_slice_in_dim(value, core * wrows, wrows, 0)
        give = lax.dynamic_slice_in_dim(value, (1 - core) * wrows, wrows, 0)
        came = send(give, core_swap)
        return jnp.where(core == 0, keep, came), jnp.where(core == 0, came, keep)

    line_b, line_a, last = tie(line_b, line_a, last)
    swapped_a = owned_rows(line_a)
    line_b = line_outward(line_joined(held_b, line_b), plan, z)
    last, line_b, others, small = tie(last, line_b, others, small)
    mask = 1
    while mask < n:
        small = small + send(small, plan.line_swap(mask))
        mask *= 2
    small = small.reshape(-1)
    grad_tokens = jnp.where(home, total, last.astype(F32))
    others = others.astype(F32)
    swapped = (swapped_a, owned_rows(line_b))
    size = part // 2
    owned_qkv = jnp.concatenate(
        [
            swapped[g][c][:, which * size : (which + 1) * size]
            for which in (2, 0, 1)
            for c in range(2)
            for g in range(2)
        ],
        1,
    ).astype(F32)

    return (
        output[None],
        grad_tokens[None],
        owned_qkv,
        others[:, 2 * width :],
        others[:, width : 2 * width],
        others[:, :width],
        small[:width],
        small[width : 2 * width],
        small[2 * width : 3 * width],
        small[3 * width : 4 * width],
        small[4 * width : small_size],
    )


def solution(mesh):
    split = P("dp", "ctx", None)
    weight = P("dp", None)
    return jax.shard_map(
        body,
        mesh=mesh,
        in_specs=(split, weight, weight, weight, weight, weight, P(), P(), P(), P(), P(), split),
        out_specs=(split, split, weight, weight, weight, weight, P(), P(), P(), P(), P()),
        check_vma=False,
    )
```

profile of v0, /device:TPU:0, one launch (start us, length us, event | category | flops | bytes accessed | tf_op | source)
XLA Modules:
  0.0 445.5 jit_solution(13958708966858357555)
XLA Ops:
  8.4 1.1 pad_maximum_fusion
  9.6 3.1 collective-permute-start.1
  12.7 27.7 %collective-permute-done.1 = bf16[512,1280]{1,0:T(8,128)(2,1)S(1)} collective-permute-done((bf16[512,1280]{1,0:T(8,128)(2,1)S(1)}, bf16[512,1280]{1,0:T(8,128)(2,1)S(1)}, u32[]{:S(2)}, u32[]{:S(2)}) %collective-permute-start.1) | collective-permute-done | bytes 1310752 | tf_op jit(solution)/shard_map/ppermute | solution.py:789
  40.4 1.9 broadcast_select_fusion.2.refs_0_.x_ref.refs_5_
  42.3 0.9 collective-permute-start.3
  43.2 1.9 broadcast_select_fusion.1.refs_2_.refs_5_
  45.1 19.5 %collective-permute-start.4 = (bf16[512,1280]{1,0:T(8,128)(2,1)S(1)}, bf16[512,1280]{1,0:T(8,128)(2,1)}, u32[]{:S(2)}, u32[]{:S(2)}) collective-permute-start(bf16[512,1280]{1,0:T(8,128)(2,1)S(1)} %broadcast_select_fusion.1.refs_2_.refs_5_), channel_id=1, source_target_pairs={{0,4},{1,5},{2,6},{3,7},{4,0},{5,1},{6,2},{7,3},{8,12},{9,13},{10,... | collective-permute-start | bytes 3932168 | tf_op jit(solution)/shard_map/ppermute | solution.py:789
  65.4 0.8 broadcast_multiply_fusion.scale_ref
  66.2 1.3 fusion.3.place_ref.refs_1_
  68.1 1.4 copy.31.col_ref.refs_3_
  69.4 1.7 collective-permute-start.5
  71.2 2.0 all-gather.3.cloned.1.call-done.refs_4_.refs_5_.refs_6_.refs_2_.refs_3_.refs_8_
  73.2 18.8 %project.1 = (bf16[640,1024]{1,0:T(8,128)(2,1)}, bf16[640,2048]{1,0:T(8,128)(2,1)}, bf16[640,2048]{1,0:T(8,128)(2,1)}, bf16[1280,2048]{1,0:T(8,128)(2,1)}) custom-call(s32[1]{0:T(128)} %bitcast.core_ref, f32[1,1280]{1,0:T(1,128)} %reshape.111.gain_ref.refs_4_, f32[640,1]{1,0:T(8,128)} %broadcast_multiply_fusion.scale_ref, bf16[512,1280]{1,0:T(8,128)(2,1)} %copy-done, ...), custom_call_target="tpu_custom_call" | custom-call | flops 8388608000 | bytes 65536 | tf_op jit(solution)/shard_map/project/pallas_call | solution.py:75
  92.0 24.0 %attention_forward.1 = (bf16[640,512]{1,0:T(8,128)(2,1)}, bf16[640,512]{1,0:T(8,128)(2,1)}, f32[8,1,1024]{2,1,0:T(1,128)}) custom-call(s32[2048]{0:T(1024)} %copy-done.25, s32[24]{0:T(128)} %fusion.3.place_ref.refs_1_, s32[1,2048]{1,0:T(1,128)} %bitcast.37, s32[2048,1]{1,0:T(8,128)} %copy.31.col_ref.refs_3_, ...), custom_call_target="tpu_custom_call" | custom-call | flops 10307921920 | bytes 65536 | tf_op jit(solution)/shard_map/attention_forward/pallas_call | solution.py:495
  116.0 2.1 collective-permute-start.6
  119.8 1.2 broadcast_select_fusion.cot_ref
  121.0 14.5 %all-gather.5.cloned.1.call-done.w_ref = bf16[1280,3840]{1,0:T(8,128)(2,1)} async-done(((bf16[160,3840]{1,0:T(8,128)(2,1)}), bf16[1280,3840]{1,0:T(8,128)(2,1)}) %all-gather.5.cloned.1.call-update) | async-done | bytes 9830416 | tf_op jit(solution)/shard_map/all_gather | solution.py:867
  135.6 0.8 copy-done.36
  136.4 20.7 %mlp.1 = (bf16[512,1280]{1,0:T(8,128)(2,1)}, bf16[640,512]{1,0:T(8,128)(2,1)}, bf16[640,512]{1,0:T(8,128)(2,1)}, f32[512,1280]{1,0:T(8,128)}, bf16[1280,512]{1,0...) custom-call(s32[1]{0:T(128)} %bitcast.core_ref, ...), custom_call_target="tpu_custom_call" | custom-call | flops 10066329600 | bytes 65536 | tf_op jit(solution)/shard_map/mlp/pallas_call | solution.py:185
  157.5 11.3 %mlp_weights.1 = bf16[1280,3840]{1,0:T(8,128)(2,1)} custom-call(s32[1]{0:T(128)} %bitcast.core_ref, bf16[640,512]{1,0:T(8,128)(2,1)} %get-tuple-element.102.near_ref.refs_9_, bf16[640,512]{1,0:T(8,128)(2,1)} %copy-done.36, bf16[1280,512]{1,0:T(8,128)(2,1)} %get-tuple-element.106.ht_ref, bf16[1280,512]{1,0:T(8,128)(2,1)} %get-tuple-element.107.nt_ref, ...), custom_call_target="tpu_custom_call" | custom-call | flops 5033164800 | bytes 20971520 | tf_op jit(solution)/shard_map/mlp_weights/pallas_call | solution.py:258
  171.0 22.7 %attention_backward.2 = (f32[640,1024]{1,0:T(8,128)}, bf16[640,1024]{1,0:T(8,128)(2,1)}, bf16[640,1024]{1,0:T(8,128)(2,1)}) custom-call(s32[2048]{0:T(1024)} %copy-done.25, s32[24]{0:T(128)} %fusion.3.place_ref.refs_1_, s32[1,2048]{1,0:T(1,128)} %bitcast.38, s32[2048,1]{1,0:T(8,128)} %copy.31.col_ref.refs_3_, ...), custom_call_target="tpu_custom_call" | custom-call | flops 12884901888 | bytes 16777216 | tf_op jit(solution)/shard_map/attention_backward/pallas_call | solution.py:537
  193.7 12.3 %input_gradient.2 = (bf16[1024,1280]{1,0:T(8,128)(2,1)}, f32[1,1280]{1,0:T(1,128)}) custom-call(s32[1]{0:T(128)} %bitcast.core_ref, bf16[640,1024]{1,0:T(8,128)(2,1)} %get-tuple-element.115.refs_0_.dkb_ref, bf16[640,1024]{1,0:T(8,128)(2,1)} %get-tuple-element.116.refs_1_.dvb_ref, ...), custom_call_target="tpu_custom_call" | custom-call | flops 3355443200 | bytes 65536 | tf_op jit(solution)/shard_map/input_gradient/pallas_call | solution.py:676
  206.1 1.9 slice.84
  208.0 5.7 %collective-permute-start.9 = (bf16[512,1280]{1,0:T(8,128)(2,1)S(1)}, bf16[512,1280]{1,0:T(8,128)(2,1)S(1)}, u32[]{:S(2)}, u32[]{:S(2)}) collective-permute-start(bf16[512,1280]{1,0:T(8,128)(2,1)S(1)} %slice.84), channel_id=1, source_target_pairs={{0,4},{1,5},{2,6},{3,7},{4,0},{5,1},{6,2},{7,3},{8,12},{9,13},{10,... | collective-permute-start | bytes 3932168 | tf_op jit(solution)/shard_map/ppermute | solution.py:789
  213.6 2.7 collective-permute-done.9
  216.7 26.8 %attention_backward.3 = (bf16[640,1024]{1,0:T(8,128)(2,1)}, bf16[640,1024]{1,0:T(8,128)(2,1)}, bf16[640,1024]{1,0:T(8,128)(2,1)}, f32[640,1]{1,0:T(8,128)}) custom-call(s32[2048]{0:T(1024)} %copy-done.25, s32[24]{0:T(128)} %fusion.3.place_ref.refs_1_, s32[1,2048]{1,0:T(1,128)} %bitcast.39, s32[2048,1]{1,0:T(8,128)} %copy.31.col_ref.refs_3_, ...), custom_call_target="tpu_custom_call" | custom-call | flops 12884901888 | bytes 16777216 | tf_op jit(solution)/shard_map/attention_backward/pallas_call | solution.py:537
  243.5 4.3 collective-permute-done.10
  247.7 3.9 collective-permute-start.11
  252.3 11.0 %weight_gradient.2 = (bf16[320,960]{1,0:T(8,128)(2,1)}, bf16[320,960]{1,0:T(8,128)(2,1)}, bf16[320,960]{1,0:T(8,128)(2,1)}, bf16[320,960]{1,0:T(8,128)(2,1)}) custom-call(s32[4]{0:T(128)} %pad_add_fusion.at_ref, bf16[1280,2048]{1,0:T(8,128)(2,1)} %get-tuple-element.132.xt_ref, bf16[640,1024]{1,0:T(8,128)(2,1)} %get-tuple-element.145.dqt_ref.refs_7_, ...), custom_call_target="tpu_custom_call" | custom-call | flops 4194304000 | bytes 12582912 | tf_op jit(solution)/shard_map/weight_gradient/pallas_call | solution.py:590
  263.4 1.4 collective-permute-start.12
  265.4 1.5 collective-permute-start.14
  266.8 10.9 %weight_gradient.3 = (bf16[320,960]{1,0:T(8,128)(2,1)}, bf16[320,960]{1,0:T(8,128)(2,1)}, bf16[320,960]{1,0:T(8,128)(2,1)}, bf16[320,960]{1,0:T(8,128)(2,1)}) custom-call(s32[4]{0:T(128)} %pad_add_fusion.at_ref, bf16[1280,2048]{1,0:T(8,128)(2,1)} %get-tuple-element.132.xt_ref, bf16[640,1024]{1,0:T(8,128)(2,1)} %get-tuple-element.145.dqt_ref.refs_7_, ...), custom_call_target="tpu_custom_call" | custom-call | flops 4194304000 | bytes 12582912 | tf_op jit(solution)/shard_map/weight_gradient/pallas_call | solution.py:590
  277.7 3.5 collective-permute-done.12
  281.2 13.6 %collective-permute-done.13 = bf16[320,960]{1,0:T(8,128)(2,1)S(1)} collective-permute-done((bf16[320,960]{1,0:T(8,128)(2,1)}, bf16[320,960]{1,0:T(8,128)(2,1)S(1)}, u32[]{:S(2)}, u32[]{:S(2)}) %collective-permute-start.13) | collective-permute-done | bytes 614432 | tf_op jit(solution)/shard_map/ppermute | solution.py:789
  294.9 0.8 copy-done.10
  295.9 2.1 add_convert_fusion.2
  298.0 1.8 collective-permute-start.15
  299.9 1.3 fusion
  301.2 3.2 collective-permute-start.16
  305.0 1.3 collective-permute-start.18
  306.4 1.5 collective-permute-start.19
  307.9 1.3 reduce.1
  312.1 14.5 %input_gradient.3 = (bf16[1024,1280]{1,0:T(8,128)(2,1)}, f32[1,1280]{1,0:T(1,128)}) custom-call(s32[1]{0:T(128)} %bitcast.core_ref, bf16[640,1024]{1,0:T(8,128)(2,1)} %get-tuple-element.128.dka_ref.refs_0_, bf16[640,1024]{1,0:T(8,128)(2,1)} %get-tuple-element.129.dva_ref.refs_1_, ...), custom_call_target="tpu_custom_call" | custom-call | flops 5033164800 | bytes 65536 | tf_op jit(solution)/shard_map/input_gradient/pallas_call | solution.py:676
  326.6 7.1 %collective-permute-done.18 = bf16[320,960]{1,0:T(8,128)(2,1)} collective-permute-done((bf16[320,960]{1,0:T(8,128)(2,1)}, bf16[320,960]{1,0:T(8,128)(2,1)}, u32[]{:S(2)}, u32[]{:S(2)}) %collective-permute-start.18) | collective-permute-done | bytes 614432 | tf_op jit(solution)/shard_map/ppermute | solution.py:789
  334.7 2.7 add_convert_fusion.6
  337.9 1.4 collective-permute-start.24
  339.3 1.8 fusion.1
  341.0 1.3 collective-permute-start.21
  343.8 1.6 add_convert_fusion.1
  345.5 1.3 collective-permute-start.30
  347.0 9.6 %collective-permute-done.21 = bf16[320,960]{1,0:T(8,128)(2,1)S(1)} collective-permute-done((bf16[320,960]{1,0:T(8,128)(2,1)S(1)}, bf16[320,960]{1,0:T(8,128)(2,1)S(1)}, u32[]{:S(2)}, u32[]{:S(2)}) %collective-permute-start.21) | collective-permute-done | bytes 614432 | tf_op jit(solution)/shard_map/ppermute | solution.py:789
  358.3 1.4 collective-permute-start.27
  359.7 1.9 add_convert_fusion.5
  362.4 1.2 select_bitcast_fusion.1
  363.6 40.7 %collective-permute-done.27 = bf16[320,960]{1,0:T(8,128)(2,1)S(1)} collective-permute-done((bf16[320,960]{1,0:T(8,128)(2,1)S(1)}, bf16[320,960]{1,0:T(8,128)(2,1)S(1)}, u32[]{:S(2)}, u32[]{:S(2)}) %collective-permute-start.27) | collective-permute-done | bytes 614432 | tf_op jit(solution)/shard_map/ppermute | solution.py:789
  404.7 1.3 collective-permute-start.29
  406.5 17.2 %collective-permute-done.29 = bf16[320,960]{1,0:T(8,128)(2,1)S(1)} collective-permute-done((bf16[320,960]{1,0:T(8,128)(2,1)S(1)}, bf16[320,960]{1,0:T(8,128)(2,1)S(1)}, u32[]{:S(2)}, u32[]{:S(2)}) %collective-permute-start.29) | collective-permute-done | bytes 614432 | tf_op jit(solution)/shard_map/ppermute | solution.py:789
  424.0 2.3 select_bitcast_fusion
  426.3 1.4 collective-permute-done.33
  427.7 0.8 collective-permute-start.34
  428.6 1.5 fusion.7
  430.1 2.7 collective-permute-done.34
  434.2 2.7 concatenate.11
  436.9 1.6 convert_element_type.153
  (166 shorter events, 20.5 us)
Async XLA Ops:
  7.2 65.9 %all-gather.3.cloned.1.call-start = ((), (), s32[]{:S(2)}) async-start(), calls=%async_computation.1 | async-start | bytes 11059200 | tf_op jit(solution)/shard_map/all_gather | solution.py:852
  8.0 127.6 %all-gather.5.cloned.1.call-start = ((), (), s32[]{:S(2)}) async-start(), calls=%async_computation.2 | async-start | bytes 11059200 | tf_op jit(solution)/shard_map/all_gather | solution.py:867
  9.5 238.2 %reduce-scatter.2.cloned.1.call-start = ((), (), s32[]{:S(2)}) async-start(), calls=%async_computation.3 | async-start | bytes 11059200 | tf_op jit(solution)/shard_map/reduce_scatter | solution.py:890
  9.6 30.7 %collective-permute-start.1 = (bf16[512,1280]{1,0:T(8,128)(2,1)S(1)}, bf16[512,1280]{1,0:T(8,128)(2,1)S(1)}, u32[]{:S(2)}, u32[]{:S(2)}) collective-permute-start(bf16[512,1280]{1,0:T(8,128)(2,1)S(1)} %bitcast.33), channel_id=1, source_target_pairs={{0,1},{1,0},{2,5},{3,4},{4,3},{5,2},{6,7},{7,6},{8,9},{9,8},{10,13... | collective-permute-start | bytes 3932168 | tf_op jit(solution)/shard_map/ppermute | solution.py:789
  42.3 22.4 %copy-start = (bf16[512,1280]{1,0:T(8,128)(2,1)}, bf16[512,1280]{1,0:T(8,128)(2,1)S(1)}, u32[]{:S(2)}) copy-start(bf16[512,1280]{1,0:T(8,128)(2,1)S(1)} %broadcast_select_fusion.2.refs_0_.x_ref.refs_5_) | copy-start | bytes 3932164
  42.3 22.4 %copy-start.28 = (s32[1,2048]{1,0:T(1,128)S(1)}, s32[1,2048]{1,0:T(1,128)}, u32[]{:S(2)}) copy-start(s32[1,2048]{1,0:T(1,128)} %param.14) | copy-start | bytes 24580
  42.3 22.9 %copy-start.37 = (bf16[80]{0:T(256)(128)(2,1)S(1)}, bf16[80]{0:T(256)(128)(2,1)}, u32[]{:S(2)}) copy-start(bf16[80]{0:T(256)(128)(2,1)} %param.23) | copy-start | bytes 484
  42.3 25.1 %copy-start.31 = (bf16[1280]{0:T(1024)(128)(2,1)S(1)}, bf16[1280]{0:T(1024)(128)(2,1)}, u32[]{:S(2)}) copy-start(bf16[1280]{0:T(1024)(128)(2,1)} %param.19) | copy-start | bytes 7684
  42.3 0.9 collective-permute-start.3
  45.1 28.0 %copy-start.1 = (bf16[512,1280]{1,0:T(8,128)(2,1)}, bf16[512,1280]{1,0:T(8,128)(2,1)S(1)}, u32[]{:S(2)}) copy-start(bf16[512,1280]{1,0:T(8,128)(2,1)S(1)} %broadcast_select_fusion.1.refs_2_.refs_5_) | copy-start | bytes 3932164
  45.1 24.3 %collective-permute-start.4 = (bf16[512,1280]{1,0:T(8,128)(2,1)S(1)}, bf16[512,1280]{1,0:T(8,128)(2,1)}, u32[]{:S(2)}, u32[]{:S(2)}) collective-permute-start(bf16[512,1280]{1,0:T(8,128)(2,1)S(1)} %broadcast_select_fusion.1.refs_2_.refs_5_), channel_id=1, source_target_pairs={{0,4},{1,5},{2,6},{3,7},{4,0},{5,1},{6,2},{7,3},{8,12},{9,13},{10,... | collective-permute-start | bytes 3932168 | tf_op jit(solution)/shard_map/ppermute | solution.py:789
  64.7 6.5 %collective-permute-start.2 = (bf16[512,1280]{1,0:T(8,128)(2,1)S(1)}, bf16[512,1280]{1,0:T(8,128)(2,1)}, u32[]{:S(2)}, u32[]{:S(2)}) collective-permute-start(bf16[512,1280]{1,0:T(8,128)(2,1)S(1)} %broadcast_select_fusion.2.refs_0_.x_ref.refs_5_), channel_id=1, source_target_pairs={{0,4},{1,5},{2,6},{3,7},{4,0},{5,1},{6,2},{7,3},{8,12},{9,13},{10,... | collective-permute-start | bytes 3932168 | tf_op jit(solution)/shard_map/ppermute | solution.py:789
  64.7 3.3 collective-permute-start
  65.4 26.6 %copy-start.20 = (f32[640,1]{1,0:T(8,128)}, f32[640,1]{1,0:T(8,128)S(1)}, u32[]{:S(2)}) copy-start(f32[640,1]{1,0:T(8,128)S(1)} %broadcast_in_dim_tile.4.refs_13_) | copy-start | bytes 7684
  68.1 23.9 %copy-start.25 = (s32[2048]{0:T(1024)}, s32[2048]{0:T(1024)S(1)}, u32[]{:S(2)}) copy-start(s32[2048]{0:T(1024)S(1)} %broadcast_select_fusion.10.ids_ref.refs_0_) | copy-start | bytes 24580
  69.4 46.5 %collective-permute-start.5 = (bf16[512,1280]{1,0:T(8,128)(2,1)}, bf16[512,1280]{1,0:T(8,128)(2,1)}, u32[]{:S(2)}, u32[]{:S(2)}) collective-permute-start(bf16[512,1280]{1,0:T(8,128)(2,1)} %bitcast.34), channel_id=1, source_target_pairs={{2,5},{3,4},{4,3},{5,2},{10,13},{11,12},{12,11},{13,10},{18,21},{1... | collective-permute-start | bytes 3932168 | tf_op jit(solution)/shard_map/ppermute | solution.py:789
  91.9 26.1 %copy-start.32 = (bf16[1280]{0:T(1024)(128)(2,1)S(1)}, bf16[1280]{0:T(1024)(128)(2,1)}, u32[]{:S(2)}) copy-start(bf16[1280]{0:T(1024)(128)(2,1)} %param.20) | copy-start | bytes 7684
  91.9 26.7 %copy-start.33 = (bf16[1280]{0:T(1024)(128)(2,1)S(1)}, bf16[1280]{0:T(1024)(128)(2,1)}, u32[]{:S(2)}) copy-start(bf16[1280]{0:T(1024)(128)(2,1)} %param.21) | copy-start | bytes 7684
  92.0 27.3 %copy-start.34 = (bf16[1280]{0:T(1024)(128)(2,1)S(1)}, bf16[1280]{0:T(1024)(128)(2,1)}, u32[]{:S(2)}) copy-start(bf16[1280]{0:T(1024)(128)(2,1)} %param.22) | copy-start | bytes 7684
  92.0 27.9 %copy-start.15 = (bf16[1,512,1280]{2,1,0:T(8,128)(2,1)S(1)}, bf16[1,512,1280]{2,1,0:T(8,128)(2,1)}, u32[]{:S(2)}) copy-start(bf16[1,512,1280]{2,1,0:T(8,128)(2,1)} %param.24) | copy-start | bytes 3932164
  116.0 19.6 %collective-permute-start.6 = (bf16[640,512]{1,0:T(8,128)(2,1)}, bf16[640,512]{1,0:T(8,128)(2,1)S(1)}, u32[]{:S(2)}, u32[]{:S(2)}) collective-permute-start(bf16[640,512]{1,0:T(8,128)(2,1)} %get-tuple-element.103.refs_10_), channel_id=1, source_target_pairs={{0,4},{1,5},{2,6},{3,7},{4,0},{5,1},{6,2},{7,3},{8,12},{9,13},{10,... | collective-permute-start | bytes 1966088 | tf_op jit(solution)/shard_map/ppermute | solution.py:789
  157.1 11.6 %collective-permute-start.7 = (bf16[640,512]{1,0:T(8,128)(2,1)}, bf16[640,512]{1,0:T(8,128)(2,1)S(1)}, u32[]{:S(2)}, u32[]{:S(2)}) collective-permute-start(bf16[640,512]{1,0:T(8,128)(2,1)} %get-tuple-element.110), channel_id=1, source_target_pairs={{0,4},{1,5},{2,6},{3,7},{4,0},{5,1},{6,2},{7,3},{8,12},{9,13},{10,... | collective-permute-start | bytes 1966088 | tf_op jit(solution)/shard_map/ppermute | solution.py:789
  170.3 35.8 %collective-permute-start.8 = (bf16[512,1280]{1,0:T(8,128)(2,1)S(1)}, bf16[512,1280]{1,0:T(8,128)(2,1)S(1)}, u32[]{:S(2)}, u32[]{:S(2)}) collective-permute-start(bf16[512,1280]{1,0:T(8,128)(2,1)S(1)} %copy-done.16), channel_id=1, source_target_pairs={{2,5},{3,4},{4,3},{5,2},{10,13},{11,12},{12,11},{13,10},{18,21},{1... | collective-permute-start | bytes 3932168 | tf_op jit(solution)/shard_map/ppermute | solution.py:789
  206.0 10.3 %copy-start.5 = (bf16[1024,1280]{1,0:T(8,128)(2,1)S(1)}, bf16[1024,1280]{1,0:T(8,128)(2,1)}, u32[]{:S(2)}) copy-start(bf16[1024,1280]{1,0:T(8,128)(2,1)} %get-tuple-element.121) | copy-start | bytes 7864324
  208.0 8.3 %collective-permute-start.9 = (bf16[512,1280]{1,0:T(8,128)(2,1)S(1)}, bf16[512,1280]{1,0:T(8,128)(2,1)S(1)}, u32[]{:S(2)}, u32[]{:S(2)}) collective-permute-start(bf16[512,1280]{1,0:T(8,128)(2,1)S(1)} %slice.84), channel_id=1, source_target_pairs={{0,4},{1,5},{2,6},{3,7},{4,0},{5,1},{6,2},{7,3},{8,12},{9,13},{10,... | collective-permute-start | bytes 3932168 | tf_op jit(solution)/shard_map/ppermute | solution.py:789
  216.6 31.1 %collective-permute-start.10 = (bf16[512,1280]{1,0:T(8,128)(2,1)S(1)}, bf16[512,1280]{1,0:T(8,128)(2,1)S(1)}, u32[]{:S(2)}, u32[]{:S(2)}) collective-permute-start(bf16[512,1280]{1,0:T(8,128)(2,1)S(1)} %add_convert_fusion), channel_id=1, source_target_pairs={{0,1},{1,0},{2,3},{3,2},{4,5},{5,4},{6,7},{7,6},{8,9},{9,8},{10,11... | collective-permute-start | bytes 3932168 | tf_op jit(solution)/shard_map/ppermute | solution.py:789
  247.7 47.1 %collective-permute-start.11 = (bf16[160,3840]{1,0:T(8,128)(2,1)}, bf16[160,3840]{1,0:T(8,128)(2,1)}, u32[]{:S(2)}, u32[]{:S(2)}) collective-permute-start(bf16[160,3840]{1,0:T(8,128)(2,1)} %reduce-scatter.2.cloned.1.call-done), channel_id=1, source_target_pairs={{0,1},{3,2},{4,5},{7,6},{8,9},{11,10},{12,13},{15,14},{16,17},{19,... | collective-permute-start | bytes 3686408 | tf_op jit(solution)/shard_map/ppermute | solution.py:789
  263.4 17.9 %collective-permute-start.12 = (bf16[320,960]{1,0:T(8,128)(2,1)}, bf16[320,960]{1,0:T(8,128)(2,1)S(1)}, u32[]{:S(2)}, u32[]{:S(2)}) collective-permute-start(bf16[320,960]{1,0:T(8,128)(2,1)} %get-tuple-element.137), channel_id=1, source_target_pairs={{0,8},{1,9},{2,10},{3,11},{4,12},{5,13},{6,14},{7,15},{8,0},{9,1},... | collective-permute-start | bytes 1843208 | tf_op jit(solution)/shard_map/ppermute | solution.py:789
  264.7 30.1 %collective-permute-start.13 = (bf16[320,960]{1,0:T(8,128)(2,1)}, bf16[320,960]{1,0:T(8,128)(2,1)S(1)}, u32[]{:S(2)}, u32[]{:S(2)}) collective-permute-start(bf16[320,960]{1,0:T(8,128)(2,1)} %get-tuple-element.138), channel_id=1, source_target_pairs={{0,16},{1,17},{2,18},{3,19},{4,20},{5,21},{6,22},{7,23},{8,24},{9,... | collective-permute-start | bytes 1843208 | tf_op jit(solution)/shard_map/ppermute | solution.py:789
  265.4 29.5 %collective-permute-start.14 = (bf16[320,960]{1,0:T(8,128)(2,1)}, bf16[320,960]{1,0:T(8,128)(2,1)S(1)}, u32[]{:S(2)}, u32[]{:S(2)}) collective-permute-start(bf16[320,960]{1,0:T(8,128)(2,1)} %get-tuple-element.139), channel_id=1, source_target_pairs={{0,24},{1,25},{2,26},{3,27},{4,28},{5,29},{6,30},{7,31},{8,16},{9,... | collective-permute-start | bytes 1843208 | tf_op jit(solution)/shard_map/ppermute | solution.py:789
  281.2 13.6 %copy-start.8 = (bf16[320,960]{1,0:T(8,128)(2,1)}, bf16[320,960]{1,0:T(8,128)(2,1)S(1)}, u32[]{:S(2)}) copy-start(bf16[320,960]{1,0:T(8,128)(2,1)S(1)} %collective-permute-done.12) | copy-start | bytes 1843204
  295.9 4.0 copy-start.7
  295.9 4.0 copy-start.9
  295.9 4.0 copy-start.11
  295.9 4.0 copy-start.13
  298.0 11.2 %copy-start.30 = (f32[1,1280]{1,0:T(1,128)S(1)}, f32[1,1280]{1,0:T(1,128)}, u32[]{:S(2)}) copy-start(f32[1,1280]{1,0:T(1,128)} %get-tuple-element.167) | copy-start | bytes 15364
  298.0 12.5 %copy-start.24 = (f32[640,1]{1,0:T(8,128)S(1)}, f32[640,1]{1,0:T(8,128)}, u32[]{:S(2)}) copy-start(f32[640,1]{1,0:T(8,128)} %get-tuple-element.169) | copy-start | bytes 7684
  298.0 35.7 %collective-permute-start.15 = (bf16[160,3840]{1,0:T(8,128)(2,1)S(1)}, bf16[160,3840]{1,0:T(8,128)(2,1)}, u32[]{:S(2)}, u32[]{:S(2)}) collective-permute-start(bf16[160,3840]{1,0:T(8,128)(2,1)S(1)} %add_convert_fusion.2), channel_id=1, source_target_pairs={{1,2},{2,1},{5,6},{6,5},{9,10},{10,9},{13,14},{14,13},{17,18},{18,... | collective-permute-start | bytes 3686408 | tf_op jit(solution)/shard_map/ppermute | solution.py:789
  301.2 25.4 %collective-permute-start.16 = (bf16[320,960]{1,0:T(8,128)(2,1)}, bf16[320,960]{1,0:T(8,128)(2,1)}, u32[]{:S(2)}, u32[]{:S(2)}) collective-permute-start(bf16[320,960]{1,0:T(8,128)(2,1)} %fusion), channel_id=1, source_target_pairs={{0,1},{3,2},{4,5},{7,6},{8,9},{11,10},{12,13},{15,14},{16,17},{19,... | collective-permute-start | bytes 1843208 | tf_op jit(solution)/shard_map/ppermute | solution.py:789
  304.4 22.2 %collective-permute-start.17 = (bf16[320,960]{1,0:T(8,128)(2,1)}, bf16[320,960]{1,0:T(8,128)(2,1)S(1)}, u32[]{:S(2)}, u32[]{:S(2)}) collective-permute-start(bf16[320,960]{1,0:T(8,128)(2,1)} %get-tuple-element.153), channel_id=1, source_target_pairs={{0,8},{1,9},{2,10},{3,11},{4,12},{5,13},{6,14},{7,15},{8,0},{9,1},... | collective-permute-start | bytes 1843208 | tf_op jit(solution)/shard_map/ppermute | solution.py:789
  305.0 28.7 %collective-permute-start.18 = (bf16[320,960]{1,0:T(8,128)(2,1)}, bf16[320,960]{1,0:T(8,128)(2,1)}, u32[]{:S(2)}, u32[]{:S(2)}) collective-permute-start(bf16[320,960]{1,0:T(8,128)(2,1)} %get-tuple-element.154), channel_id=1, source_target_pairs={{0,16},{1,17},{2,18},{3,19},{4,20},{5,21},{6,22},{7,23},{8,24},{9,... | collective-permute-start | bytes 1843208 | tf_op jit(solution)/shard_map/ppermute | solution.py:789
  306.4 27.4 %collective-permute-start.19 = (bf16[320,960]{1,0:T(8,128)(2,1)}, bf16[320,960]{1,0:T(8,128)(2,1)}, u32[]{:S(2)}, u32[]{:S(2)}) collective-permute-start(bf16[320,960]{1,0:T(8,128)(2,1)} %get-tuple-element.155), channel_id=1, source_target_pairs={{0,24},{1,25},{2,26},{3,27},{4,28},{5,29},{6,30},{7,31},{8,16},{9,... | collective-permute-start | bytes 1843208 | tf_op jit(solution)/shard_map/ppermute | solution.py:789
  312.1 21.7 %copy-start.29 = (f32[1,1280]{1,0:T(1,128)S(1)}, f32[1,1280]{1,0:T(1,128)}, u32[]{:S(2)}) copy-start(f32[1,1280]{1,0:T(1,128)} %get-tuple-element.164) | copy-start | bytes 15364
  312.1 22.4 %copy-start.27 = (f32[1280]{0:T(1024)S(1)}, f32[1280]{0:T(1024)}, u32[]{:S(2)}) copy-start(f32[1280]{0:T(1024)} %reduce.1) | copy-start | bytes 15364
  312.1 22.4 %copy-start.26 = (f32[1280]{0:T(1024)S(1)}, f32[1280]{0:T(1024)}, u32[]{:S(2)}) copy-start(f32[1280]{0:T(1024)} %reduce.2) | copy-start | bytes 15364
  312.1 22.4 %copy-start.38 = (bf16[80]{0:T(256)(128)(2,1)S(1)}, bf16[80]{0:T(256)(128)(2,1)}, u32[]{:S(2)}) copy-start(bf16[80]{0:T(256)(128)(2,1)} %param.23) | copy-start | bytes 484
  334.6 3.3 collective-permute-start.23
  337.5 19.2 %collective-permute-start.20 = (bf16[512,1280]{1,0:T(8,128)(2,1)S(1)}, bf16[512,1280]{1,0:T(8,128)(2,1)S(1)}, u32[]{:S(2)}, u32[]{:S(2)}) collective-permute-start(bf16[512,1280]{1,0:T(8,128)(2,1)S(1)} %slice.87), channel_id=1, source_target_pairs={{0,4},{1,5},{2,6},{3,7},{4,0},{5,1},{6,2},{7,3},{8,12},{9,13},{10,... | collective-permute-start | bytes 3932168 | tf_op jit(solution)/shard_map/ppermute | solution.py:789
  337.9 5.2 %collective-permute-start.24 = (f32[48,128]{1,0:T(8,128)S(1)}, f32[48,128]{1,0:T(8,128)S(1)}, u32[]{:S(2)}, u32[]{:S(2)}) collective-permute-start(f32[48,128]{1,0:T(8,128)S(1)} %fusion.6), channel_id=1, source_target_pairs={{0,8},{1,9},{2,10},{3,11},{4,12},{5,13},{6,14},{7,15},{8,0},{9,1},... | collective-permute-start | bytes 73736 | tf_op jit(solution)/shard_map/ppermute | solution.py:789
  341.0 15.6 %collective-permute-start.21 = (bf16[320,960]{1,0:T(8,128)(2,1)S(1)}, bf16[320,960]{1,0:T(8,128)(2,1)S(1)}, u32[]{:S(2)}, u32[]{:S(2)}) collective-permute-start(bf16[320,960]{1,0:T(8,128)(2,1)S(1)} %fusion.1), channel_id=1, source_target_pairs={{0,1},{3,2},{4,5},{7,6},{8,9},{11,10},{12,13},{15,14},{16,17},{19,... | collective-permute-start | bytes 1843208 | tf_op jit(solution)/shard_map/ppermute | solution.py:789
  342.4 14.3 %collective-permute-start.22 = (bf16[320,960]{1,0:T(8,128)(2,1)S(1)}, bf16[320,960]{1,0:T(8,128)(2,1)S(1)}, u32[]{:S(2)}, u32[]{:S(2)}) collective-permute-start(bf16[320,960]{1,0:T(8,128)(2,1)S(1)} %add_convert_fusion.6), channel_id=1, source_target_pairs={{1,2},{2,1},{5,6},{6,5},{9,10},{10,9},{13,14},{14,13},{17,18},{18,... | collective-permute-start | bytes 1843208 | tf_op jit(solution)/shard_map/ppermute | solution.py:789
  343.1 13.5 %copy-start.2 = (f32[512,1280]{1,0:T(8,128)S(1)}, f32[512,1280]{1,0:T(8,128)}, u32[]{:S(2)}) copy-start(f32[512,1280]{1,0:T(8,128)} %get-tuple-element.157) | copy-start | bytes 7864324
  343.1 3.9 collective-permute-start.25
  345.5 60.6 %collective-permute-start.30 = (bf16[160,3840]{1,0:T(8,128)(2,1)S(1)}, bf16[160,3840]{1,0:T(8,128)(2,1)S(1)}, u32[]{:S(2)}, u32[]{:S(2)}) collective-permute-start(bf16[160,3840]{1,0:T(8,128)(2,1)S(1)} %add_convert_fusion.1), channel_id=1, source_target_pairs={{1,0},{2,3},{5,4},{6,7},{9,8},{10,11},{13,12},{14,15},{17,16},{18,... | collective-permute-start | bytes 3686408 | tf_op jit(solution)/shard_map/ppermute | solution.py:789
  357.3 47.1 %collective-permute-start.28 = (bf16[512,1280]{1,0:T(8,128)(2,1)S(1)}, bf16[512,1280]{1,0:T(8,128)(2,1)S(1)}, u32[]{:S(2)}, u32[]{:S(2)}) collective-permute-start(bf16[512,1280]{1,0:T(8,128)(2,1)S(1)} %fusion.2), channel_id=1, source_target_pairs={{2,5},{3,4},{4,3},{5,2},{10,13},{11,12},{12,11},{13,10},{18,21},{1... | collective-permute-start | bytes 3932168 | tf_op jit(solution)/shard_map/ppermute | solution.py:789
  358.3 4.1 copy-start.17
  358.3 4.1 copy-start.19
  358.3 46.0 %collective-permute-start.27 = (bf16[320,960]{1,0:T(8,128)(2,1)S(1)}, bf16[320,960]{1,0:T(8,128)(2,1)S(1)}, u32[]{:S(2)}, u32[]{:S(2)}) collective-permute-start(bf16[320,960]{1,0:T(8,128)(2,1)S(1)} %add_convert_fusion.4), channel_id=1, source_target_pairs={{1,0},{2,3},{5,4},{6,7},{9,8},{10,11},{13,12},{14,15},{17,16},{18,... | collective-permute-start | bytes 1843208 | tf_op jit(solution)/shard_map/ppermute | solution.py:789
  361.7 42.7 %collective-permute-start.26 = (bf16[320,960]{1,0:T(8,128)(2,1)S(1)}, bf16[320,960]{1,0:T(8,128)(2,1)S(1)}, u32[]{:S(2)}, u32[]{:S(2)}) collective-permute-start(bf16[320,960]{1,0:T(8,128)(2,1)S(1)} %add_convert_fusion.5), channel_id=1, source_target_pairs={{1,2},{2,1},{5,6},{6,5},{9,10},{10,9},{13,14},{14,13},{17,18},{18,... | collective-permute-start | bytes 1843208 | tf_op jit(solution)/shard_map/ppermute | solution.py:789
  404.4 1.8 collective-permute-start.31
  404.7 19.0 %collective-permute-start.29 = (bf16[320,960]{1,0:T(8,128)(2,1)S(1)}, bf16[320,960]{1,0:T(8,128)(2,1)S(1)}, u32[]{:S(2)}, u32[]{:S(2)}) collective-permute-start(bf16[320,960]{1,0:T(8,128)(2,1)S(1)} %add_convert_fusion.3), channel_id=1, source_target_pairs={{1,0},{2,3},{5,4},{6,7},{9,8},{10,11},{13,12},{14,15},{17,16},{18,... | collective-permute-start | bytes 1843208 | tf_op jit(solution)/shard_map/ppermute | solution.py:789
  423.8 3.9 collective-permute-start.33
  424.0 9.9 %collective-permute-start.32 = (bf16[160,960]{1,0:T(8,128)(2,1)S(1)}, bf16[160,960]{1,0:T(8,128)(2,1)S(1)}, u32[]{:S(2)}, u32[]{:S(2)}) collective-permute-start(bf16[160,960]{1,0:T(8,128)(2,1)S(1)} %constant_dynamic-slice_fusion), channel_id=1, source_target_pairs={{0,4},{1,5},{2,6},{3,7},{4,0},{5,1},{6,2},{7,3},{8,12},{9,13},{10,... | collective-permute-start | bytes 921608 | tf_op jit(solution)/shard_map/ppermute | solution.py:789
  427.7 5.0 %collective-permute-start.34 = (f32[48,128]{1,0:T(8,128)S(1)}, f32[48,128]{1,0:T(8,128)S(1)}, u32[]{:S(2)}, u32[]{:S(2)}) collective-permute-start(f32[48,128]{1,0:T(8,128)S(1)} %add.124), channel_id=1, source_target_pairs={{0,2},{1,3},{2,0},{3,1},{4,6},{5,7},{6,4},{7,5},{8,10},{9,11},{10,... | collective-permute-start | bytes 73736 | tf_op jit(solution)/shard_map/ppermute | solution.py:789
  (13 other events, 18.7 us)
Sparse Core Ops, SparseCore 0:
  9.9 63.1 all-gather.2
  75.0 60.4 all-gather.4
  168.9 78.2 reduce-scatter.1
where the time goes:
time: 453 us; the launch traced here: 445 us
  Pallas kernels  173 us (38%)
  waiting for transfers between devices  148 us (33%)
  starting transfers between devices  61.7 us (14%)
  other arithmetic  30.4 us (7%)
  local copies, waits for them, and re-layouts  17.6 us (4%)
  between operations  14.9 us (3%)
    ppermute x35, waiting for transfers between devices, send(): return lax.ppermute(value, AXES, pairs)  131 us
    ppermute x35, starting transfers between devices, send(): return lax.ppermute(value, AXES, pairs)  61.6 us
    pallas_call x2, Pallas kernels, attention_backward(): pl.pallas_call(functools.partial(backward_kernel, hd, tile, base, count,...  49.5 us
    pallas_call x2, Pallas kernels, input_gradient(): pl.pallas_call(functools.partial(dx_kernel, part, bool(dqs), n), grid_spe...  26.8 us
    pallas_call x1, Pallas kernels, attention_forward(): pl.pallas_call(functools.partial(forward_kernel, hd, tile), grid=(heads /...  24 us
    pallas_call x2, Pallas kernels, weight_gradient(): pl.pallas_call(functools.partial(weight_kernel, size, nq), grid_spec=pltp...  21.9 us
    pallas_call x1, Pallas kernels, mlp(): pl.pallas_call(functools.partial(mlp_kernel, part), grid_spec=pltpu.Prefe...  20.7 us
    pallas_call x1, Pallas kernels, project(): pl.pallas_call(functools.partial(project_kernel, part, query_slots, n), g...  18.8 us
  transfers between devices with their start and end apart: 38, of which 14 were waited for; matrix products, arithmetic and copies ran while one was open for 8% of the time, Pallas kernels for 34%

commit v1 on v0

--- a/solution.py
+++ b/solution.py
@@ -614,10 +614,9 @@
     if queries:
         dq_ref, wq_ref = rest[:2]
         rest = rest[2:]
-    dx_ref, gg_ref, g_ref, xs = rest
+    dx_refs, (gg_ref, g_ref, xs) = rest[:n], rest[n:]
     i = pl.program_id(0)
-    width = dx_ref.shape[1]
-    tile = dx_ref.shape[0]
+    tile, width = xs.shape
     step = width // 5
     dk = dk_ref[...].T
     dv = dv_ref[...].T
@@ -649,7 +648,12 @@
     gg_ref[...] += jnp.sum(gn, 0, keepdims=True)
     scaled = g * gain_ref[...]
     mean = jnp.mean(gn * gain_ref[...], -1, keepdims=True)
-    dx_ref[...] = (inverse * (scaled - normed * mean)).astype(BF)
+    out = (inverse * (scaled - normed * mean)).astype(BF)
+    for s in range(n):
+
+        @pl.when(i // per_slot == s)
+        def _(s=s):
+            dx_refs[s][...] = out
 
 
 def input_gradient(dkvs, dqs, w_full, slots, core, gain):
@@ -657,6 +661,7 @@
     n = len(slots)
     rows, width = slots[0].shape
     tile = 256
+    per_slot = rows // tile
     once = pl.Buffered(1)
     dkv = pl.BlockSpec((part, tile), lambda i, c: (0, i))
 
@@ -680,13 +685,19 @@
             grid=(n * rows // tile,),
             in_specs=specs,
             out_specs=[
-                pl.BlockSpec((tile, width), lambda i, c: (i, 0)),
+                *[
+                    pl.BlockSpec(
+                        (tile, width),
+                        lambda i, c, s=s: (jnp.clip(i - s * per_slot, 0, per_slot - 1), 0),
+                    )
+                    for s in range(n)
+                ],
                 pl.BlockSpec((1, width), lambda i, c: (0, 0)),
             ],
             scratch_shapes=[pltpu.VMEM((tile, width), F32), pltpu.VMEM((tile, width), BF)],
         ),
         out_shape=[
-            jax.ShapeDtypeStruct((n * rows, width), BF),
+            *[jax.ShapeDtypeStruct((rows, width), BF)] * n,
             jax.ShapeDtypeStruct((1, width), F32),
         ],
         compiler_params=pltpu.CompilerParams(vmem_limit_bytes=60 << 20),
@@ -905,16 +916,16 @@
 
     gain_row = gain_one.reshape(1, -1)
     dq_part, *late_kv = backward(early_qt)
-    late_dx, gain_late = input_gradient(late_kv, (), full_qkv, slots[2:], core_at, gain_row)
-    late_dx, dq_part, away_output = tie(late_dx, dq_part, away_output)
+    *late_dx, gain_late = input_gradient(late_kv, (), full_qkv, slots[2:], core_at, gain_row)
+    dq_part, away_output, *late_dx = tie(dq_part, away_output, *late_dx)
     output = jnp.where(home, output, away_output)
     late_got = [
-        send(late_dx[(2 * k + 1) * rows : (2 * k + 2) * rows], core_swap) for k in range(half - 1)
+        send(late_dx[2 * k + 1], core_swap) for k in range(half - 1)
     ]
     dq_part, *late_got = tie(dq_part, *late_got)
     turned = []
     for k in range(half - 1):
-        mine = late_dx[2 * k * rows : (2 * k + 1) * rows].astype(F32)
+        mine = late_dx[2 * k].astype(F32)
         turned.append(
             send((mine + late_got[k].astype(F32)).astype(BF), plan.turn(-k - 1, False))
         )
@@ -927,24 +938,27 @@
     grads_a = weight_gradient(xt, dqt, early_kv, late_kv, at, pairs, 0)
     later_dq, *grads_a = tie(dqt, *grads_a)
     came_a = to_owners(grads_a)
-    grads_b = weight_gradient(xt, later_dq, early_kv, late_kv, at, pairs, 1)
-    last_dq, line_o, *rest = tie(dqt, line_o, *came_a, *grads_b)
-    came_a, grads_b = rest[: pairs - 1], rest[pairs - 1 :]
+    near_dx, far_dx, gain_early = input_gradient(
+        early_kv, (later_dq,), full_qkv, slots[:2], core_at, gain_row
+    )
+    near_dx, far_dx, gain_early, last_dq, line_o, *came_a = tie(
+        near_dx, far_dx, gain_early, dqt, line_o, *came_a
+    )
+    got = send(far_dx, core_swap)
+    held_a, line_a = line_inward(add_up(grads_a, came_a), plan, BF)
     held_o, line_o = line_across(held_o, line_o, plan, BF)
+    grads_b = weight_gradient(xt, last_dq, early_kv, late_kv, at, pairs, 1)
+    got, line_a, *grads_b = tie(got, line_a, *grads_b)
     came_b = to_owners(grads_b)
-    held_a, line_a = line_inward(add_up(grads_a, came_a), plan, BF)
-    dx, gain_early = input_gradient(
-        early_kv, (last_dq,), full_qkv, slots[:2], core_at, gain_row
-    )
-    dx, gain_early, line_o, line_a, *came_b = tie(dx, gain_early, line_o, line_a, *came_b)
-    got = send(dx[rows:], core_swap)
-    others = line_outward(line_joined(held_o, line_o), plan, z)
-    held_b, line_b = line_inward(add_up(grads_b, came_b), plan, BF)
-    held_a, line_a = line_across(held_a, line_a, plan, BF)
-    total = dx[:rows].astype(F32) + got.astype(F32) + grad_middle
+    total = near_dx.astype(F32) + got.astype(F32) + grad_middle
     for one in turned:
         total = total + one.astype(F32)
     last = send(total.astype(BF), plan.mirror())
+    held_a, line_a = line_across(held_a, line_a, plan, BF)
+    gain_early, line_a, line_o, *came_b = tie(gain_early, line_a, line_o, *came_b)
+    held_b, line_b = line_inward(add_up(grads_b, came_b), plan, BF)
+    line_a = line_outward(line_joined(held_a, line_a), plan, z)
+    others = line_outward(line_joined(held_o, line_o), plan, z)
 
     scale_slope = SOFT_FACTOR / math.sqrt(hd) * scale_exp / (1.0 + scale_exp)
     grad_scale = jnp.sum(gs.reshape(heads // 2, hd), 0)
@@ -964,7 +978,6 @@
         mask *= 2
     line_b, line_a, small = tie(line_b, line_a, small)
     held_b, line_b = line_across(held_b, line_b, plan, BF)
-    line_a = line_outward(line_joined(held_a, line_a), plan, z)
 
     def owned_rows(value):
         keep = lax.dynamic_slice_in_dim(value, core * wrows, wrows, 0)
@@ -975,7 +988,7 @@
     line_b, line_a, last = tie(line_b, line_a, last)
     swapped_a = owned_rows(line_a)
     line_b = line_outward(line_joined(held_b, line_b), plan, z)
-    last, line_b, others, small = tie(last, line_b, others, small)
+    line_b, others, small = tie(line_b, others, small)
     mask = 1
     while mask < n:
         small = small + send(small, plan.line_swap(mask))

time: 453 us -> 450 us (level)
  waiting for transfers between devices: 148 us -> 135 us
  starting transfers between devices: 61.7 us -> 71.7 us
  other arithmetic: 30.4 us -> 35.3 us
    ppermute x35, waiting for transfers between devices: 131 us -> 116 us  [send(): return lax.ppermute(value, AXES, pairs)]
    ppermute x35, starting transfers between devices: 61.6 us -> 71.6 us  [send(): return lax.ppermute(value, AXES, pairs)]
  transfers between devices with their start and end apart: 38 -> 38, of which waited for: 14 -> 14; matrix products, arithmetic and copies ran while one was open for 8% -> 9% of each run, Pallas kernels for 34% -> 34%
where the time goes in v1:
time: 450 us; the launch traced here: 443 us
  Pallas kernels  170 us (38%)
  waiting for transfers between devices  135 us (30%)
  starting transfers between devices  71.7 us (16%)
  other arithmetic  35.3 us (8%)
  local copies, waits for them, and re-layouts  15.5 us (3%)
  between operations  15 us (3%)
    ppermute x35, waiting for transfers between devices, send(): return lax.ppermute(value, AXES, pairs)  116 us
    ppermute x35, starting transfers between devices, send(): return lax.ppermute(value, AXES, pairs)  71.6 us
    pallas_call x2, Pallas kernels, attention_backward(): pl.pallas_call(functools.partial(backward_kernel, hd, tile, base, count,...  47 us
    pallas_call x2, Pallas kernels, input_gradient(): pl.pallas_call(functools.partial(dx_kernel, part, bool(dqs), n), grid_spe...  27.7 us
    pallas_call x1, Pallas kernels, attention_forward(): pl.pallas_call(functools.partial(forward_kernel, hd, tile), grid=(heads /...  22.4 us
    pallas_call x2, Pallas kernels, weight_gradient(): pl.pallas_call(functools.partial(weight_kernel, size, nq), grid_spec=pltp...  22.3 us
    pallas_call x1, Pallas kernels, mlp(): pl.pallas_call(functools.partial(mlp_kernel, part), grid_spec=pltpu.Prefe...  20.7 us
    pallas_call x1, Pallas kernels, project(): pl.pallas_call(functools.partial(project_kernel, part, query_slots, n), g...  18.8 us
  transfers between devices with their start and end apart: 38, of which 14 were waited for; matrix products, arithmetic and copies ran while one was open for 9% of the time, Pallas kernels for 34%

profile of v1, /device:TPU:0, one launch (start us, length us, event | category | flops | bytes accessed | tf_op | source)
XLA Modules:
  0.0 442.7 jit_solution(423473190916761692)
XLA Ops:
  8.4 1.1 pad_maximum_fusion
  9.6 3.1 collective-permute-start.1
  12.7 27.7 %collective-permute-done.1 = bf16[512,1280]{1,0:T(8,128)(2,1)S(1)} collective-permute-done((bf16[512,1280]{1,0:T(8,128)(2,1)S(1)}, bf16[512,1280]{1,0:T(8,128)(2,1)S(1)}, u32[]{:S(2)}, u32[]{:S(2)}) %collective-permute-start.1) | collective-permute-done | bytes 1310752 | tf_op jit(solution)/shard_map/ppermute | solution.py:800
  40.4 1.9 broadcast_select_fusion.2.refs_0_.x_ref.refs_5_
  43.3 1.9 broadcast_select_fusion.1.refs_2_.refs_5_
  45.2 19.5 %collective-permute-start.4 = (bf16[512,1280]{1,0:T(8,128)(2,1)S(1)}, bf16[512,1280]{1,0:T(8,128)(2,1)}, u32[]{:S(2)}, u32[]{:S(2)}) collective-permute-start(bf16[512,1280]{1,0:T(8,128)(2,1)S(1)} %broadcast_select_fusion.1.refs_2_.refs_5_), channel_id=1, source_target_pairs={{0,4},{1,5},{2,6},{3,7},{4,0},{5,1},{6,2},{7,3},{8,12},{9,13},{10,... | collective-permute-start | bytes 3932168 | tf_op jit(solution)/shard_map/ppermute | solution.py:800
  66.2 1.3 fusion.3.place_ref.refs_1_
  68.1 1.4 copy.31.col_ref.refs_3_
  69.5 1.7 collective-permute-start.5
  71.2 2.0 all-gather.3.cloned.1.call-done.refs_4_.refs_5_.refs_6_.refs_2_.refs_3_.refs_8_
  73.2 18.8 %project.1 = (bf16[640,1024]{1,0:T(8,128)(2,1)}, bf16[640,2048]{1,0:T(8,128)(2,1)}, bf16[640,2048]{1,0:T(8,128)(2,1)}, bf16[1280,2048]{1,0:T(8,128)(2,1)}) custom-call(s32[1]{0:T(128)} %bitcast.core_ref, f32[1,1280]{1,0:T(1,128)} %reshape.111.gain_ref.refs_4_, f32[640,1]{1,0:T(8,128)} %broadcast_multiply_fusion.scale_ref, bf16[512,1280]{1,0:T(8,128)(2,1)} %copy-done, ...), custom_call_target="tpu_custom_call" | custom-call | flops 8388608000 | bytes 65536 | tf_op jit(solution)/shard_map/project/pallas_call | solution.py:75
  92.0 22.4 %attention_forward.1 = (bf16[640,512]{1,0:T(8,128)(2,1)}, bf16[640,512]{1,0:T(8,128)(2,1)}, f32[8,1,1024]{2,1,0:T(1,128)}) custom-call(s32[2048]{0:T(1024)} %copy-done.23, s32[24]{0:T(128)} %fusion.3.place_ref.refs_1_, s32[1,2048]{1,0:T(1,128)} %bitcast.37, s32[2048,1]{1,0:T(8,128)} %copy.31.col_ref.refs_3_, ...), custom_call_target="tpu_custom_call" | custom-call | flops 10307921920 | bytes 65536 | tf_op jit(solution)/shard_map/attention_forward/pallas_call | solution.py:495
  114.3 2.2 collective-permute-start.6
  118.3 1.2 broadcast_select_fusion.cot_ref
  119.5 16.1 %all-gather.5.cloned.1.call-done.w_ref = bf16[1280,3840]{1,0:T(8,128)(2,1)} async-done(((bf16[160,3840]{1,0:T(8,128)(2,1)}), bf16[1280,3840]{1,0:T(8,128)(2,1)}) %all-gather.5.cloned.1.call-update) | async-done | bytes 9830416 | tf_op jit(solution)/shard_map/all_gather | solution.py:878
  136.4 20.7 %mlp.1 = (bf16[512,1280]{1,0:T(8,128)(2,1)}, bf16[640,512]{1,0:T(8,128)(2,1)}, bf16[640,512]{1,0:T(8,128)(2,1)}, f32[512,1280]{1,0:T(8,128)}, bf16[1280,512]{1,0...) custom-call(s32[1]{0:T(128)} %bitcast.core_ref, ...), custom_call_target="tpu_custom_call" | custom-call | flops 10066329600 | bytes 65536 | tf_op jit(solution)/shard_map/mlp/pallas_call | solution.py:185
  157.5 11.2 %mlp_weights.1 = bf16[1280,3840]{1,0:T(8,128)(2,1)} custom-call(s32[1]{0:T(128)} %bitcast.core_ref, bf16[640,512]{1,0:T(8,128)(2,1)} %get-tuple-element.108.near_ref.refs_9_, bf16[640,512]{1,0:T(8,128)(2,1)} %copy-done.35, bf16[1280,512]{1,0:T(8,128)(2,1)} %get-tuple-element.112.ht_ref, bf16[1280,512]{1,0:T(8,128)(2,1)} %get-tuple-element.113.nt_ref, ...), custom_call_target="tpu_custom_call" | custom-call | flops 5033164800 | bytes 20971520 | tf_op jit(solution)/shard_map/mlp_weights/pallas_call | solution.py:258
  171.0 22.7 %attention_backward.2 = (f32[640,1024]{1,0:T(8,128)}, bf16[640,1024]{1,0:T(8,128)(2,1)}, bf16[640,1024]{1,0:T(8,128)(2,1)}) custom-call(s32[2048]{0:T(1024)} %copy-done.23, s32[24]{0:T(128)} %fusion.3.place_ref.refs_1_, s32[1,2048]{1,0:T(1,128)} %bitcast.38, s32[2048,1]{1,0:T(8,128)} %copy.31.col_ref.refs_3_, ...), custom_call_target="tpu_custom_call" | custom-call | flops 12884901888 | bytes 16777216 | tf_op jit(solution)/shard_map/attention_backward/pallas_call | solution.py:537
  193.8 12.9 %input_gradient.2 = (bf16[512,1280]{1,0:T(8,128)(2,1)}, bf16[512,1280]{1,0:T(8,128)(2,1)}, f32[1,1280]{1,0:T(1,128)}) custom-call(s32[1]{0:T(128)} %bitcast.core_ref, bf16[640,1024]{1,0:T(8,128)(2,1)} %get-tuple-element.122.refs_0_.dkb_ref, bf16[640,1024]{1,0:T(8,128)(2,1)} %get-tuple-element.123.refs_1_.dvb_ref, ...), custom_call_target="tpu_custom_call" | custom-call | flops 3355443200 | bytes 65536 | tf_op jit(solution)/shard_map/input_gradient/pallas_call | solution.py:681
  206.7 5.6 %collective-permute-start.9 = (bf16[512,1280]{1,0:T(8,128)(2,1)}, bf16[512,1280]{1,0:T(8,128)(2,1)S(1)}, u32[]{:S(2)}, u32[]{:S(2)}) collective-permute-start(bf16[512,1280]{1,0:T(8,128)(2,1)} %get-tuple-element.128), channel_id=1, source_target_pairs={{0,4},{1,5},{2,6},{3,7},{4,0},{5,1},{6,2},{7,3},{8,12},{9,13},{10,... | collective-permute-start | bytes 3932168 | tf_op jit(solution)/shard_map/ppermute | solution.py:800
  212.3 2.9 collective-permute-done.9
  215.1 1.7 add_convert_fusion
  216.9 24.2 %attention_backward.3 = (bf16[640,1024]{1,0:T(8,128)(2,1)}, bf16[640,1024]{1,0:T(8,128)(2,1)}, bf16[640,1024]{1,0:T(8,128)(2,1)}, f32[640,1]{1,0:T(8,128)}) custom-call(s32[2048]{0:T(1024)} %copy-done.23, s32[24]{0:T(128)} %fusion.3.place_ref.refs_1_, s32[1,2048]{1,0:T(1,128)} %bitcast.39, s32[2048,1]{1,0:T(8,128)} %copy.31.col_ref.refs_3_, ...), custom_call_target="tpu_custom_call" | custom-call | flops 12884901888 | bytes 16777216 | tf_op jit(solution)/shard_map/attention_backward/pallas_call | solution.py:537
  241.2 6.9 %collective-permute-done.10 = bf16[512,1280]{1,0:T(8,128)(2,1)} collective-permute-done((bf16[512,1280]{1,0:T(8,128)(2,1)S(1)}, bf16[512,1280]{1,0:T(8,128)(2,1)}, u32[]{:S(2)}, u32[]{:S(2)}) %collective-permute-start.10) | collective-permute-done | bytes 1310752 | tf_op jit(solution)/shard_map/ppermute | solution.py:800
  248.0 3.6 collective-permute-start.11
  252.3 11.2 %weight_gradient.2 = (bf16[320,960]{1,0:T(8,128)(2,1)}, bf16[320,960]{1,0:T(8,128)(2,1)}, bf16[320,960]{1,0:T(8,128)(2,1)}, bf16[320,960]{1,0:T(8,128)(2,1)}) custom-call(s32[4]{0:T(128)} %pad_add_fusion.at_ref, bf16[1280,2048]{1,0:T(8,128)(2,1)} %get-tuple-element.139.xt_ref, bf16[640,1024]{1,0:T(8,128)(2,1)} %get-tuple-element.158.dqt_ref.refs_7_, ...), custom_call_target="tpu_custom_call" | custom-call | flops 4194304000 | bytes 12582912 | tf_op jit(solution)/shard_map/weight_gradient/pallas_call | solution.py:590
  263.5 1.4 collective-permute-start.12
  265.5 1.5 collective-permute-start.14
  267.4 14.9 %input_gradient.3 = (bf16[512,1280]{1,0:T(8,128)(2,1)}, bf16[512,1280]{1,0:T(8,128)(2,1)}, f32[1,1280]{1,0:T(1,128)}) custom-call(s32[1]{0:T(128)} %bitcast.core_ref, bf16[640,1024]{1,0:T(8,128)(2,1)} %get-tuple-element.136.dka_ref.refs_0_, bf16[640,1024]{1,0:T(8,128)(2,1)} %get-tuple-element.137.dva_ref.refs_1_, ...), custom_call_target="tpu_custom_call" | custom-call | flops 5033164800 | bytes 65536 | tf_op jit(solution)/shard_map/input_gradient/pallas_call | solution.py:681
  282.3 12.7 %collective-permute-done.13 = bf16[320,960]{1,0:T(8,128)(2,1)S(1)} collective-permute-done((bf16[320,960]{1,0:T(8,128)(2,1)}, bf16[320,960]{1,0:T(8,128)(2,1)S(1)}, u32[]{:S(2)}, u32[]{:S(2)}) %collective-permute-start.13) | collective-permute-done | bytes 614432 | tf_op jit(solution)/shard_map/ppermute | solution.py:800
  296.0 2.1 collective-permute-start.16
  298.2 2.6 add_convert_fusion.2
  300.8 1.7 collective-permute-start.18
  302.5 11.1 %weight_gradient.3 = (bf16[320,960]{1,0:T(8,128)(2,1)}, bf16[320,960]{1,0:T(8,128)(2,1)}, bf16[320,960]{1,0:T(8,128)(2,1)}, bf16[320,960]{1,0:T(8,128)(2,1)}) custom-call(s32[4]{0:T(128)} %pad_add_fusion.at_ref, bf16[1280,2048]{1,0:T(8,128)(2,1)} %get-tuple-element.139.xt_ref, bf16[640,1024]{1,0:T(8,128)(2,1)} %get-tuple-element.158.dqt_ref.refs_7_, ...), custom_call_target="tpu_custom_call" | custom-call | flops 4194304000 | bytes 12582912 | tf_op jit(solution)/shard_map/weight_gradient/pallas_call | solution.py:590
  313.7 1.0 copy-done.6
  314.7 2.5 add_convert_fusion.6
  318.6 1.4 collective-permute-start.20
  320.0 1.4 collective-permute-start.21
  321.5 3.4 fusion.2
  324.9 1.7 collective-permute-start.28
  326.6 9.1 %collective-permute-done.19 = bf16[320,960]{1,0:T(8,128)(2,1)S(1)} collective-permute-done((bf16[320,960]{1,0:T(8,128)(2,1)}, bf16[320,960]{1,0:T(8,128)(2,1)S(1)}, u32[]{:S(2)}, u32[]{:S(2)}) %collective-permute-start.19) | collective-permute-done | bytes 614432 | tf_op jit(solution)/shard_map/ppermute | solution.py:800
  335.7 14.1 %collective-permute-done.20 = bf16[320,960]{1,0:T(8,128)(2,1)S(1)} collective-permute-done((bf16[320,960]{1,0:T(8,128)(2,1)}, bf16[320,960]{1,0:T(8,128)(2,1)S(1)}, u32[]{:S(2)}, u32[]{:S(2)}) %collective-permute-start.20) | collective-permute-done | bytes 614432 | tf_op jit(solution)/shard_map/ppermute | solution.py:800
  351.1 1.4 collective-permute-start.25
  352.7 9.8 %collective-permute-start.22 = (bf16[320,960]{1,0:T(8,128)(2,1)S(1)}, bf16[320,960]{1,0:T(8,128)(2,1)S(1)}, u32[]{:S(2)}, u32[]{:S(2)}) collective-permute-start(bf16[320,960]{1,0:T(8,128)(2,1)S(1)} %fusion.1), channel_id=1, source_target_pairs={{0,1},{3,2},{4,5},{7,6},{8,9},{11,10},{12,13},{15,14},{16,17},{19,... | collective-permute-start | bytes 1843208 | tf_op jit(solution)/shard_map/ppermute | solution.py:800
  362.5 1.3 collective-permute-start.23
  363.9 1.4 collective-permute-start.26
  365.3 3.0 add_convert_fusion.1
  368.3 1.3 collective-permute-start.31
  369.6 12.5 %collective-permute-done.23 = bf16[320,960]{1,0:T(8,128)(2,1)S(1)} collective-permute-done((bf16[320,960]{1,0:T(8,128)(2,1)S(1)}, bf16[320,960]{1,0:T(8,128)(2,1)S(1)}, u32[]{:S(2)}, u32[]{:S(2)}) %collective-permute-start.23) | collective-permute-done | bytes 614432 | tf_op jit(solution)/shard_map/ppermute | solution.py:800
  382.2 1.5 add_convert_fusion.4
  383.6 1.5 collective-permute-start.27
  385.1 2.5 select_bitcast_fusion.1
  387.8 1.5 add_convert_fusion.3
  389.3 1.7 collective-permute-start.30
  391.0 17.5 %collective-permute-done.31 = bf16[160,3840]{1,0:T(8,128)(2,1)} collective-permute-done((bf16[160,3840]{1,0:T(8,128)(2,1)}, bf16[160,3840]{1,0:T(8,128)(2,1)}, u32[]{:S(2)}, u32[]{:S(2)}) %collective-permute-start.31) | collective-permute-done | bytes 1228832 | tf_op jit(solution)/shard_map/ppermute | solution.py:800
  408.5 1.4 broadcast_select_fusion.3
  410.0 4.1 select_bitcast_fusion
  414.4 6.7 %collective-permute-done.30 = bf16[320,960]{1,0:T(8,128)(2,1)S(1)} collective-permute-done((bf16[320,960]{1,0:T(8,128)(2,1)S(1)}, bf16[320,960]{1,0:T(8,128)(2,1)S(1)}, u32[]{:S(2)}, u32[]{:S(2)}) %collective-permute-start.30) | collective-permute-done | bytes 614432 | tf_op jit(solution)/shard_map/ppermute | solution.py:800
  421.3 3.7 collective-permute-done.33
  425.0 1.4 collective-permute-start.34
  426.4 1.5 fusion.7
  427.9 2.0 collective-permute-done.34
  431.4 2.7 concatenate.11
  434.1 1.6 convert_element_type.153
  (160 shorter events, 17.5 us)
Async XLA Ops:
  7.2 65.9 %all-gather.3.cloned.1.call-start = ((), (), s32[]{:S(2)}) async-start(), calls=%async_computation.1 | async-start | bytes 11059200 | tf_op jit(solution)/shard_map/all_gather | solution.py:863
  8.0 127.6 %all-gather.5.cloned.1.call-start = ((), (), s32[]{:S(2)}) async-start(), calls=%async_computation.2 | async-start | bytes 11059200 | tf_op jit(solution)/shard_map/all_gather | solution.py:878
  9.6 238.5 %reduce-scatter.2.cloned.1.call-start = ((), (), s32[]{:S(2)}) async-start(), calls=%async_computation.3 | async-start | bytes 11059200 | tf_op jit(solution)/shard_map/reduce_scatter | solution.py:901
  9.6 30.7 %collective-permute-start.1 = (bf16[512,1280]{1,0:T(8,128)(2,1)S(1)}, bf16[512,1280]{1,0:T(8,128)(2,1)S(1)}, u32[]{:S(2)}, u32[]{:S(2)}) collective-permute-start(bf16[512,1280]{1,0:T(8,128)(2,1)S(1)} %bitcast.33), channel_id=1, source_target_pairs={{0,1},{1,0},{2,5},{3,4},{4,3},{5,2},{6,7},{7,6},{8,9},{9,8},{10,13... | collective-permute-start | bytes 3932168 | tf_op jit(solution)/shard_map/ppermute | solution.py:800
  42.3 22.4 %copy-start = (bf16[512,1280]{1,0:T(8,128)(2,1)}, bf16[512,1280]{1,0:T(8,128)(2,1)S(1)}, u32[]{:S(2)}) copy-start(bf16[512,1280]{1,0:T(8,128)(2,1)S(1)} %broadcast_select_fusion.2.refs_0_.x_ref.refs_5_) | copy-start | bytes 3932164
  42.3 22.4 %copy-start.24 = (s32[1,2048]{1,0:T(1,128)S(1)}, s32[1,2048]{1,0:T(1,128)}, u32[]{:S(2)}) copy-start(s32[1,2048]{1,0:T(1,128)} %param.14) | copy-start | bytes 24580
  42.3 22.9 %copy-start.36 = (bf16[80]{0:T(256)(128)(2,1)S(1)}, bf16[80]{0:T(256)(128)(2,1)}, u32[]{:S(2)}) copy-start(bf16[80]{0:T(256)(128)(2,1)} %param.23) | copy-start | bytes 484
  42.4 25.1 %copy-start.30 = (bf16[1280]{0:T(1024)(128)(2,1)S(1)}, bf16[1280]{0:T(1024)(128)(2,1)}, u32[]{:S(2)}) copy-start(bf16[1280]{0:T(1024)(128)(2,1)} %param.19) | copy-start | bytes 7684
  42.4 0.9 collective-permute-start.3
  45.2 28.0 %copy-start.1 = (bf16[512,1280]{1,0:T(8,128)(2,1)}, bf16[512,1280]{1,0:T(8,128)(2,1)S(1)}, u32[]{:S(2)}) copy-start(bf16[512,1280]{1,0:T(8,128)(2,1)S(1)} %broadcast_select_fusion.1.refs_2_.refs_5_) | copy-start | bytes 3932164
  45.2 24.3 %collective-permute-start.4 = (bf16[512,1280]{1,0:T(8,128)(2,1)S(1)}, bf16[512,1280]{1,0:T(8,128)(2,1)}, u32[]{:S(2)}, u32[]{:S(2)}) collective-permute-start(bf16[512,1280]{1,0:T(8,128)(2,1)S(1)} %broadcast_select_fusion.1.refs_2_.refs_5_), channel_id=1, source_target_pairs={{0,4},{1,5},{2,6},{3,7},{4,0},{5,1},{6,2},{7,3},{8,12},{9,13},{10,... | collective-permute-start | bytes 3932168 | tf_op jit(solution)/shard_map/ppermute | solution.py:800
  64.7 6.5 %collective-permute-start.2 = (bf16[512,1280]{1,0:T(8,128)(2,1)S(1)}, bf16[512,1280]{1,0:T(8,128)(2,1)}, u32[]{:S(2)}, u32[]{:S(2)}) collective-permute-start(bf16[512,1280]{1,0:T(8,128)(2,1)S(1)} %broadcast_select_fusion.2.refs_0_.x_ref.refs_5_), channel_id=1, source_target_pairs={{0,4},{1,5},{2,6},{3,7},{4,0},{5,1},{6,2},{7,3},{8,12},{9,13},{10,... | collective-permute-start | bytes 3932168 | tf_op jit(solution)/shard_map/ppermute | solution.py:800
  64.8 3.3 collective-permute-start
  65.4 26.5 %copy-start.17 = (f32[640,1]{1,0:T(8,128)}, f32[640,1]{1,0:T(8,128)S(1)}, u32[]{:S(2)}) copy-start(f32[640,1]{1,0:T(8,128)S(1)} %broadcast_in_dim_tile.4.refs_13_) | copy-start | bytes 7684
  68.1 23.8 %copy-start.23 = (s32[2048]{0:T(1024)}, s32[2048]{0:T(1024)S(1)}, u32[]{:S(2)}) copy-start(s32[2048]{0:T(1024)S(1)} %broadcast_select_fusion.10.ids_ref.refs_0_) | copy-start | bytes 24580
  69.5 44.8 %collective-permute-start.5 = (bf16[512,1280]{1,0:T(8,128)(2,1)}, bf16[512,1280]{1,0:T(8,128)(2,1)}, u32[]{:S(2)}, u32[]{:S(2)}) collective-permute-start(bf16[512,1280]{1,0:T(8,128)(2,1)} %bitcast.34), channel_id=1, source_target_pairs={{2,5},{3,4},{4,3},{5,2},{10,13},{11,12},{12,11},{13,10},{18,21},{1... | collective-permute-start | bytes 3932168 | tf_op jit(solution)/shard_map/ppermute | solution.py:800
  91.9 24.6 %copy-start.31 = (bf16[1280]{0:T(1024)(128)(2,1)S(1)}, bf16[1280]{0:T(1024)(128)(2,1)}, u32[]{:S(2)}) copy-start(bf16[1280]{0:T(1024)(128)(2,1)} %param.20) | copy-start | bytes 7684
  91.9 25.2 %copy-start.32 = (bf16[1280]{0:T(1024)(128)(2,1)S(1)}, bf16[1280]{0:T(1024)(128)(2,1)}, u32[]{:S(2)}) copy-start(bf16[1280]{0:T(1024)(128)(2,1)} %param.21) | copy-start | bytes 7684
  91.9 25.8 %copy-start.33 = (bf16[1280]{0:T(1024)(128)(2,1)S(1)}, bf16[1280]{0:T(1024)(128)(2,1)}, u32[]{:S(2)}) copy-start(bf16[1280]{0:T(1024)(128)(2,1)} %param.22) | copy-start | bytes 7684
  92.0 26.4 %copy-start.14 = (bf16[1,512,1280]{2,1,0:T(8,128)(2,1)S(1)}, bf16[1,512,1280]{2,1,0:T(8,128)(2,1)}, u32[]{:S(2)}) copy-start(bf16[1,512,1280]{2,1,0:T(8,128)(2,1)} %param.24) | copy-start | bytes 3932164
  114.3 21.3 %collective-permute-start.6 = (bf16[640,512]{1,0:T(8,128)(2,1)}, bf16[640,512]{1,0:T(8,128)(2,1)S(1)}, u32[]{:S(2)}, u32[]{:S(2)}) collective-permute-start(bf16[640,512]{1,0:T(8,128)(2,1)} %get-tuple-element.109.refs_10_), channel_id=1, source_target_pairs={{0,4},{1,5},{2,6},{3,7},{4,0},{5,1},{6,2},{7,3},{8,12},{9,13},{10,... | collective-permute-start | bytes 1966088 | tf_op jit(solution)/shard_map/ppermute | solution.py:800
  157.2 11.6 %collective-permute-start.7 = (bf16[640,512]{1,0:T(8,128)(2,1)}, bf16[640,512]{1,0:T(8,128)(2,1)S(1)}, u32[]{:S(2)}, u32[]{:S(2)}) collective-permute-start(bf16[640,512]{1,0:T(8,128)(2,1)} %get-tuple-element.116), channel_id=1, source_target_pairs={{0,4},{1,5},{2,6},{3,7},{4,0},{5,1},{6,2},{7,3},{8,12},{9,13},{10,... | collective-permute-start | bytes 1966088 | tf_op jit(solution)/shard_map/ppermute | solution.py:800
  170.3 36.4 %collective-permute-start.8 = (bf16[512,1280]{1,0:T(8,128)(2,1)S(1)}, bf16[512,1280]{1,0:T(8,128)(2,1)S(1)}, u32[]{:S(2)}, u32[]{:S(2)}) collective-permute-start(bf16[512,1280]{1,0:T(8,128)(2,1)S(1)} %copy-done.15), channel_id=1, source_target_pairs={{2,5},{3,4},{4,3},{5,2},{10,13},{11,12},{12,11},{13,10},{18,21},{1... | collective-permute-start | bytes 3932168 | tf_op jit(solution)/shard_map/ppermute | solution.py:800
  206.6 10.2 %copy-start.16 = (bf16[512,1280]{1,0:T(8,128)(2,1)}, bf16[512,1280]{1,0:T(8,128)(2,1)S(1)}, u32[]{:S(2)}) copy-start(bf16[512,1280]{1,0:T(8,128)(2,1)S(1)} %collective-permute-done.8) | copy-start | bytes 3932164
  206.7 8.5 %collective-permute-start.9 = (bf16[512,1280]{1,0:T(8,128)(2,1)}, bf16[512,1280]{1,0:T(8,128)(2,1)S(1)}, u32[]{:S(2)}, u32[]{:S(2)}) collective-permute-start(bf16[512,1280]{1,0:T(8,128)(2,1)} %get-tuple-element.128), channel_id=1, source_target_pairs={{0,4},{1,5},{2,6},{3,7},{4,0},{5,1},{6,2},{7,3},{8,12},{9,13},{10,... | collective-permute-start | bytes 3932168 | tf_op jit(solution)/shard_map/ppermute | solution.py:800
  216.8 31.2 %collective-permute-start.10 = (bf16[512,1280]{1,0:T(8,128)(2,1)S(1)}, bf16[512,1280]{1,0:T(8,128)(2,1)}, u32[]{:S(2)}, u32[]{:S(2)}) collective-permute-start(bf16[512,1280]{1,0:T(8,128)(2,1)S(1)} %add_convert_fusion), channel_id=1, source_target_pairs={{0,1},{1,0},{2,3},{3,2},{4,5},{5,4},{6,7},{7,6},{8,9},{9,8},{10,11... | collective-permute-start | bytes 3932168 | tf_op jit(solution)/shard_map/ppermute | solution.py:800
  248.0 47.0 %collective-permute-start.11 = (bf16[160,3840]{1,0:T(8,128)(2,1)}, bf16[160,3840]{1,0:T(8,128)(2,1)}, u32[]{:S(2)}, u32[]{:S(2)}) collective-permute-start(bf16[160,3840]{1,0:T(8,128)(2,1)} %reduce-scatter.2.cloned.1.call-done), channel_id=1, source_target_pairs={{0,1},{3,2},{4,5},{7,6},{8,9},{11,10},{12,13},{15,14},{16,17},{19,... | collective-permute-start | bytes 3686408 | tf_op jit(solution)/shard_map/ppermute | solution.py:800
  252.3 14.7 %copy-start.28 = (f32[1,1280]{1,0:T(1,128)S(1)}, f32[1,1280]{1,0:T(1,128)}, u32[]{:S(2)}) copy-start(f32[1,1280]{1,0:T(1,128)} %get-tuple-element.179) | copy-start | bytes 15364
  252.3 14.7 %copy-start.27 = (f32[1,1280]{1,0:T(1,128)S(1)}, f32[1,1280]{1,0:T(1,128)}, u32[]{:S(2)}) copy-start(f32[1,1280]{1,0:T(1,128)} %get-tuple-element.180) | copy-start | bytes 15364
  252.3 14.7 %copy-start.26 = (f32[1,1280]{1,0:T(1,128)S(1)}, f32[1,1280]{1,0:T(1,128)}, u32[]{:S(2)}) copy-start(f32[1,1280]{1,0:T(1,128)} %get-tuple-element.181) | copy-start | bytes 15364
  252.3 14.8 %copy-start.22 = (f32[640,1]{1,0:T(8,128)S(1)}, f32[640,1]{1,0:T(8,128)}, u32[]{:S(2)}) copy-start(f32[640,1]{1,0:T(8,128)} %get-tuple-element.182) | copy-start | bytes 7684
  263.5 18.8 %collective-permute-start.12 = (bf16[320,960]{1,0:T(8,128)(2,1)}, bf16[320,960]{1,0:T(8,128)(2,1)S(1)}, u32[]{:S(2)}, u32[]{:S(2)}) collective-permute-start(bf16[320,960]{1,0:T(8,128)(2,1)} %get-tuple-element.149), channel_id=1, source_target_pairs={{0,8},{1,9},{2,10},{3,11},{4,12},{5,13},{6,14},{7,15},{8,0},{9,1},... | collective-permute-start | bytes 1843208 | tf_op jit(solution)/shard_map/ppermute | solution.py:800
  264.9 30.1 %collective-permute-start.13 = (bf16[320,960]{1,0:T(8,128)(2,1)}, bf16[320,960]{1,0:T(8,128)(2,1)S(1)}, u32[]{:S(2)}, u32[]{:S(2)}) collective-permute-start(bf16[320,960]{1,0:T(8,128)(2,1)} %get-tuple-element.150), channel_id=1, source_target_pairs={{0,16},{1,17},{2,18},{3,19},{4,20},{5,21},{6,22},{7,23},{8,24},{9,... | collective-permute-start | bytes 1843208 | tf_op jit(solution)/shard_map/ppermute | solution.py:800
  265.5 29.5 %collective-permute-start.14 = (bf16[320,960]{1,0:T(8,128)(2,1)}, bf16[320,960]{1,0:T(8,128)(2,1)S(1)}, u32[]{:S(2)}, u32[]{:S(2)}) collective-permute-start(bf16[320,960]{1,0:T(8,128)(2,1)} %get-tuple-element.151), channel_id=1, source_target_pairs={{0,24},{1,25},{2,26},{3,27},{4,28},{5,29},{6,30},{7,31},{8,16},{9,... | collective-permute-start | bytes 1843208 | tf_op jit(solution)/shard_map/ppermute | solution.py:800
  267.4 27.7 %copy-start.9 = (bf16[320,960]{1,0:T(8,128)(2,1)S(1)}, bf16[320,960]{1,0:T(8,128)(2,1)}, u32[]{:S(2)}) copy-start(bf16[320,960]{1,0:T(8,128)(2,1)} %get-tuple-element.154) | copy-start | bytes 1843204
  282.3 13.3 %copy-start.10 = (bf16[320,960]{1,0:T(8,128)(2,1)}, bf16[320,960]{1,0:T(8,128)(2,1)S(1)}, u32[]{:S(2)}) copy-start(bf16[320,960]{1,0:T(8,128)(2,1)S(1)} %collective-permute-done.12) | copy-start | bytes 1843204
  295.0 3.2 copy-start.18
  296.0 17.6 %collective-permute-start.16 = (bf16[320,960]{1,0:T(8,128)(2,1)S(1)}, bf16[320,960]{1,0:T(8,128)(2,1)}, u32[]{:S(2)}, u32[]{:S(2)}) collective-permute-start(bf16[320,960]{1,0:T(8,128)(2,1)S(1)} %fusion), channel_id=1, source_target_pairs={{0,1},{3,2},{4,5},{7,6},{8,9},{11,10},{12,13},{15,14},{16,17},{19,... | collective-permute-start | bytes 1843208 | tf_op jit(solution)/shard_map/ppermute | solution.py:800
  298.2 15.5 %collective-permute-start.15 = (bf16[512,1280]{1,0:T(8,128)(2,1)}, bf16[512,1280]{1,0:T(8,128)(2,1)S(1)}, u32[]{:S(2)}, u32[]{:S(2)}) collective-permute-start(bf16[512,1280]{1,0:T(8,128)(2,1)} %get-tuple-element.153), channel_id=1, source_target_pairs={{0,4},{1,5},{2,6},{3,7},{4,0},{5,1},{6,2},{7,3},{8,12},{9,13},{10,... | collective-permute-start | bytes 3932168 | tf_op jit(solution)/shard_map/ppermute | solution.py:800
  300.8 24.1 %collective-permute-start.18 = (bf16[160,3840]{1,0:T(8,128)(2,1)}, bf16[160,3840]{1,0:T(8,128)(2,1)}, u32[]{:S(2)}, u32[]{:S(2)}) collective-permute-start(bf16[160,3840]{1,0:T(8,128)(2,1)} %add_convert_fusion.2), channel_id=1, source_target_pairs={{1,2},{2,1},{5,6},{6,5},{9,10},{10,9},{13,14},{14,13},{17,18},{18,... | collective-permute-start | bytes 3686408 | tf_op jit(solution)/shard_map/ppermute | solution.py:800
  314.7 6.8 %copy-start.2 = (f32[512,1280]{1,0:T(8,128)S(1)}, f32[512,1280]{1,0:T(8,128)}, u32[]{:S(2)}) copy-start(f32[512,1280]{1,0:T(8,128)} %get-tuple-element.164) | copy-start | bytes 7864324
  314.7 6.8 %copy-start.4 = (bf16[512,1280]{1,0:T(8,128)(2,1)S(1)}, bf16[512,1280]{1,0:T(8,128)(2,1)}, u32[]{:S(2)}) copy-start(bf16[512,1280]{1,0:T(8,128)(2,1)} %get-tuple-element.152) | copy-start | bytes 3932164
  317.2 9.4 %collective-permute-start.17 = (bf16[320,960]{1,0:T(8,128)(2,1)S(1)}, bf16[320,960]{1,0:T(8,128)(2,1)S(1)}, u32[]{:S(2)}, u32[]{:S(2)}) collective-permute-start(bf16[320,960]{1,0:T(8,128)(2,1)S(1)} %add_convert_fusion.6), channel_id=1, source_target_pairs={{1,2},{2,1},{5,6},{6,5},{9,10},{10,9},{13,14},{14,13},{17,18},{18,... | collective-permute-start | bytes 1843208 | tf_op jit(solution)/shard_map/ppermute | solution.py:800
  317.9 17.8 %collective-permute-start.19 = (bf16[320,960]{1,0:T(8,128)(2,1)}, bf16[320,960]{1,0:T(8,128)(2,1)S(1)}, u32[]{:S(2)}, u32[]{:S(2)}) collective-permute-start(bf16[320,960]{1,0:T(8,128)(2,1)} %get-tuple-element.170), channel_id=1, source_target_pairs={{0,8},{1,9},{2,10},{3,11},{4,12},{5,13},{6,14},{7,15},{8,0},{9,1},... | collective-permute-start | bytes 1843208 | tf_op jit(solution)/shard_map/ppermute | solution.py:800
  318.6 31.1 %collective-permute-start.20 = (bf16[320,960]{1,0:T(8,128)(2,1)}, bf16[320,960]{1,0:T(8,128)(2,1)S(1)}, u32[]{:S(2)}, u32[]{:S(2)}) collective-permute-start(bf16[320,960]{1,0:T(8,128)(2,1)} %get-tuple-element.171), channel_id=1, source_target_pairs={{0,16},{1,17},{2,18},{3,19},{4,20},{5,21},{6,22},{7,23},{8,24},{9,... | collective-permute-start | bytes 1843208 | tf_op jit(solution)/shard_map/ppermute | solution.py:800
  320.0 29.8 %collective-permute-start.21 = (bf16[320,960]{1,0:T(8,128)(2,1)}, bf16[320,960]{1,0:T(8,128)(2,1)S(1)}, u32[]{:S(2)}, u32[]{:S(2)}) collective-permute-start(bf16[320,960]{1,0:T(8,128)(2,1)} %get-tuple-element.172), channel_id=1, source_target_pairs={{0,24},{1,25},{2,26},{3,27},{4,28},{5,29},{6,30},{7,31},{8,16},{9,... | collective-permute-start | bytes 1843208 | tf_op jit(solution)/shard_map/ppermute | solution.py:800
  321.4 28.3 %copy-start.25 = (f32[1,1280]{1,0:T(1,128)S(1)}, f32[1,1280]{1,0:T(1,128)}, u32[]{:S(2)}) copy-start(f32[1,1280]{1,0:T(1,128)} %get-tuple-element.177) | copy-start | bytes 15364
  321.4 28.3 %copy-start.29 = (f32[1,1280]{1,0:T(1,128)S(1)}, f32[1,1280]{1,0:T(1,128)}, u32[]{:S(2)}) copy-start(f32[1,1280]{1,0:T(1,128)} %get-tuple-element.178) | copy-start | bytes 15364
  321.4 28.5 %copy-start.8 = (bf16[320,960]{1,0:T(8,128)(2,1)S(1)}, bf16[320,960]{1,0:T(8,128)(2,1)}, u32[]{:S(2)}) copy-start(bf16[320,960]{1,0:T(8,128)(2,1)} %get-tuple-element.166) | copy-start | bytes 1843204
  324.9 62.8 %collective-permute-start.28 = (bf16[512,1280]{1,0:T(8,128)(2,1)}, bf16[512,1280]{1,0:T(8,128)(2,1)}, u32[]{:S(2)}, u32[]{:S(2)}) collective-permute-start(bf16[512,1280]{1,0:T(8,128)(2,1)} %fusion.2), channel_id=1, source_target_pairs={{2,5},{3,4},{4,3},{5,2},{10,13},{11,12},{12,11},{13,10},{18,21},{1... | collective-permute-start | bytes 3932168 | tf_op jit(solution)/shard_map/ppermute | solution.py:800
  349.9 1.3 collective-permute-start.24
  351.1 12.7 %collective-permute-start.25 = (f32[48,128]{1,0:T(8,128)S(1)}, f32[48,128]{1,0:T(8,128)S(1)}, u32[]{:S(2)}, u32[]{:S(2)}) collective-permute-start(f32[48,128]{1,0:T(8,128)S(1)} %fusion.6), channel_id=1, source_target_pairs={{0,8},{1,9},{2,10},{3,11},{4,12},{5,13},{6,14},{7,15},{8,0},{9,1},... | collective-permute-start | bytes 73736 | tf_op jit(solution)/shard_map/ppermute | solution.py:800
  352.7 29.4 %collective-permute-start.22 = (bf16[320,960]{1,0:T(8,128)(2,1)S(1)}, bf16[320,960]{1,0:T(8,128)(2,1)S(1)}, u32[]{:S(2)}, u32[]{:S(2)}) collective-permute-start(bf16[320,960]{1,0:T(8,128)(2,1)S(1)} %fusion.1), channel_id=1, source_target_pairs={{0,1},{3,2},{4,5},{7,6},{8,9},{11,10},{12,13},{15,14},{16,17},{19,... | collective-permute-start | bytes 1843208 | tf_op jit(solution)/shard_map/ppermute | solution.py:800
  362.5 19.5 %collective-permute-start.23 = (bf16[320,960]{1,0:T(8,128)(2,1)S(1)}, bf16[320,960]{1,0:T(8,128)(2,1)S(1)}, u32[]{:S(2)}, u32[]{:S(2)}) collective-permute-start(bf16[320,960]{1,0:T(8,128)(2,1)S(1)} %add_convert_fusion.5), channel_id=1, source_target_pairs={{1,0},{2,3},{5,4},{6,7},{9,8},{10,11},{13,12},{14,15},{17,16},{18,... | collective-permute-start | bytes 1843208 | tf_op jit(solution)/shard_map/ppermute | solution.py:800
  363.9 5.7 %collective-permute-start.26 = (f32[48,128]{1,0:T(8,128)S(1)}, f32[48,128]{1,0:T(8,128)S(1)}, u32[]{:S(2)}, u32[]{:S(2)}) collective-permute-start(f32[48,128]{1,0:T(8,128)S(1)} %fusion.12), channel_id=1, source_target_pairs={{0,16},{1,17},{2,18},{3,19},{4,20},{5,21},{6,22},{7,23},{8,24},{9,... | collective-permute-start | bytes 73736 | tf_op jit(solution)/shard_map/ppermute | solution.py:800
  368.3 40.3 %collective-permute-start.31 = (bf16[160,3840]{1,0:T(8,128)(2,1)}, bf16[160,3840]{1,0:T(8,128)(2,1)}, u32[]{:S(2)}, u32[]{:S(2)}) collective-permute-start(bf16[160,3840]{1,0:T(8,128)(2,1)} %add_convert_fusion.1), channel_id=1, source_target_pairs={{1,0},{2,3},{5,4},{6,7},{9,8},{10,11},{13,12},{14,15},{17,16},{18,... | collective-permute-start | bytes 3686408 | tf_op jit(solution)/shard_map/ppermute | solution.py:800
  383.6 4.0 collective-permute-start.27
  387.7 26.4 %collective-permute-start.29 = (bf16[160,960]{1,0:T(8,128)(2,1)S(1)}, bf16[160,960]{1,0:T(8,128)(2,1)S(1)}, u32[]{:S(2)}, u32[]{:S(2)}) collective-permute-start(bf16[160,960]{1,0:T(8,128)(2,1)S(1)} %constant_dynamic-slice_fusion.1), channel_id=1, source_target_pairs={{0,4},{1,5},{2,6},{3,7},{4,0},{5,1},{6,2},{7,3},{8,12},{9,13},{10,... | collective-permute-start | bytes 921608 | tf_op jit(solution)/shard_map/ppermute | solution.py:800
  389.3 20.7 %copy-start.5 = (bf16[512,1280]{1,0:T(8,128)(2,1)S(1)}, bf16[512,1280]{1,0:T(8,128)(2,1)}, u32[]{:S(2)}) copy-start(bf16[512,1280]{1,0:T(8,128)(2,1)} %get-tuple-element.152) | copy-start | bytes 3932164
  389.3 20.7 %copy-start.7 = (bf16[512,1280]{1,0:T(8,128)(2,1)S(1)}, bf16[512,1280]{1,0:T(8,128)(2,1)}, u32[]{:S(2)}) copy-start(bf16[512,1280]{1,0:T(8,128)(2,1)} %copy-done.6) | copy-start | bytes 3932164
  389.3 31.7 %collective-permute-start.30 = (bf16[320,960]{1,0:T(8,128)(2,1)S(1)}, bf16[320,960]{1,0:T(8,128)(2,1)S(1)}, u32[]{:S(2)}, u32[]{:S(2)}) collective-permute-start(bf16[320,960]{1,0:T(8,128)(2,1)S(1)} %add_convert_fusion.3), channel_id=1, source_target_pairs={{1,0},{2,3},{5,4},{6,7},{9,8},{10,11},{13,12},{14,15},{17,16},{18,... | collective-permute-start | bytes 1843208 | tf_op jit(solution)/shard_map/ppermute | solution.py:800
  421.1 3.9 collective-permute-start.33
  421.2 9.8 %collective-permute-start.32 = (bf16[160,960]{1,0:T(8,128)(2,1)S(1)}, bf16[160,960]{1,0:T(8,128)(2,1)S(1)}, u32[]{:S(2)}, u32[]{:S(2)}) collective-permute-start(bf16[160,960]{1,0:T(8,128)(2,1)S(1)} %constant_dynamic-slice_fusion), channel_id=1, source_target_pairs={{0,4},{1,5},{2,6},{3,7},{4,0},{5,1},{6,2},{7,3},{8,12},{9,13},{10,... | collective-permute-start | bytes 921608 | tf_op jit(solution)/shard_map/ppermute | solution.py:800
  425.0 4.9 %collective-permute-start.34 = (f32[48,128]{1,0:T(8,128)S(1)}, f32[48,128]{1,0:T(8,128)S(1)}, u32[]{:S(2)}, u32[]{:S(2)}) collective-permute-start(f32[48,128]{1,0:T(8,128)S(1)} %add.124), channel_id=1, source_target_pairs={{0,2},{1,3},{2,0},{3,1},{4,6},{5,7},{6,4},{7,5},{8,10},{9,11},{10,... | collective-permute-start | bytes 73736 | tf_op jit(solution)/shard_map/ppermute | solution.py:800
  (11 other events, 13.1 us)
Sparse Core Ops, SparseCore 0:
  9.9 63.1 all-gather.2
  75.0 60.5 all-gather.4
  168.9 78.2 reduce-scatter.1

commit v2 on v1

--- a/solution.py
+++ b/solution.py
@@ -948,18 +948,6 @@
     held_a, line_a = line_inward(add_up(grads_a, came_a), plan, BF)
     held_o, line_o = line_across(held_o, line_o, plan, BF)
     grads_b = weight_gradient(xt, last_dq, early_kv, late_kv, at, pairs, 1)
-    got, line_a, *grads_b = tie(got, line_a, *grads_b)
-    came_b = to_owners(grads_b)
-    total = near_dx.astype(F32) + got.astype(F32) + grad_middle
-    for one in turned:
-        total = total + one.astype(F32)
-    last = send(total.astype(BF), plan.mirror())
-    held_a, line_a = line_across(held_a, line_a, plan, BF)
-    gain_early, line_a, line_o, *came_b = tie(gain_early, line_a, line_o, *came_b)
-    held_b, line_b = line_inward(add_up(grads_b, came_b), plan, BF)
-    line_a = line_outward(line_joined(held_a, line_a), plan, z)
-    others = line_outward(line_joined(held_o, line_o), plan, z)
-
     scale_slope = SOFT_FACTOR / math.sqrt(hd) * scale_exp / (1.0 + scale_exp)
     grad_scale = jnp.sum(gs.reshape(heads // 2, hd), 0)
     grad_scale = grad_scale * scale_slope / (scale_dim * LOG2E)
@@ -976,7 +964,19 @@
     while mask < pairs:
         small = small + send(small, plan.pair_swap(mask))
         mask *= 2
-    line_b, line_a, small = tie(line_b, line_a, small)
+    got, line_a, small, *grads_b = tie(got, line_a, small, *grads_b)
+    came_b = to_owners(grads_b)
+    total = near_dx.astype(F32) + got.astype(F32) + grad_middle
+    for one in turned:
+        total = total + one.astype(F32)
+    last = send(total.astype(BF), plan.mirror())
+    held_a, line_a = line_across(held_a, line_a, plan, BF)
+    line_a, line_o, *came_b = tie(line_a, line_o, *came_b)
+    held_b, line_b = line_inward(add_up(grads_b, came_b), plan, BF)
+    line_a = line_outward(line_joined(held_a, line_a), plan, z)
+    others = line_outward(line_joined(held_o, line_o), plan, z)
+
+    line_b, line_a = tie(line_b, line_a)
     held_b, line_b = line_across(held_b, line_b, plan, BF)
 
     def owned_rows(value):
@@ -985,11 +985,13 @@
         came = send(give, core_swap)
         return jnp.where(core == 0, keep, came), jnp.where(core == 0, came, keep)
 
-    line_b, line_a, last = tie(line_b, line_a, last)
+    line_b, line_a, last, small = tie(line_b, line_a, last, small)
     swapped_a = owned_rows(line_a)
     line_b = line_outward(line_joined(held_b, line_b), plan, z)
-    line_b, others, small = tie(line_b, others, small)
-    mask = 1
+    came = send(small, plan.line_swap(1))
+    line_b, others, came = tie(line_b, others, came)
+    small = small + came
+    mask = 2
     while mask < n:
         small = small + send(small, plan.line_swap(mask))
         mask *= 2

time: 450 us -> 446 us (level)
  waiting for transfers between devices: 135 us -> 128 us
    ppermute x35, waiting for transfers between devices: 116 us -> 111 us  [send(): return lax.ppermute(value, AXES, pairs)]
  transfers between devices with their start and end apart: 38 -> 38, of which waited for: 14 -> 14; matrix products, arithmetic and copies ran while one was open for 9% -> 10% of each run, Pallas kernels for 34% -> 35%
where the time goes in v2:
time: 446 us; the launch traced here: 439 us
  Pallas kernels  174 us (39%)
  waiting for transfers between devices  128 us (29%)
  starting transfers between devices  69.1 us (15%)
  other arithmetic  37.2 us (8%)
  local copies, waits for them, and re-layouts  15.2 us (3%)
  between operations  14.8 us (3%)
    ppermute x35, waiting for transfers between devices, send(): return lax.ppermute(value, AXES, pairs)  111 us
    ppermute x35, starting transfers between devices, send(): return lax.ppermute(value, AXES, pairs)  69 us
    pallas_call x2, Pallas kernels, attention_backward(): pl.pallas_call(functools.partial(backward_kernel, hd, tile, base, count,...  49.4 us
    pallas_call x2, Pallas kernels, input_gradient(): pl.pallas_call(functools.partial(dx_kernel, part, bool(dqs), n), grid_spe...  27.7 us
    pallas_call x1, Pallas kernels, attention_forward(): pl.pallas_call(functools.partial(forward_kernel, hd, tile), grid=(heads /...  24.2 us
    pallas_call x2, Pallas kernels, weight_gradient(): pl.pallas_call(functools.partial(weight_kernel, size, nq), grid_spec=pltp...  22.2 us
    pallas_call x1, Pallas kernels, mlp(): pl.pallas_call(functools.partial(mlp_kernel, part), grid_spec=pltpu.Prefe...  20.7 us
    pallas_call x1, Pallas kernels, project(): pl.pallas_call(functools.partial(project_kernel, part, query_slots, n), g...  18.8 us
  transfers between devices with their start and end apart: 38, of which 14 were waited for; matrix products, arithmetic and copies ran while one was open for 10% of the time, Pallas kernels for 35%

profile of v2, /device:TPU:0, one launch (start us, length us, event | category | flops | bytes accessed | tf_op | source)
XLA Modules:
  0.0 438.7 jit_solution(6406079321952975409)
XLA Ops:
  8.4 1.1 pad_maximum_fusion
  9.6 3.1 collective-permute-start.1
  12.7 27.7 %collective-permute-done.1 = bf16[512,1280]{1,0:T(8,128)(2,1)S(1)} collective-permute-done((bf16[512,1280]{1,0:T(8,128)(2,1)S(1)}, bf16[512,1280]{1,0:T(8,128)(2,1)S(1)}, u32[]{:S(2)}, u32[]{:S(2)}) %collective-permute-start.1) | collective-permute-done | bytes 1310752 | tf_op jit(solution)/shard_map/ppermute | solution.py:800
  40.4 1.9 broadcast_select_fusion.2.refs_0_.x_ref.refs_5_
  42.4 0.9 collective-permute-start.3
  43.3 1.9 broadcast_select_fusion.1.refs_2_.refs_5_
  45.2 19.5 %collective-permute-start.4 = (bf16[512,1280]{1,0:T(8,128)(2,1)S(1)}, bf16[512,1280]{1,0:T(8,128)(2,1)}, u32[]{:S(2)}, u32[]{:S(2)}) collective-permute-start(bf16[512,1280]{1,0:T(8,128)(2,1)S(1)} %broadcast_select_fusion.1.refs_2_.refs_5_), channel_id=1, source_target_pairs={{0,4},{1,5},{2,6},{3,7},{4,0},{5,1},{6,2},{7,3},{8,12},{9,13},{10,... | collective-permute-start | bytes 3932168 | tf_op jit(solution)/shard_map/ppermute | solution.py:800
  66.2 1.3 fusion.3.place_ref.refs_1_
  68.1 1.4 copy.31.col_ref.refs_3_
  69.5 1.7 collective-permute-start.5
  71.2 2.0 all-gather.3.cloned.1.call-done.refs_4_.refs_5_.refs_6_.refs_2_.refs_3_.refs_8_
  73.2 18.8 %project.1 = (bf16[640,1024]{1,0:T(8,128)(2,1)}, bf16[640,2048]{1,0:T(8,128)(2,1)}, bf16[640,2048]{1,0:T(8,128)(2,1)}, bf16[1280,2048]{1,0:T(8,128)(2,1)}) custom-call(s32[1]{0:T(128)} %bitcast.core_ref, f32[1,1280]{1,0:T(1,128)} %reshape.111.gain_ref.refs_4_, f32[640,1]{1,0:T(8,128)} %broadcast_multiply_fusion.scale_ref, bf16[512,1280]{1,0:T(8,128)(2,1)} %copy-done, ...), custom_call_target="tpu_custom_call" | custom-call | flops 8388608000 | bytes 65536 | tf_op jit(solution)/shard_map/project/pallas_call | solution.py:75
  92.0 24.2 %attention_forward.1 = (bf16[640,512]{1,0:T(8,128)(2,1)}, bf16[640,512]{1,0:T(8,128)(2,1)}, f32[8,1,1024]{2,1,0:T(1,128)}) custom-call(s32[2048]{0:T(1024)} %copy-done.24, s32[24]{0:T(128)} %fusion.3.place_ref.refs_1_, s32[1,2048]{1,0:T(1,128)} %bitcast.37, s32[2048,1]{1,0:T(8,128)} %copy.31.col_ref.refs_3_, ...), custom_call_target="tpu_custom_call" | custom-call | flops 10307921920 | bytes 65536 | tf_op jit(solution)/shard_map/attention_forward/pallas_call | solution.py:495
  116.2 2.2 collective-permute-start.6
  120.1 1.2 broadcast_select_fusion.cot_ref
  121.3 14.3 %all-gather.5.cloned.1.call-done.w_ref = bf16[1280,3840]{1,0:T(8,128)(2,1)} async-done(((bf16[160,3840]{1,0:T(8,128)(2,1)}), bf16[1280,3840]{1,0:T(8,128)(2,1)}) %all-gather.5.cloned.1.call-update) | async-done | bytes 9830416 | tf_op jit(solution)/shard_map/all_gather | solution.py:878
  135.6 0.8 copy-done.35
  136.4 20.7 %mlp.1 = (bf16[512,1280]{1,0:T(8,128)(2,1)}, bf16[640,512]{1,0:T(8,128)(2,1)}, bf16[640,512]{1,0:T(8,128)(2,1)}, f32[512,1280]{1,0:T(8,128)}, bf16[1280,512]{1,0...) custom-call(s32[1]{0:T(128)} %bitcast.core_ref, ...), custom_call_target="tpu_custom_call" | custom-call | flops 10066329600 | bytes 65536 | tf_op jit(solution)/shard_map/mlp/pallas_call | solution.py:185
  157.4 11.2 %mlp_weights.1 = bf16[1280,3840]{1,0:T(8,128)(2,1)} custom-call(s32[1]{0:T(128)} %bitcast.core_ref, bf16[640,512]{1,0:T(8,128)(2,1)} %get-tuple-element.108.near_ref.refs_9_, bf16[640,512]{1,0:T(8,128)(2,1)} %copy-done.35, bf16[1280,512]{1,0:T(8,128)(2,1)} %get-tuple-element.112.ht_ref, bf16[1280,512]{1,0:T(8,128)(2,1)} %get-tuple-element.113.nt_ref, ...), custom_call_target="tpu_custom_call" | custom-call | flops 5033164800 | bytes 20971520 | tf_op jit(solution)/shard_map/mlp_weights/pallas_call | solution.py:258
  171.0 22.7 %attention_backward.2 = (f32[640,1024]{1,0:T(8,128)}, bf16[640,1024]{1,0:T(8,128)(2,1)}, bf16[640,1024]{1,0:T(8,128)(2,1)}) custom-call(s32[2048]{0:T(1024)} %copy-done.24, s32[24]{0:T(128)} %fusion.3.place_ref.refs_1_, s32[1,2048]{1,0:T(1,128)} %bitcast.38, s32[2048,1]{1,0:T(8,128)} %copy.31.col_ref.refs_3_, ...), custom_call_target="tpu_custom_call" | custom-call | flops 12884901888 | bytes 16777216 | tf_op jit(solution)/shard_map/attention_backward/pallas_call | solution.py:537
  193.7 12.9 %input_gradient.2 = (bf16[512,1280]{1,0:T(8,128)(2,1)}, bf16[512,1280]{1,0:T(8,128)(2,1)}, f32[1,1280]{1,0:T(1,128)}) custom-call(s32[1]{0:T(128)} %bitcast.core_ref, bf16[640,1024]{1,0:T(8,128)(2,1)} %get-tuple-element.122.refs_0_.dkb_ref, bf16[640,1024]{1,0:T(8,128)(2,1)} %get-tuple-element.123.refs_1_.dvb_ref, ...), custom_call_target="tpu_custom_call" | custom-call | flops 3355443200 | bytes 65536 | tf_op jit(solution)/shard_map/input_gradient/pallas_call | solution.py:681
  206.6 5.6 %collective-permute-start.9 = (bf16[512,1280]{1,0:T(8,128)(2,1)}, bf16[512,1280]{1,0:T(8,128)(2,1)S(1)}, u32[]{:S(2)}, u32[]{:S(2)}) collective-permute-start(bf16[512,1280]{1,0:T(8,128)(2,1)} %get-tuple-element.128), channel_id=1, source_target_pairs={{0,4},{1,5},{2,6},{3,7},{4,0},{5,1},{6,2},{7,3},{8,12},{9,13},{10,... | collective-permute-start | bytes 3932168 | tf_op jit(solution)/shard_map/ppermute | solution.py:800
  212.2 2.9 collective-permute-done.9
  215.1 1.7 add_convert_fusion
  216.9 26.7 %attention_backward.3 = (bf16[640,1024]{1,0:T(8,128)(2,1)}, bf16[640,1024]{1,0:T(8,128)(2,1)}, bf16[640,1024]{1,0:T(8,128)(2,1)}, f32[640,1]{1,0:T(8,128)}) custom-call(s32[2048]{0:T(1024)} %copy-done.24, s32[24]{0:T(128)} %fusion.3.place_ref.refs_1_, s32[1,2048]{1,0:T(1,128)} %bitcast.39, s32[2048,1]{1,0:T(8,128)} %copy.31.col_ref.refs_3_, ...), custom_call_target="tpu_custom_call" | custom-call | flops 12884901888 | bytes 16777216 | tf_op jit(solution)/shard_map/attention_backward/pallas_call | solution.py:537
  243.6 4.4 %collective-permute-done.10 = bf16[512,1280]{1,0:T(8,128)(2,1)} collective-permute-done((bf16[512,1280]{1,0:T(8,128)(2,1)S(1)}, bf16[512,1280]{1,0:T(8,128)(2,1)}, u32[]{:S(2)}, u32[]{:S(2)}) %collective-permute-start.10) | collective-permute-done | bytes 1310752 | tf_op jit(solution)/shard_map/ppermute | solution.py:800
  248.0 3.6 collective-permute-start.11
  252.3 11.2 %weight_gradient.2 = (bf16[320,960]{1,0:T(8,128)(2,1)}, bf16[320,960]{1,0:T(8,128)(2,1)}, bf16[320,960]{1,0:T(8,128)(2,1)}, bf16[320,960]{1,0:T(8,128)(2,1)}) custom-call(s32[4]{0:T(128)} %pad_add_fusion.at_ref, bf16[1280,2048]{1,0:T(8,128)(2,1)} %get-tuple-element.139.xt_ref, bf16[640,1024]{1,0:T(8,128)(2,1)} %get-tuple-element.164.dqt_ref.refs_7_, ...), custom_call_target="tpu_custom_call" | custom-call | flops 4194304000 | bytes 12582912 | tf_op jit(solution)/shard_map/weight_gradient/pallas_call | solution.py:590
  263.4 1.4 collective-permute-start.12
  265.5 1.4 collective-permute-start.14
  267.3 14.9 %input_gradient.3 = (bf16[512,1280]{1,0:T(8,128)(2,1)}, bf16[512,1280]{1,0:T(8,128)(2,1)}, f32[1,1280]{1,0:T(1,128)}) custom-call(s32[1]{0:T(128)} %bitcast.core_ref, bf16[640,1024]{1,0:T(8,128)(2,1)} %get-tuple-element.136.dka_ref.refs_0_, bf16[640,1024]{1,0:T(8,128)(2,1)} %get-tuple-element.137.dva_ref.refs_1_, ...), custom_call_target="tpu_custom_call" | custom-call | flops 5033164800 | bytes 65536 | tf_op jit(solution)/shard_map/input_gradient/pallas_call | solution.py:681
  282.2 12.8 %collective-permute-done.13 = bf16[320,960]{1,0:T(8,128)(2,1)S(1)} collective-permute-done((bf16[320,960]{1,0:T(8,128)(2,1)}, bf16[320,960]{1,0:T(8,128)(2,1)S(1)}, u32[]{:S(2)}, u32[]{:S(2)}) %collective-permute-start.13) | collective-permute-done | bytes 614432 | tf_op jit(solution)/shard_map/ppermute | solution.py:800
  296.4 3.0 add_convert_fusion.2
  300.2 1.3 fusion
  301.5 1.3 collective-permute-start.16
  302.8 1.7 collective-permute-start.21
  304.6 1.4 collective-permute-start.19
  306.0 11.1 %weight_gradient.3 = (bf16[320,960]{1,0:T(8,128)(2,1)}, bf16[320,960]{1,0:T(8,128)(2,1)}, bf16[320,960]{1,0:T(8,128)(2,1)}, bf16[320,960]{1,0:T(8,128)(2,1)}) custom-call(s32[4]{0:T(128)} %pad_add_fusion.at_ref, bf16[1280,2048]{1,0:T(8,128)(2,1)} %get-tuple-element.139.xt_ref, bf16[640,1024]{1,0:T(8,128)(2,1)} %get-tuple-element.164.dqt_ref.refs_7_, ...), custom_call_target="tpu_custom_call" | custom-call | flops 4194304000 | bytes 12582912 | tf_op jit(solution)/shard_map/weight_gradient/pallas_call | solution.py:590
  317.4 0.8 copy-done.19
  318.6 2.5 add_convert_fusion.6
  321.8 1.4 collective-permute-start.22
  323.9 1.4 collective-permute-start.24
  325.4 3.3 fusion.2
  328.7 1.9 collective-permute-start.28
  330.6 9.2 %collective-permute-done.22 = bf16[320,960]{1,0:T(8,128)(2,1)S(1)} collective-permute-done((bf16[320,960]{1,0:T(8,128)(2,1)}, bf16[320,960]{1,0:T(8,128)(2,1)S(1)}, u32[]{:S(2)}, u32[]{:S(2)}) %collective-permute-start.22) | collective-permute-done | bytes 614432 | tf_op jit(solution)/shard_map/ppermute | solution.py:800
  339.7 13.4 %collective-permute-done.23 = bf16[320,960]{1,0:T(8,128)(2,1)S(1)} collective-permute-done((bf16[320,960]{1,0:T(8,128)(2,1)}, bf16[320,960]{1,0:T(8,128)(2,1)S(1)}, u32[]{:S(2)}, u32[]{:S(2)}) %collective-permute-start.23) | collective-permute-done | bytes 614432 | tf_op jit(solution)/shard_map/ppermute | solution.py:800
  353.9 9.3 %collective-permute-start.25 = (bf16[320,960]{1,0:T(8,128)(2,1)S(1)}, bf16[320,960]{1,0:T(8,128)(2,1)S(1)}, u32[]{:S(2)}, u32[]{:S(2)}) collective-permute-start(bf16[320,960]{1,0:T(8,128)(2,1)S(1)} %fusion.1), channel_id=1, source_target_pairs={{0,1},{3,2},{4,5},{7,6},{8,9},{11,10},{12,13},{15,14},{16,17},{19,... | collective-permute-start | bytes 1843208 | tf_op jit(solution)/shard_map/ppermute | solution.py:800
  363.2 1.3 collective-permute-start.26
  364.5 3.0 add_convert_fusion.1
  367.5 1.3 collective-permute-start.31
  368.7 14.0 %collective-permute-done.26 = bf16[320,960]{1,0:T(8,128)(2,1)S(1)} collective-permute-done((bf16[320,960]{1,0:T(8,128)(2,1)S(1)}, bf16[320,960]{1,0:T(8,128)(2,1)S(1)}, u32[]{:S(2)}, u32[]{:S(2)}) %collective-permute-start.26) | collective-permute-done | bytes 614432 | tf_op jit(solution)/shard_map/ppermute | solution.py:800
  382.8 1.5 add_convert_fusion.4
  384.3 1.5 collective-permute-start.27
  385.8 2.5 select_bitcast_fusion.1
  388.4 1.5 add_convert_fusion.3
  390.0 1.4 collective-permute-start.30
  391.4 17.8 %collective-permute-done.31 = bf16[160,3840]{1,0:T(8,128)(2,1)} collective-permute-done((bf16[160,3840]{1,0:T(8,128)(2,1)}, bf16[160,3840]{1,0:T(8,128)(2,1)}, u32[]{:S(2)}, u32[]{:S(2)}) %collective-permute-start.31) | collective-permute-done | bytes 1228832 | tf_op jit(solution)/shard_map/ppermute | solution.py:800
  409.2 1.4 broadcast_select_fusion.3
  410.6 4.1 select_bitcast_fusion
  415.0 5.9 %collective-permute-done.30 = bf16[320,960]{1,0:T(8,128)(2,1)S(1)} collective-permute-done((bf16[320,960]{1,0:T(8,128)(2,1)S(1)}, bf16[320,960]{1,0:T(8,128)(2,1)S(1)}, u32[]{:S(2)}, u32[]{:S(2)}) %collective-permute-start.30) | collective-permute-done | bytes 614432 | tf_op jit(solution)/shard_map/ppermute | solution.py:800
  421.8 1.5 fusion.7
  423.3 2.7 collective-permute-done.34
  427.4 2.7 concatenate.11
  430.1 1.6 convert_element_type.153
  (160 shorter events, 17.4 us)
Async XLA Ops:
  7.2 65.9 %all-gather.3.cloned.1.call-start = ((), (), s32[]{:S(2)}) async-start(), calls=%async_computation.1 | async-start | bytes 11059200 | tf_op jit(solution)/shard_map/all_gather | solution.py:863
  8.0 127.6 %all-gather.5.cloned.1.call-start = ((), (), s32[]{:S(2)}) async-start(), calls=%async_computation.2 | async-start | bytes 11059200 | tf_op jit(solution)/shard_map/all_gather | solution.py:878
  9.6 238.4 %reduce-scatter.2.cloned.1.call-start = ((), (), s32[]{:S(2)}) async-start(), calls=%async_computation.3 | async-start | bytes 11059200 | tf_op jit(solution)/shard_map/reduce_scatter | solution.py:901
  9.6 30.7 %collective-permute-start.1 = (bf16[512,1280]{1,0:T(8,128)(2,1)S(1)}, bf16[512,1280]{1,0:T(8,128)(2,1)S(1)}, u32[]{:S(2)}, u32[]{:S(2)}) collective-permute-start(bf16[512,1280]{1,0:T(8,128)(2,1)S(1)} %bitcast.33), channel_id=1, source_target_pairs={{0,1},{1,0},{2,5},{3,4},{4,3},{5,2},{6,7},{7,6},{8,9},{9,8},{10,13... | collective-permute-start | bytes 3932168 | tf_op jit(solution)/shard_map/ppermute | solution.py:800
  42.3 22.4 %copy-start = (bf16[512,1280]{1,0:T(8,128)(2,1)}, bf16[512,1280]{1,0:T(8,128)(2,1)S(1)}, u32[]{:S(2)}) copy-start(bf16[512,1280]{1,0:T(8,128)(2,1)S(1)} %broadcast_select_fusion.2.refs_0_.x_ref.refs_5_) | copy-start | bytes 3932164
  42.3 22.4 %copy-start.25 = (s32[1,2048]{1,0:T(1,128)S(1)}, s32[1,2048]{1,0:T(1,128)}, u32[]{:S(2)}) copy-start(s32[1,2048]{1,0:T(1,128)} %param.14) | copy-start | bytes 24580
  42.3 22.9 %copy-start.36 = (bf16[80]{0:T(256)(128)(2,1)S(1)}, bf16[80]{0:T(256)(128)(2,1)}, u32[]{:S(2)}) copy-start(bf16[80]{0:T(256)(128)(2,1)} %param.23) | copy-start | bytes 484
  42.4 25.1 %copy-start.30 = (bf16[1280]{0:T(1024)(128)(2,1)S(1)}, bf16[1280]{0:T(1024)(128)(2,1)}, u32[]{:S(2)}) copy-start(bf16[1280]{0:T(1024)(128)(2,1)} %param.19) | copy-start | bytes 7684
  42.4 0.9 collective-permute-start.3
  45.2 28.0 %copy-start.1 = (bf16[512,1280]{1,0:T(8,128)(2,1)}, bf16[512,1280]{1,0:T(8,128)(2,1)S(1)}, u32[]{:S(2)}) copy-start(bf16[512,1280]{1,0:T(8,128)(2,1)S(1)} %broadcast_select_fusion.1.refs_2_.refs_5_) | copy-start | bytes 3932164
  45.2 24.3 %collective-permute-start.4 = (bf16[512,1280]{1,0:T(8,128)(2,1)S(1)}, bf16[512,1280]{1,0:T(8,128)(2,1)}, u32[]{:S(2)}, u32[]{:S(2)}) collective-permute-start(bf16[512,1280]{1,0:T(8,128)(2,1)S(1)} %broadcast_select_fusion.1.refs_2_.refs_5_), channel_id=1, source_target_pairs={{0,4},{1,5},{2,6},{3,7},{4,0},{5,1},{6,2},{7,3},{8,12},{9,13},{10,... | collective-permute-start | bytes 3932168 | tf_op jit(solution)/shard_map/ppermute | solution.py:800
  64.7 6.5 %collective-permute-start.2 = (bf16[512,1280]{1,0:T(8,128)(2,1)S(1)}, bf16[512,1280]{1,0:T(8,128)(2,1)}, u32[]{:S(2)}, u32[]{:S(2)}) collective-permute-start(bf16[512,1280]{1,0:T(8,128)(2,1)S(1)} %broadcast_select_fusion.2.refs_0_.x_ref.refs_5_), channel_id=1, source_target_pairs={{0,4},{1,5},{2,6},{3,7},{4,0},{5,1},{6,2},{7,3},{8,12},{9,13},{10,... | collective-permute-start | bytes 3932168 | tf_op jit(solution)/shard_map/ppermute | solution.py:800
  64.8 3.3 collective-permute-start
  65.4 26.5 %copy-start.18 = (f32[640,1]{1,0:T(8,128)}, f32[640,1]{1,0:T(8,128)S(1)}, u32[]{:S(2)}) copy-start(f32[640,1]{1,0:T(8,128)S(1)} %broadcast_in_dim_tile.4.refs_13_) | copy-start | bytes 7684
  68.1 23.8 %copy-start.24 = (s32[2048]{0:T(1024)}, s32[2048]{0:T(1024)S(1)}, u32[]{:S(2)}) copy-start(s32[2048]{0:T(1024)S(1)} %broadcast_select_fusion.10.ids_ref.refs_0_) | copy-start | bytes 24580
  69.5 46.7 %collective-permute-start.5 = (bf16[512,1280]{1,0:T(8,128)(2,1)}, bf16[512,1280]{1,0:T(8,128)(2,1)}, u32[]{:S(2)}, u32[]{:S(2)}) collective-permute-start(bf16[512,1280]{1,0:T(8,128)(2,1)} %bitcast.34), channel_id=1, source_target_pairs={{2,5},{3,4},{4,3},{5,2},{10,13},{11,12},{12,11},{13,10},{18,21},{1... | collective-permute-start | bytes 3932168 | tf_op jit(solution)/shard_map/ppermute | solution.py:800
  91.9 26.4 %copy-start.31 = (bf16[1280]{0:T(1024)(128)(2,1)S(1)}, bf16[1280]{0:T(1024)(128)(2,1)}, u32[]{:S(2)}) copy-start(bf16[1280]{0:T(1024)(128)(2,1)} %param.20) | copy-start | bytes 7684
  91.9 27.0 %copy-start.32 = (bf16[1280]{0:T(1024)(128)(2,1)S(1)}, bf16[1280]{0:T(1024)(128)(2,1)}, u32[]{:S(2)}) copy-start(bf16[1280]{0:T(1024)(128)(2,1)} %param.21) | copy-start | bytes 7684
  91.9 27.6 %copy-start.33 = (bf16[1280]{0:T(1024)(128)(2,1)S(1)}, bf16[1280]{0:T(1024)(128)(2,1)}, u32[]{:S(2)}) copy-start(bf16[1280]{0:T(1024)(128)(2,1)} %param.22) | copy-start | bytes 7684
  91.9 28.2 %copy-start.15 = (bf16[1,512,1280]{2,1,0:T(8,128)(2,1)S(1)}, bf16[1,512,1280]{2,1,0:T(8,128)(2,1)}, u32[]{:S(2)}) copy-start(bf16[1,512,1280]{2,1,0:T(8,128)(2,1)} %param.24) | copy-start | bytes 3932164
  116.2 19.4 %collective-permute-start.6 = (bf16[640,512]{1,0:T(8,128)(2,1)}, bf16[640,512]{1,0:T(8,128)(2,1)S(1)}, u32[]{:S(2)}, u32[]{:S(2)}) collective-permute-start(bf16[640,512]{1,0:T(8,128)(2,1)} %get-tuple-element.109.refs_10_), channel_id=1, source_target_pairs={{0,4},{1,5},{2,6},{3,7},{4,0},{5,1},{6,2},{7,3},{8,12},{9,13},{10,... | collective-permute-start | bytes 1966088 | tf_op jit(solution)/shard_map/ppermute | solution.py:800
  157.1 11.6 %collective-permute-start.7 = (bf16[640,512]{1,0:T(8,128)(2,1)}, bf16[640,512]{1,0:T(8,128)(2,1)S(1)}, u32[]{:S(2)}, u32[]{:S(2)}) collective-permute-start(bf16[640,512]{1,0:T(8,128)(2,1)} %get-tuple-element.116), channel_id=1, source_target_pairs={{0,4},{1,5},{2,6},{3,7},{4,0},{5,1},{6,2},{7,3},{8,12},{9,13},{10,... | collective-permute-start | bytes 1966088 | tf_op jit(solution)/shard_map/ppermute | solution.py:800
  170.2 36.4 %collective-permute-start.8 = (bf16[512,1280]{1,0:T(8,128)(2,1)S(1)}, bf16[512,1280]{1,0:T(8,128)(2,1)S(1)}, u32[]{:S(2)}, u32[]{:S(2)}) collective-permute-start(bf16[512,1280]{1,0:T(8,128)(2,1)S(1)} %copy-done.16), channel_id=1, source_target_pairs={{2,5},{3,4},{4,3},{5,2},{10,13},{11,12},{12,11},{13,10},{18,21},{1... | collective-permute-start | bytes 3932168 | tf_op jit(solution)/shard_map/ppermute | solution.py:800
  206.6 10.2 %copy-start.17 = (bf16[512,1280]{1,0:T(8,128)(2,1)}, bf16[512,1280]{1,0:T(8,128)(2,1)S(1)}, u32[]{:S(2)}) copy-start(bf16[512,1280]{1,0:T(8,128)(2,1)S(1)} %collective-permute-done.8) | copy-start | bytes 3932164
  206.6 8.5 %collective-permute-start.9 = (bf16[512,1280]{1,0:T(8,128)(2,1)}, bf16[512,1280]{1,0:T(8,128)(2,1)S(1)}, u32[]{:S(2)}, u32[]{:S(2)}) collective-permute-start(bf16[512,1280]{1,0:T(8,128)(2,1)} %get-tuple-element.128), channel_id=1, source_target_pairs={{0,4},{1,5},{2,6},{3,7},{4,0},{5,1},{6,2},{7,3},{8,12},{9,13},{10,... | collective-permute-start | bytes 3932168 | tf_op jit(solution)/shard_map/ppermute | solution.py:800
  216.8 31.2 %collective-permute-start.10 = (bf16[512,1280]{1,0:T(8,128)(2,1)S(1)}, bf16[512,1280]{1,0:T(8,128)(2,1)}, u32[]{:S(2)}, u32[]{:S(2)}) collective-permute-start(bf16[512,1280]{1,0:T(8,128)(2,1)S(1)} %add_convert_fusion), channel_id=1, source_target_pairs={{0,1},{1,0},{2,3},{3,2},{4,5},{5,4},{6,7},{7,6},{8,9},{9,8},{10,11... | collective-permute-start | bytes 3932168 | tf_op jit(solution)/shard_map/ppermute | solution.py:800
  248.0 47.0 %collective-permute-start.11 = (bf16[160,3840]{1,0:T(8,128)(2,1)}, bf16[160,3840]{1,0:T(8,128)(2,1)}, u32[]{:S(2)}, u32[]{:S(2)}) collective-permute-start(bf16[160,3840]{1,0:T(8,128)(2,1)} %reduce-scatter.2.cloned.1.call-done), channel_id=1, source_target_pairs={{0,1},{3,2},{4,5},{7,6},{8,9},{11,10},{12,13},{15,14},{16,17},{19,... | collective-permute-start | bytes 3686408 | tf_op jit(solution)/shard_map/ppermute | solution.py:800
  252.2 14.7 %copy-start.28 = (f32[1,1280]{1,0:T(1,128)S(1)}, f32[1,1280]{1,0:T(1,128)}, u32[]{:S(2)}) copy-start(f32[1,1280]{1,0:T(1,128)} %get-tuple-element.160) | copy-start | bytes 15364
  252.2 14.7 %copy-start.27 = (f32[1,1280]{1,0:T(1,128)S(1)}, f32[1,1280]{1,0:T(1,128)}, u32[]{:S(2)}) copy-start(f32[1,1280]{1,0:T(1,128)} %get-tuple-element.161) | copy-start | bytes 15364
  252.2 14.7 %copy-start.26 = (f32[1,1280]{1,0:T(1,128)S(1)}, f32[1,1280]{1,0:T(1,128)}, u32[]{:S(2)}) copy-start(f32[1,1280]{1,0:T(1,128)} %get-tuple-element.162) | copy-start | bytes 15364
  252.3 14.8 %copy-start.23 = (f32[640,1]{1,0:T(8,128)S(1)}, f32[640,1]{1,0:T(8,128)}, u32[]{:S(2)}) copy-start(f32[640,1]{1,0:T(8,128)} %get-tuple-element.163) | copy-start | bytes 7684
  263.4 18.7 %collective-permute-start.12 = (bf16[320,960]{1,0:T(8,128)(2,1)}, bf16[320,960]{1,0:T(8,128)(2,1)S(1)}, u32[]{:S(2)}, u32[]{:S(2)}) collective-permute-start(bf16[320,960]{1,0:T(8,128)(2,1)} %get-tuple-element.149), channel_id=1, source_target_pairs={{0,8},{1,9},{2,10},{3,11},{4,12},{5,13},{6,14},{7,15},{8,0},{9,1},... | collective-permute-start | bytes 1843208 | tf_op jit(solution)/shard_map/ppermute | solution.py:800
  264.8 30.2 %collective-permute-start.13 = (bf16[320,960]{1,0:T(8,128)(2,1)}, bf16[320,960]{1,0:T(8,128)(2,1)S(1)}, u32[]{:S(2)}, u32[]{:S(2)}) collective-permute-start(bf16[320,960]{1,0:T(8,128)(2,1)} %get-tuple-element.150), channel_id=1, source_target_pairs={{0,16},{1,17},{2,18},{3,19},{4,20},{5,21},{6,22},{7,23},{8,24},{9,... | collective-permute-start | bytes 1843208 | tf_op jit(solution)/shard_map/ppermute | solution.py:800
  265.5 29.5 %collective-permute-start.14 = (bf16[320,960]{1,0:T(8,128)(2,1)}, bf16[320,960]{1,0:T(8,128)(2,1)S(1)}, u32[]{:S(2)}, u32[]{:S(2)}) collective-permute-start(bf16[320,960]{1,0:T(8,128)(2,1)} %get-tuple-element.151), channel_id=1, source_target_pairs={{0,24},{1,25},{2,26},{3,27},{4,28},{5,29},{6,30},{7,31},{8,16},{9,... | collective-permute-start | bytes 1843208 | tf_op jit(solution)/shard_map/ppermute | solution.py:800
  267.3 27.7 %copy-start.29 = (f32[1,1280]{1,0:T(1,128)S(1)}, f32[1,1280]{1,0:T(1,128)}, u32[]{:S(2)}) copy-start(f32[1,1280]{1,0:T(1,128)} %get-tuple-element.158) | copy-start | bytes 15364
  282.2 18.0 %copy-start.9 = (bf16[320,960]{1,0:T(8,128)(2,1)}, bf16[320,960]{1,0:T(8,128)(2,1)S(1)}, u32[]{:S(2)}) copy-start(bf16[320,960]{1,0:T(8,128)(2,1)S(1)} %collective-permute-done.12) | copy-start | bytes 1843204
  295.0 5.2 %copy-start.10 = (bf16[320,960]{1,0:T(8,128)(2,1)}, bf16[320,960]{1,0:T(8,128)(2,1)S(1)}, u32[]{:S(2)}) copy-start(bf16[320,960]{1,0:T(8,128)(2,1)S(1)} %collective-permute-done.13) | copy-start | bytes 1843204
  295.8 4.3 copy-start.8
  295.8 3.5 collective-permute-start.17
  295.9 4.2 copy-start.12
  295.9 21.4 %collective-permute-start.15 = (bf16[512,1280]{1,0:T(8,128)(2,1)}, bf16[512,1280]{1,0:T(8,128)(2,1)S(1)}, u32[]{:S(2)}, u32[]{:S(2)}) collective-permute-start(bf16[512,1280]{1,0:T(8,128)(2,1)} %get-tuple-element.153), channel_id=1, source_target_pairs={{0,4},{1,5},{2,6},{3,7},{4,0},{5,1},{6,2},{7,3},{8,12},{9,13},{10,... | collective-permute-start | bytes 3932168 | tf_op jit(solution)/shard_map/ppermute | solution.py:800
  299.4 5.1 %collective-permute-start.18 = (f32[48,128]{1,0:T(8,128)S(1)}, f32[48,128]{1,0:T(8,128)S(1)}, u32[]{:S(2)}, u32[]{:S(2)}) collective-permute-start(f32[48,128]{1,0:T(8,128)S(1)} %fusion.6), channel_id=1, source_target_pairs={{0,8},{1,9},{2,10},{3,11},{4,12},{5,13},{6,14},{7,15},{8,0},{9,1},... | collective-permute-start | bytes 73736 | tf_op jit(solution)/shard_map/ppermute | solution.py:800
  301.5 15.9 %collective-permute-start.16 = (bf16[320,960]{1,0:T(8,128)(2,1)}, bf16[320,960]{1,0:T(8,128)(2,1)S(1)}, u32[]{:S(2)}, u32[]{:S(2)}) collective-permute-start(bf16[320,960]{1,0:T(8,128)(2,1)} %fusion), channel_id=1, source_target_pairs={{0,1},{3,2},{4,5},{7,6},{8,9},{11,10},{12,13},{15,14},{16,17},{19,... | collective-permute-start | bytes 1843208 | tf_op jit(solution)/shard_map/ppermute | solution.py:800
  302.8 25.9 %collective-permute-start.21 = (bf16[160,3840]{1,0:T(8,128)(2,1)}, bf16[160,3840]{1,0:T(8,128)(2,1)}, u32[]{:S(2)}, u32[]{:S(2)}) collective-permute-start(bf16[160,3840]{1,0:T(8,128)(2,1)} %add_convert_fusion.2), channel_id=1, source_target_pairs={{1,2},{2,1},{5,6},{6,5},{9,10},{10,9},{13,14},{14,13},{17,18},{18,... | collective-permute-start | bytes 3686408 | tf_op jit(solution)/shard_map/ppermute | solution.py:800
  304.6 12.5 %collective-permute-start.19 = (f32[48,128]{1,0:T(8,128)S(1)}, f32[48,128]{1,0:T(8,128)S(1)}, u32[]{:S(2)}, u32[]{:S(2)}) collective-permute-start(f32[48,128]{1,0:T(8,128)S(1)} %fusion.12), channel_id=1, source_target_pairs={{0,16},{1,17},{2,18},{3,19},{4,20},{5,21},{6,22},{7,23},{8,24},{9,... | collective-permute-start | bytes 73736 | tf_op jit(solution)/shard_map/ppermute | solution.py:800
  318.6 6.8 %copy-start.2 = (f32[512,1280]{1,0:T(8,128)S(1)}, f32[512,1280]{1,0:T(8,128)}, u32[]{:S(2)}) copy-start(f32[512,1280]{1,0:T(8,128)} %get-tuple-element.170) | copy-start | bytes 7864324
  318.6 6.8 %copy-start.4 = (bf16[512,1280]{1,0:T(8,128)(2,1)S(1)}, bf16[512,1280]{1,0:T(8,128)(2,1)}, u32[]{:S(2)}) copy-start(bf16[512,1280]{1,0:T(8,128)(2,1)} %get-tuple-element.152) | copy-start | bytes 3932164
  321.1 9.5 %collective-permute-start.20 = (bf16[320,960]{1,0:T(8,128)(2,1)S(1)}, bf16[320,960]{1,0:T(8,128)(2,1)S(1)}, u32[]{:S(2)}, u32[]{:S(2)}) collective-permute-start(bf16[320,960]{1,0:T(8,128)(2,1)S(1)} %add_convert_fusion.6), channel_id=1, source_target_pairs={{1,2},{2,1},{5,6},{6,5},{9,10},{10,9},{13,14},{14,13},{17,18},{18,... | collective-permute-start | bytes 1843208 | tf_op jit(solution)/shard_map/ppermute | solution.py:800
  321.8 17.9 %collective-permute-start.22 = (bf16[320,960]{1,0:T(8,128)(2,1)}, bf16[320,960]{1,0:T(8,128)(2,1)S(1)}, u32[]{:S(2)}, u32[]{:S(2)}) collective-permute-start(bf16[320,960]{1,0:T(8,128)(2,1)} %get-tuple-element.175), channel_id=1, source_target_pairs={{0,8},{1,9},{2,10},{3,11},{4,12},{5,13},{6,14},{7,15},{8,0},{9,1},... | collective-permute-start | bytes 1843208 | tf_op jit(solution)/shard_map/ppermute | solution.py:800
  323.2 29.9 %collective-permute-start.23 = (bf16[320,960]{1,0:T(8,128)(2,1)}, bf16[320,960]{1,0:T(8,128)(2,1)S(1)}, u32[]{:S(2)}, u32[]{:S(2)}) collective-permute-start(bf16[320,960]{1,0:T(8,128)(2,1)} %get-tuple-element.176), channel_id=1, source_target_pairs={{0,16},{1,17},{2,18},{3,19},{4,20},{5,21},{6,22},{7,23},{8,24},{9,... | collective-permute-start | bytes 1843208 | tf_op jit(solution)/shard_map/ppermute | solution.py:800
  323.9 29.2 %collective-permute-start.24 = (bf16[320,960]{1,0:T(8,128)(2,1)}, bf16[320,960]{1,0:T(8,128)(2,1)S(1)}, u32[]{:S(2)}, u32[]{:S(2)}) collective-permute-start(bf16[320,960]{1,0:T(8,128)(2,1)} %get-tuple-element.177), channel_id=1, source_target_pairs={{0,24},{1,25},{2,26},{3,27},{4,28},{5,29},{6,30},{7,31},{8,16},{9,... | collective-permute-start | bytes 1843208 | tf_op jit(solution)/shard_map/ppermute | solution.py:800
  328.7 24.7 %copy-start.13 = (bf16[320,960]{1,0:T(8,128)(2,1)S(1)}, bf16[320,960]{1,0:T(8,128)(2,1)}, u32[]{:S(2)}) copy-start(bf16[320,960]{1,0:T(8,128)(2,1)} %get-tuple-element.172) | copy-start | bytes 1843204
  328.7 59.6 %collective-permute-start.28 = (bf16[512,1280]{1,0:T(8,128)(2,1)}, bf16[512,1280]{1,0:T(8,128)(2,1)}, u32[]{:S(2)}, u32[]{:S(2)}) collective-permute-start(bf16[512,1280]{1,0:T(8,128)(2,1)} %fusion.2), channel_id=1, source_target_pairs={{2,5},{3,4},{4,3},{5,2},{10,13},{11,12},{12,11},{13,10},{18,21},{1... | collective-permute-start | bytes 3932168 | tf_op jit(solution)/shard_map/ppermute | solution.py:800
  353.9 28.9 %collective-permute-start.25 = (bf16[320,960]{1,0:T(8,128)(2,1)S(1)}, bf16[320,960]{1,0:T(8,128)(2,1)S(1)}, u32[]{:S(2)}, u32[]{:S(2)}) collective-permute-start(bf16[320,960]{1,0:T(8,128)(2,1)S(1)} %fusion.1), channel_id=1, source_target_pairs={{0,1},{3,2},{4,5},{7,6},{8,9},{11,10},{12,13},{15,14},{16,17},{19,... | collective-permute-start | bytes 1843208 | tf_op jit(solution)/shard_map/ppermute | solution.py:800
  363.2 19.6 %collective-permute-start.26 = (bf16[320,960]{1,0:T(8,128)(2,1)S(1)}, bf16[320,960]{1,0:T(8,128)(2,1)S(1)}, u32[]{:S(2)}, u32[]{:S(2)}) collective-permute-start(bf16[320,960]{1,0:T(8,128)(2,1)S(1)} %add_convert_fusion.5), channel_id=1, source_target_pairs={{1,0},{2,3},{5,4},{6,7},{9,8},{10,11},{13,12},{14,15},{17,16},{18,... | collective-permute-start | bytes 1843208 | tf_op jit(solution)/shard_map/ppermute | solution.py:800
  367.5 41.7 %collective-permute-start.31 = (bf16[160,3840]{1,0:T(8,128)(2,1)}, bf16[160,3840]{1,0:T(8,128)(2,1)}, u32[]{:S(2)}, u32[]{:S(2)}) collective-permute-start(bf16[160,3840]{1,0:T(8,128)(2,1)} %add_convert_fusion.1), channel_id=1, source_target_pairs={{1,0},{2,3},{5,4},{6,7},{9,8},{10,11},{13,12},{14,15},{17,16},{18,... | collective-permute-start | bytes 3686408 | tf_op jit(solution)/shard_map/ppermute | solution.py:800
  384.3 4.0 collective-permute-start.27
  388.4 26.4 %collective-permute-start.29 = (bf16[160,960]{1,0:T(8,128)(2,1)S(1)}, bf16[160,960]{1,0:T(8,128)(2,1)S(1)}, u32[]{:S(2)}, u32[]{:S(2)}) collective-permute-start(bf16[160,960]{1,0:T(8,128)(2,1)S(1)} %constant_dynamic-slice_fusion.1), channel_id=1, source_target_pairs={{0,4},{1,5},{2,6},{3,7},{4,0},{5,1},{6,2},{7,3},{8,12},{9,13},{10,... | collective-permute-start | bytes 921608 | tf_op jit(solution)/shard_map/ppermute | solution.py:800
  390.0 20.7 %copy-start.5 = (bf16[512,1280]{1,0:T(8,128)(2,1)S(1)}, bf16[512,1280]{1,0:T(8,128)(2,1)}, u32[]{:S(2)}) copy-start(bf16[512,1280]{1,0:T(8,128)(2,1)} %get-tuple-element.152) | copy-start | bytes 3932164
  390.0 20.7 %copy-start.7 = (bf16[512,1280]{1,0:T(8,128)(2,1)S(1)}, bf16[512,1280]{1,0:T(8,128)(2,1)}, u32[]{:S(2)}) copy-start(bf16[512,1280]{1,0:T(8,128)(2,1)} %copy-done.6) | copy-start | bytes 3932164
  390.0 31.0 %collective-permute-start.30 = (bf16[320,960]{1,0:T(8,128)(2,1)S(1)}, bf16[320,960]{1,0:T(8,128)(2,1)S(1)}, u32[]{:S(2)}, u32[]{:S(2)}) collective-permute-start(bf16[320,960]{1,0:T(8,128)(2,1)S(1)} %add_convert_fusion.3), channel_id=1, source_target_pairs={{1,0},{2,3},{5,4},{6,7},{9,8},{10,11},{13,12},{14,15},{17,16},{18,... | collective-permute-start | bytes 1843208 | tf_op jit(solution)/shard_map/ppermute | solution.py:800
  414.7 6.5 %collective-permute-start.32 = (f32[48,128]{1,0:T(8,128)S(1)}, f32[48,128]{1,0:T(8,128)S(1)}, u32[]{:S(2)}, u32[]{:S(2)}) collective-permute-start(f32[48,128]{1,0:T(8,128)S(1)} %add.109), channel_id=1, source_target_pairs={{0,1},{1,0},{2,3},{3,2},{4,5},{5,4},{6,7},{7,6},{8,9},{9,8},{10,11... | collective-permute-start | bytes 73736 | tf_op jit(solution)/shard_map/ppermute | solution.py:800
  421.2 4.7 %collective-permute-start.34 = (f32[48,128]{1,0:T(8,128)S(1)}, f32[48,128]{1,0:T(8,128)S(1)}, u32[]{:S(2)}, u32[]{:S(2)}) collective-permute-start(f32[48,128]{1,0:T(8,128)S(1)} %add.124), channel_id=1, source_target_pairs={{0,2},{1,3},{2,0},{3,1},{4,6},{5,7},{6,4},{7,5},{8,10},{9,11},{10,... | collective-permute-start | bytes 73736 | tf_op jit(solution)/shard_map/ppermute | solution.py:800
  421.7 5.4 %collective-permute-start.33 = (bf16[160,960]{1,0:T(8,128)(2,1)S(1)}, bf16[160,960]{1,0:T(8,128)(2,1)S(1)}, u32[]{:S(2)}, u32[]{:S(2)}) collective-permute-start(bf16[160,960]{1,0:T(8,128)(2,1)S(1)} %constant_dynamic-slice_fusion), channel_id=1, source_target_pairs={{0,4},{1,5},{2,6},{3,7},{4,0},{5,1},{6,2},{7,3},{8,12},{9,13},{10,... | collective-permute-start | bytes 921608 | tf_op jit(solution)/shard_map/ppermute | solution.py:800
  (11 other events, 13.1 us)
Sparse Core Ops, SparseCore 0:
  9.9 63.1 all-gather.2
  75.0 60.5 all-gather.4
  168.8 78.2 reduce-scatter.1

commit v3 on v2

--- a/solution.py
+++ b/solution.py
@@ -1002,13 +1002,13 @@
     size = part // 2
     owned_qkv = jnp.concatenate(
         [
-            swapped[g][c][:, which * size : (which + 1) * size]
+            swapped[g][c][:, which * size : (which + 1) * size].astype(F32)
             for which in (2, 0, 1)
             for c in range(2)
             for g in range(2)
         ],
         1,
-    ).astype(F32)
+    )
 
     return (
         output[None],

time: 446 us -> 446 us (level)
  no operation moved by 1% of the time
where the time goes in v3:
time: 446 us; the launch traced here: 439 us
  Pallas kernels  174 us (39%)
  waiting for transfers between devices  128 us (29%)
  starting transfers between devices  69.1 us (15%)
  other arithmetic  37.2 us (8%)
  local copies, waits for them, and re-layouts  15.2 us (3%)
  between operations  14.8 us (3%)
    ppermute x35, waiting for transfers between devices, send(): return lax.ppermute(value, AXES, pairs)  111 us
    ppermute x35, starting transfers between devices, send(): return lax.ppermute(value, AXES, pairs)  69 us
    pallas_call x2, Pallas kernels, attention_backward(): pl.pallas_call(functools.partial(backward_kernel, hd, tile, base, count,...  49.4 us
    pallas_call x2, Pallas kernels, input_gradient(): pl.pallas_call(functools.partial(dx_kernel, part, bool(dqs), n), grid_spe...  27.7 us
    pallas_call x1, Pallas kernels, attention_forward(): pl.pallas_call(functools.partial(forward_kernel, hd, tile), grid=(heads /...  24.2 us
    pallas_call x2, Pallas kernels, weight_gradient(): pl.pallas_call(functools.partial(weight_kernel, size, nq), grid_spec=pltp...  22.2 us
    pallas_call x1, Pallas kernels, mlp(): pl.pallas_call(functools.partial(mlp_kernel, part), grid_spec=pltpu.Prefe...  20.7 us
    pallas_call x1, Pallas kernels, project(): pl.pallas_call(functools.partial(project_kernel, part, query_slots, n), g...  18.8 us
  transfers between devices with their start and end apart: 38, of which 14 were waited for; matrix products, arithmetic and copies ran while one was open for 10% of the time, Pallas kernels for 35%

profile of v3, /device:TPU:0, one launch (start us, length us, event | category | flops | bytes accessed | tf_op | source)
XLA Modules:
  0.0 438.7 jit_solution(6406079321952975409)
XLA Ops:
  8.4 1.1 pad_maximum_fusion
  9.6 3.1 collective-permute-start.1
  12.7 27.7 %collective-permute-done.1 = bf16[512,1280]{1,0:T(8,128)(2,1)S(1)} collective-permute-done((bf16[512,1280]{1,0:T(8,128)(2,1)S(1)}, bf16[512,1280]{1,0:T(8,128)(2,1)S(1)}, u32[]{:S(2)}, u32[]{:S(2)}) %collective-permute-start.1) | collective-permute-done | bytes 1310752 | tf_op jit(solution)/shard_map/ppermute | solution.py:800
  40.4 1.9 broadcast_select_fusion.2.refs_0_.x_ref.refs_5_
  42.4 0.9 collective-permute-start.3
  43.3 1.9 broadcast_select_fusion.1.refs_2_.refs_5_
  45.2 19.5 %collective-permute-start.4 = (bf16[512,1280]{1,0:T(8,128)(2,1)S(1)}, bf16[512,1280]{1,0:T(8,128)(2,1)}, u32[]{:S(2)}, u32[]{:S(2)}) collective-permute-start(bf16[512,1280]{1,0:T(8,128)(2,1)S(1)} %broadcast_select_fusion.1.refs_2_.refs_5_), channel_id=1, source_target_pairs={{0,4},{1,5},{2,6},{3,7},{4,0},{5,1},{6,2},{7,3},{8,12},{9,13},{10,... | collective-permute-start | bytes 3932168 | tf_op jit(solution)/shard_map/ppermute | solution.py:800
  66.2 1.3 fusion.3.place_ref.refs_1_
  68.1 1.4 copy.31.col_ref.refs_3_
  69.5 1.7 collective-permute-start.5
  71.2 2.0 all-gather.3.cloned.1.call-done.refs_4_.refs_5_.refs_6_.refs_2_.refs_3_.refs_8_
  73.2 18.8 %project.1 = (bf16[640,1024]{1,0:T(8,128)(2,1)}, bf16[640,2048]{1,0:T(8,128)(2,1)}, bf16[640,2048]{1,0:T(8,128)(2,1)}, bf16[1280,2048]{1,0:T(8,128)(2,1)}) custom-call(s32[1]{0:T(128)} %bitcast.core_ref, f32[1,1280]{1,0:T(1,128)} %reshape.111.gain_ref.refs_4_, f32[640,1]{1,0:T(8,128)} %broadcast_multiply_fusion.scale_ref, bf16[512,1280]{1,0:T(8,128)(2,1)} %copy-done, ...), custom_call_target="tpu_custom_call" | custom-call | flops 8388608000 | bytes 65536 | tf_op jit(solution)/shard_map/project/pallas_call | solution.py:75
  92.0 24.2 %attention_forward.1 = (bf16[640,512]{1,0:T(8,128)(2,1)}, bf16[640,512]{1,0:T(8,128)(2,1)}, f32[8,1,1024]{2,1,0:T(1,128)}) custom-call(s32[2048]{0:T(1024)} %copy-done.24, s32[24]{0:T(128)} %fusion.3.place_ref.refs_1_, s32[1,2048]{1,0:T(1,128)} %bitcast.37, s32[2048,1]{1,0:T(8,128)} %copy.31.col_ref.refs_3_, ...), custom_call_target="tpu_custom_call" | custom-call | flops 10307921920 | bytes 65536 | tf_op jit(solution)/shard_map/attention_forward/pallas_call | solution.py:495
  116.2 2.2 collective-permute-start.6
  120.1 1.2 broadcast_select_fusion.cot_ref
  121.3 14.3 %all-gather.5.cloned.1.call-done.w_ref = bf16[1280,3840]{1,0:T(8,128)(2,1)} async-done(((bf16[160,3840]{1,0:T(8,128)(2,1)}), bf16[1280,3840]{1,0:T(8,128)(2,1)}) %all-gather.5.cloned.1.call-update) | async-done | bytes 9830416 | tf_op jit(solution)/shard_map/all_gather | solution.py:878
  135.6 0.8 copy-done.35
  136.4 20.7 %mlp.1 = (bf16[512,1280]{1,0:T(8,128)(2,1)}, bf16[640,512]{1,0:T(8,128)(2,1)}, bf16[640,512]{1,0:T(8,128)(2,1)}, f32[512,1280]{1,0:T(8,128)}, bf16[1280,512]{1,0...) custom-call(s32[1]{0:T(128)} %bitcast.core_ref, ...), custom_call_target="tpu_custom_call" | custom-call | flops 10066329600 | bytes 65536 | tf_op jit(solution)/shard_map/mlp/pallas_call | solution.py:185
  157.4 11.2 %mlp_weights.1 = bf16[1280,3840]{1,0:T(8,128)(2,1)} custom-call(s32[1]{0:T(128)} %bitcast.core_ref, bf16[640,512]{1,0:T(8,128)(2,1)} %get-tuple-element.108.near_ref.refs_9_, bf16[640,512]{1,0:T(8,128)(2,1)} %copy-done.35, bf16[1280,512]{1,0:T(8,128)(2,1)} %get-tuple-element.112.ht_ref, bf16[1280,512]{1,0:T(8,128)(2,1)} %get-tuple-element.113.nt_ref, ...), custom_call_target="tpu_custom_call" | custom-call | flops 5033164800 | bytes 20971520 | tf_op jit(solution)/shard_map/mlp_weights/pallas_call | solution.py:258
  171.0 22.7 %attention_backward.2 = (f32[640,1024]{1,0:T(8,128)}, bf16[640,1024]{1,0:T(8,128)(2,1)}, bf16[640,1024]{1,0:T(8,128)(2,1)}) custom-call(s32[2048]{0:T(1024)} %copy-done.24, s32[24]{0:T(128)} %fusion.3.place_ref.refs_1_, s32[1,2048]{1,0:T(1,128)} %bitcast.38, s32[2048,1]{1,0:T(8,128)} %copy.31.col_ref.refs_3_, ...), custom_call_target="tpu_custom_call" | custom-call | flops 12884901888 | bytes 16777216 | tf_op jit(solution)/shard_map/attention_backward/pallas_call | solution.py:537
  193.7 12.9 %input_gradient.2 = (bf16[512,1280]{1,0:T(8,128)(2,1)}, bf16[512,1280]{1,0:T(8,128)(2,1)}, f32[1,1280]{1,0:T(1,128)}) custom-call(s32[1]{0:T(128)} %bitcast.core_ref, bf16[640,1024]{1,0:T(8,128)(2,1)} %get-tuple-element.122.refs_0_.dkb_ref, bf16[640,1024]{1,0:T(8,128)(2,1)} %get-tuple-element.123.refs_1_.dvb_ref, ...), custom_call_target="tpu_custom_call" | custom-call | flops 3355443200 | bytes 65536 | tf_op jit(solution)/shard_map/input_gradient/pallas_call | solution.py:681
  206.6 5.6 %collective-permute-start.9 = (bf16[512,1280]{1,0:T(8,128)(2,1)}, bf16[512,1280]{1,0:T(8,128)(2,1)S(1)}, u32[]{:S(2)}, u32[]{:S(2)}) collective-permute-start(bf16[512,1280]{1,0:T(8,128)(2,1)} %get-tuple-element.128), channel_id=1, source_target_pairs={{0,4},{1,5},{2,6},{3,7},{4,0},{5,1},{6,2},{7,3},{8,12},{9,13},{10,... | collective-permute-start | bytes 3932168 | tf_op jit(solution)/shard_map/ppermute | solution.py:800
  212.2 2.9 collective-permute-done.9
  215.1 1.7 add_convert_fusion
  216.9 26.7 %attention_backward.3 = (bf16[640,1024]{1,0:T(8,128)(2,1)}, bf16[640,1024]{1,0:T(8,128)(2,1)}, bf16[640,1024]{1,0:T(8,128)(2,1)}, f32[640,1]{1,0:T(8,128)}) custom-call(s32[2048]{0:T(1024)} %copy-done.24, s32[24]{0:T(128)} %fusion.3.place_ref.refs_1_, s32[1,2048]{1,0:T(1,128)} %bitcast.39, s32[2048,1]{1,0:T(8,128)} %copy.31.col_ref.refs_3_, ...), custom_call_target="tpu_custom_call" | custom-call | flops 12884901888 | bytes 16777216 | tf_op jit(solution)/shard_map/attention_backward/pallas_call | solution.py:537
  243.6 4.4 %collective-permute-done.10 = bf16[512,1280]{1,0:T(8,128)(2,1)} collective-permute-done((bf16[512,1280]{1,0:T(8,128)(2,1)S(1)}, bf16[512,1280]{1,0:T(8,128)(2,1)}, u32[]{:S(2)}, u32[]{:S(2)}) %collective-permute-start.10) | collective-permute-done | bytes 1310752 | tf_op jit(solution)/shard_map/ppermute | solution.py:800
  248.0 3.6 collective-permute-start.11
  252.3 11.2 %weight_gradient.2 = (bf16[320,960]{1,0:T(8,128)(2,1)}, bf16[320,960]{1,0:T(8,128)(2,1)}, bf16[320,960]{1,0:T(8,128)(2,1)}, bf16[320,960]{1,0:T(8,128)(2,1)}) custom-call(s32[4]{0:T(128)} %pad_add_fusion.at_ref, bf16[1280,2048]{1,0:T(8,128)(2,1)} %get-tuple-element.139.xt_ref, bf16[640,1024]{1,0:T(8,128)(2,1)} %get-tuple-element.164.dqt_ref.refs_7_, ...), custom_call_target="tpu_custom_call" | custom-call | flops 4194304000 | bytes 12582912 | tf_op jit(solution)/shard_map/weight_gradient/pallas_call | solution.py:590
  263.4 1.4 collective-permute-start.12
  265.5 1.4 collective-permute-start.14
  267.3 14.9 %input_gradient.3 = (bf16[512,1280]{1,0:T(8,128)(2,1)}, bf16[512,1280]{1,0:T(8,128)(2,1)}, f32[1,1280]{1,0:T(1,128)}) custom-call(s32[1]{0:T(128)} %bitcast.core_ref, bf16[640,1024]{1,0:T(8,128)(2,1)} %get-tuple-element.136.dka_ref.refs_0_, bf16[640,1024]{1,0:T(8,128)(2,1)} %get-tuple-element.137.dva_ref.refs_1_, ...), custom_call_target="tpu_custom_call" | custom-call | flops 5033164800 | bytes 65536 | tf_op jit(solution)/shard_map/input_gradient/pallas_call | solution.py:681
  282.2 12.8 %collective-permute-done.13 = bf16[320,960]{1,0:T(8,128)(2,1)S(1)} collective-permute-done((bf16[320,960]{1,0:T(8,128)(2,1)}, bf16[320,960]{1,0:T(8,128)(2,1)S(1)}, u32[]{:S(2)}, u32[]{:S(2)}) %collective-permute-start.13) | collective-permute-done | bytes 614432 | tf_op jit(solution)/shard_map/ppermute | solution.py:800
  296.4 3.0 add_convert_fusion.2
  300.2 1.3 fusion
  301.5 1.3 collective-permute-start.16
  302.8 1.7 collective-permute-start.21
  304.6 1.4 collective-permute-start.19
  306.0 11.1 %weight_gradient.3 = (bf16[320,960]{1,0:T(8,128)(2,1)}, bf16[320,960]{1,0:T(8,128)(2,1)}, bf16[320,960]{1,0:T(8,128)(2,1)}, bf16[320,960]{1,0:T(8,128)(2,1)}) custom-call(s32[4]{0:T(128)} %pad_add_fusion.at_ref, bf16[1280,2048]{1,0:T(8,128)(2,1)} %get-tuple-element.139.xt_ref, bf16[640,1024]{1,0:T(8,128)(2,1)} %get-tuple-element.164.dqt_ref.refs_7_, ...), custom_call_target="tpu_custom_call" | custom-call | flops 4194304000 | bytes 12582912 | tf_op jit(solution)/shard_map/weight_gradient/pallas_call | solution.py:590
  317.4 0.8 copy-done.19
  318.6 2.5 add_convert_fusion.6
  321.8 1.4 collective-permute-start.22
  323.9 1.4 collective-permute-start.24
  325.4 3.3 fusion.2
  328.7 1.9 collective-permute-start.28
  330.6 9.2 %collective-permute-done.22 = bf16[320,960]{1,0:T(8,128)(2,1)S(1)} collective-permute-done((bf16[320,960]{1,0:T(8,128)(2,1)}, bf16[320,960]{1,0:T(8,128)(2,1)S(1)}, u32[]{:S(2)}, u32[]{:S(2)}) %collective-permute-start.22) | collective-permute-done | bytes 614432 | tf_op jit(solution)/shard_map/ppermute | solution.py:800
  339.7 13.4 %collective-permute-done.23 = bf16[320,960]{1,0:T(8,128)(2,1)S(1)} collective-permute-done((bf16[320,960]{1,0:T(8,128)(2,1)}, bf16[320,960]{1,0:T(8,128)(2,1)S(1)}, u32[]{:S(2)}, u32[]{:S(2)}) %collective-permute-start.23) | collective-permute-done | bytes 614432 | tf_op jit(solution)/shard_map/ppermute | solution.py:800
  353.9 9.3 %collective-permute-start.25 = (bf16[320,960]{1,0:T(8,128)(2,1)S(1)}, bf16[320,960]{1,0:T(8,128)(2,1)S(1)}, u32[]{:S(2)}, u32[]{:S(2)}) collective-permute-start(bf16[320,960]{1,0:T(8,128)(2,1)S(1)} %fusion.1), channel_id=1, source_target_pairs={{0,1},{3,2},{4,5},{7,6},{8,9},{11,10},{12,13},{15,14},{16,17},{19,... | collective-permute-start | bytes 1843208 | tf_op jit(solution)/shard_map/ppermute | solution.py:800
  363.2 1.3 collective-permute-start.26
  364.5 3.0 add_convert_fusion.1
  367.5 1.3 collective-permute-start.31
  368.7 14.0 %collective-permute-done.26 = bf16[320,960]{1,0:T(8,128)(2,1)S(1)} collective-permute-done((bf16[320,960]{1,0:T(8,128)(2,1)S(1)}, bf16[320,960]{1,0:T(8,128)(2,1)S(1)}, u32[]{:S(2)}, u32[]{:S(2)}) %collective-permute-start.26) | collective-permute-done | bytes 614432 | tf_op jit(solution)/shard_map/ppermute | solution.py:800
  382.8 1.5 add_convert_fusion.4
  384.3 1.5 collective-permute-start.27
  385.8 2.5 select_bitcast_fusion.1
  388.4 1.5 add_convert_fusion.3
  390.0 1.4 collective-permute-start.30
  391.4 17.8 %collective-permute-done.31 = bf16[160,3840]{1,0:T(8,128)(2,1)} collective-permute-done((bf16[160,3840]{1,0:T(8,128)(2,1)}, bf16[160,3840]{1,0:T(8,128)(2,1)}, u32[]{:S(2)}, u32[]{:S(2)}) %collective-permute-start.31) | collective-permute-done | bytes 1228832 | tf_op jit(solution)/shard_map/ppermute | solution.py:800
  409.2 1.4 broadcast_select_fusion.3
  410.6 4.1 select_bitcast_fusion
  415.0 5.9 %collective-permute-done.30 = bf16[320,960]{1,0:T(8,128)(2,1)S(1)} collective-permute-done((bf16[320,960]{1,0:T(8,128)(2,1)S(1)}, bf16[320,960]{1,0:T(8,128)(2,1)S(1)}, u32[]{:S(2)}, u32[]{:S(2)}) %collective-permute-start.30) | collective-permute-done | bytes 614432 | tf_op jit(solution)/shard_map/ppermute | solution.py:800
  421.8 1.5 fusion.7
  423.3 2.7 collective-permute-done.34
  427.4 2.7 concatenate.14
  430.1 1.6 concatenate.15
  (160 shorter events, 17.4 us)
Async XLA Ops:
  7.2 65.9 %all-gather.3.cloned.1.call-start = ((), (), s32[]{:S(2)}) async-start(), calls=%async_computation.1 | async-start | bytes 11059200 | tf_op jit(solution)/shard_map/all_gather | solution.py:863
  8.0 127.6 %all-gather.5.cloned.1.call-start = ((), (), s32[]{:S(2)}) async-start(), calls=%async_computation.2 | async-start | bytes 11059200 | tf_op jit(solution)/shard_map/all_gather | solution.py:878
  9.6 238.4 %reduce-scatter.2.cloned.1.call-start = ((), (), s32[]{:S(2)}) async-start(), calls=%async_computation.3 | async-start | bytes 11059200 | tf_op jit(solution)/shard_map/reduce_scatter | solution.py:901
  9.6 30.7 %collective-permute-start.1 = (bf16[512,1280]{1,0:T(8,128)(2,1)S(1)}, bf16[512,1280]{1,0:T(8,128)(2,1)S(1)}, u32[]{:S(2)}, u32[]{:S(2)}) collective-permute-start(bf16[512,1280]{1,0:T(8,128)(2,1)S(1)} %bitcast.33), channel_id=1, source_target_pairs={{0,1},{1,0},{2,5},{3,4},{4,3},{5,2},{6,7},{7,6},{8,9},{9,8},{10,13... | collective-permute-start | bytes 3932168 | tf_op jit(solution)/shard_map/ppermute | solution.py:800
  42.3 22.4 %copy-start = (bf16[512,1280]{1,0:T(8,128)(2,1)}, bf16[512,1280]{1,0:T(8,128)(2,1)S(1)}, u32[]{:S(2)}) copy-start(bf16[512,1280]{1,0:T(8,128)(2,1)S(1)} %broadcast_select_fusion.2.refs_0_.x_ref.refs_5_) | copy-start | bytes 3932164
  42.3 22.4 %copy-start.25 = (s32[1,2048]{1,0:T(1,128)S(1)}, s32[1,2048]{1,0:T(1,128)}, u32[]{:S(2)}) copy-start(s32[1,2048]{1,0:T(1,128)} %param.14) | copy-start | bytes 24580
  42.3 22.9 %copy-start.36 = (bf16[80]{0:T(256)(128)(2,1)S(1)}, bf16[80]{0:T(256)(128)(2,1)}, u32[]{:S(2)}) copy-start(bf16[80]{0:T(256)(128)(2,1)} %param.23) | copy-start | bytes 484
  42.4 25.1 %copy-start.30 = (bf16[1280]{0:T(1024)(128)(2,1)S(1)}, bf16[1280]{0:T(1024)(128)(2,1)}, u32[]{:S(2)}) copy-start(bf16[1280]{0:T(1024)(128)(2,1)} %param.19) | copy-start | bytes 7684
  42.4 0.9 collective-permute-start.3
  45.2 28.0 %copy-start.1 = (bf16[512,1280]{1,0:T(8,128)(2,1)}, bf16[512,1280]{1,0:T(8,128)(2,1)S(1)}, u32[]{:S(2)}) copy-start(bf16[512,1280]{1,0:T(8,128)(2,1)S(1)} %broadcast_select_fusion.1.refs_2_.refs_5_) | copy-start | bytes 3932164
  45.2 24.3 %collective-permute-start.4 = (bf16[512,1280]{1,0:T(8,128)(2,1)S(1)}, bf16[512,1280]{1,0:T(8,128)(2,1)}, u32[]{:S(2)}, u32[]{:S(2)}) collective-permute-start(bf16[512,1280]{1,0:T(8,128)(2,1)S(1)} %broadcast_select_fusion.1.refs_2_.refs_5_), channel_id=1, source_target_pairs={{0,4},{1,5},{2,6},{3,7},{4,0},{5,1},{6,2},{7,3},{8,12},{9,13},{10,... | collective-permute-start | bytes 3932168 | tf_op jit(solution)/shard_map/ppermute | solution.py:800
  64.7 6.5 %collective-permute-start.2 = (bf16[512,1280]{1,0:T(8,128)(2,1)S(1)}, bf16[512,1280]{1,0:T(8,128)(2,1)}, u32[]{:S(2)}, u32[]{:S(2)}) collective-permute-start(bf16[512,1280]{1,0:T(8,128)(2,1)S(1)} %broadcast_select_fusion.2.refs_0_.x_ref.refs_5_), channel_id=1, source_target_pairs={{0,4},{1,5},{2,6},{3,7},{4,0},{5,1},{6,2},{7,3},{8,12},{9,13},{10,... | collective-permute-start | bytes 3932168 | tf_op jit(solution)/shard_map/ppermute | solution.py:800
  64.8 3.3 collective-permute-start
  65.4 26.5 %copy-start.18 = (f32[640,1]{1,0:T(8,128)}, f32[640,1]{1,0:T(8,128)S(1)}, u32[]{:S(2)}) copy-start(f32[640,1]{1,0:T(8,128)S(1)} %broadcast_in_dim_tile.4.refs_13_) | copy-start | bytes 7684
  68.1 23.8 %copy-start.24 = (s32[2048]{0:T(1024)}, s32[2048]{0:T(1024)S(1)}, u32[]{:S(2)}) copy-start(s32[2048]{0:T(1024)S(1)} %broadcast_select_fusion.10.ids_ref.refs_0_) | copy-start | bytes 24580
  69.5 46.7 %collective-permute-start.5 = (bf16[512,1280]{1,0:T(8,128)(2,1)}, bf16[512,1280]{1,0:T(8,128)(2,1)}, u32[]{:S(2)}, u32[]{:S(2)}) collective-permute-start(bf16[512,1280]{1,0:T(8,128)(2,1)} %bitcast.34), channel_id=1, source_target_pairs={{2,5},{3,4},{4,3},{5,2},{10,13},{11,12},{12,11},{13,10},{18,21},{1... | collective-permute-start | bytes 3932168 | tf_op jit(solution)/shard_map/ppermute | solution.py:800
  91.9 26.4 %copy-start.31 = (bf16[1280]{0:T(1024)(128)(2,1)S(1)}, bf16[1280]{0:T(1024)(128)(2,1)}, u32[]{:S(2)}) copy-start(bf16[1280]{0:T(1024)(128)(2,1)} %param.20) | copy-start | bytes 7684
  91.9 27.0 %copy-start.32 = (bf16[1280]{0:T(1024)(128)(2,1)S(1)}, bf16[1280]{0:T(1024)(128)(2,1)}, u32[]{:S(2)}) copy-start(bf16[1280]{0:T(1024)(128)(2,1)} %param.21) | copy-start | bytes 7684
  91.9 27.6 %copy-start.33 = (bf16[1280]{0:T(1024)(128)(2,1)S(1)}, bf16[1280]{0:T(1024)(128)(2,1)}, u32[]{:S(2)}) copy-start(bf16[1280]{0:T(1024)(128)(2,1)} %param.22) | copy-start | bytes 7684
  91.9 28.2 %copy-start.15 = (bf16[1,512,1280]{2,1,0:T(8,128)(2,1)S(1)}, bf16[1,512,1280]{2,1,0:T(8,128)(2,1)}, u32[]{:S(2)}) copy-start(bf16[1,512,1280]{2,1,0:T(8,128)(2,1)} %param.24) | copy-start | bytes 3932164
  116.2 19.4 %collective-permute-start.6 = (bf16[640,512]{1,0:T(8,128)(2,1)}, bf16[640,512]{1,0:T(8,128)(2,1)S(1)}, u32[]{:S(2)}, u32[]{:S(2)}) collective-permute-start(bf16[640,512]{1,0:T(8,128)(2,1)} %get-tuple-element.109.refs_10_), channel_id=1, source_target_pairs={{0,4},{1,5},{2,6},{3,7},{4,0},{5,1},{6,2},{7,3},{8,12},{9,13},{10,... | collective-permute-start | bytes 1966088 | tf_op jit(solution)/shard_map/ppermute | solution.py:800
  157.1 11.6 %collective-permute-start.7 = (bf16[640,512]{1,0:T(8,128)(2,1)}, bf16[640,512]{1,0:T(8,128)(2,1)S(1)}, u32[]{:S(2)}, u32[]{:S(2)}) collective-permute-start(bf16[640,512]{1,0:T(8,128)(2,1)} %get-tuple-element.116), channel_id=1, source_target_pairs={{0,4},{1,5},{2,6},{3,7},{4,0},{5,1},{6,2},{7,3},{8,12},{9,13},{10,... | collective-permute-start | bytes 1966088 | tf_op jit(solution)/shard_map/ppermute | solution.py:800
  170.2 36.4 %collective-permute-start.8 = (bf16[512,1280]{1,0:T(8,128)(2,1)S(1)}, bf16[512,1280]{1,0:T(8,128)(2,1)S(1)}, u32[]{:S(2)}, u32[]{:S(2)}) collective-permute-start(bf16[512,1280]{1,0:T(8,128)(2,1)S(1)} %copy-done.16), channel_id=1, source_target_pairs={{2,5},{3,4},{4,3},{5,2},{10,13},{11,12},{12,11},{13,10},{18,21},{1... | collective-permute-start | bytes 3932168 | tf_op jit(solution)/shard_map/ppermute | solution.py:800
  206.6 10.2 %copy-start.17 = (bf16[512,1280]{1,0:T(8,128)(2,1)}, bf16[512,1280]{1,0:T(8,128)(2,1)S(1)}, u32[]{:S(2)}) copy-start(bf16[512,1280]{1,0:T(8,128)(2,1)S(1)} %collective-permute-done.8) | copy-start | bytes 3932164
  206.6 8.5 %collective-permute-start.9 = (bf16[512,1280]{1,0:T(8,128)(2,1)}, bf16[512,1280]{1,0:T(8,128)(2,1)S(1)}, u32[]{:S(2)}, u32[]{:S(2)}) collective-permute-start(bf16[512,1280]{1,0:T(8,128)(2,1)} %get-tuple-element.128), channel_id=1, source_target_pairs={{0,4},{1,5},{2,6},{3,7},{4,0},{5,1},{6,2},{7,3},{8,12},{9,13},{10,... | collective-permute-start | bytes 3932168 | tf_op jit(solution)/shard_map/ppermute | solution.py:800
  216.8 31.2 %collective-permute-start.10 = (bf16[512,1280]{1,0:T(8,128)(2,1)S(1)}, bf16[512,1280]{1,0:T(8,128)(2,1)}, u32[]{:S(2)}, u32[]{:S(2)}) collective-permute-start(bf16[512,1280]{1,0:T(8,128)(2,1)S(1)} %add_convert_fusion), channel_id=1, source_target_pairs={{0,1},{1,0},{2,3},{3,2},{4,5},{5,4},{6,7},{7,6},{8,9},{9,8},{10,11... | collective-permute-start | bytes 3932168 | tf_op jit(solution)/shard_map/ppermute | solution.py:800
  248.0 47.0 %collective-permute-start.11 = (bf16[160,3840]{1,0:T(8,128)(2,1)}, bf16[160,3840]{1,0:T(8,128)(2,1)}, u32[]{:S(2)}, u32[]{:S(2)}) collective-permute-start(bf16[160,3840]{1,0:T(8,128)(2,1)} %reduce-scatter.2.cloned.1.call-done), channel_id=1, source_target_pairs={{0,1},{3,2},{4,5},{7,6},{8,9},{11,10},{12,13},{15,14},{16,17},{19,... | collective-permute-start | bytes 3686408 | tf_op jit(solution)/shard_map/ppermute | solution.py:800
  252.2 14.7 %copy-start.28 = (f32[1,1280]{1,0:T(1,128)S(1)}, f32[1,1280]{1,0:T(1,128)}, u32[]{:S(2)}) copy-start(f32[1,1280]{1,0:T(1,128)} %get-tuple-element.160) | copy-start | bytes 15364
  252.2 14.7 %copy-start.27 = (f32[1,1280]{1,0:T(1,128)S(1)}, f32[1,1280]{1,0:T(1,128)}, u32[]{:S(2)}) copy-start(f32[1,1280]{1,0:T(1,128)} %get-tuple-element.161) | copy-start | bytes 15364
  252.2 14.7 %copy-start.26 = (f32[1,1280]{1,0:T(1,128)S(1)}, f32[1,1280]{1,0:T(1,128)}, u32[]{:S(2)}) copy-start(f32[1,1280]{1,0:T(1,128)} %get-tuple-element.162) | copy-start | bytes 15364
  252.3 14.8 %copy-start.23 = (f32[640,1]{1,0:T(8,128)S(1)}, f32[640,1]{1,0:T(8,128)}, u32[]{:S(2)}) copy-start(f32[640,1]{1,0:T(8,128)} %get-tuple-element.163) | copy-start | bytes 7684
  263.4 18.7 %collective-permute-start.12 = (bf16[320,960]{1,0:T(8,128)(2,1)}, bf16[320,960]{1,0:T(8,128)(2,1)S(1)}, u32[]{:S(2)}, u32[]{:S(2)}) collective-permute-start(bf16[320,960]{1,0:T(8,128)(2,1)} %get-tuple-element.149), channel_id=1, source_target_pairs={{0,8},{1,9},{2,10},{3,11},{4,12},{5,13},{6,14},{7,15},{8,0},{9,1},... | collective-permute-start | bytes 1843208 | tf_op jit(solution)/shard_map/ppermute | solution.py:800
  264.8 30.2 %collective-permute-start.13 = (bf16[320,960]{1,0:T(8,128)(2,1)}, bf16[320,960]{1,0:T(8,128)(2,1)S(1)}, u32[]{:S(2)}, u32[]{:S(2)}) collective-permute-start(bf16[320,960]{1,0:T(8,128)(2,1)} %get-tuple-element.150), channel_id=1, source_target_pairs={{0,16},{1,17},{2,18},{3,19},{4,20},{5,21},{6,22},{7,23},{8,24},{9,... | collective-permute-start | bytes 1843208 | tf_op jit(solution)/shard_map/ppermute | solution.py:800
  265.5 29.5 %collective-permute-start.14 = (bf16[320,960]{1,0:T(8,128)(2,1)}, bf16[320,960]{1,0:T(8,128)(2,1)S(1)}, u32[]{:S(2)}, u32[]{:S(2)}) collective-permute-start(bf16[320,960]{1,0:T(8,128)(2,1)} %get-tuple-element.151), channel_id=1, source_target_pairs={{0,24},{1,25},{2,26},{3,27},{4,28},{5,29},{6,30},{7,31},{8,16},{9,... | collective-permute-start | bytes 1843208 | tf_op jit(solution)/shard_map/ppermute | solution.py:800
  267.3 27.7 %copy-start.29 = (f32[1,1280]{1,0:T(1,128)S(1)}, f32[1,1280]{1,0:T(1,128)}, u32[]{:S(2)}) copy-start(f32[1,1280]{1,0:T(1,128)} %get-tuple-element.158) | copy-start | bytes 15364
  282.2 18.0 %copy-start.9 = (bf16[320,960]{1,0:T(8,128)(2,1)}, bf16[320,960]{1,0:T(8,128)(2,1)S(1)}, u32[]{:S(2)}) copy-start(bf16[320,960]{1,0:T(8,128)(2,1)S(1)} %collective-permute-done.12) | copy-start | bytes 1843204
  295.0 5.2 %copy-start.10 = (bf16[320,960]{1,0:T(8,128)(2,1)}, bf16[320,960]{1,0:T(8,128)(2,1)S(1)}, u32[]{:S(2)}) copy-start(bf16[320,960]{1,0:T(8,128)(2,1)S(1)} %collective-permute-done.13) | copy-start | bytes 1843204
  295.8 4.3 copy-start.8
  295.8 3.5 collective-permute-start.17
  295.9 4.2 copy-start.12
  295.9 21.4 %collective-permute-start.15 = (bf16[512,1280]{1,0:T(8,128)(2,1)}, bf16[512,1280]{1,0:T(8,128)(2,1)S(1)}, u32[]{:S(2)}, u32[]{:S(2)}) collective-permute-start(bf16[512,1280]{1,0:T(8,128)(2,1)} %get-tuple-element.153), channel_id=1, source_target_pairs={{0,4},{1,5},{2,6},{3,7},{4,0},{5,1},{6,2},{7,3},{8,12},{9,13},{10,... | collective-permute-start | bytes 3932168 | tf_op jit(solution)/shard_map/ppermute | solution.py:800
  299.4 5.1 %collective-permute-start.18 = (f32[48,128]{1,0:T(8,128)S(1)}, f32[48,128]{1,0:T(8,128)S(1)}, u32[]{:S(2)}, u32[]{:S(2)}) collective-permute-start(f32[48,128]{1,0:T(8,128)S(1)} %fusion.6), channel_id=1, source_target_pairs={{0,8},{1,9},{2,10},{3,11},{4,12},{5,13},{6,14},{7,15},{8,0},{9,1},... | collective-permute-start | bytes 73736 | tf_op jit(solution)/shard_map/ppermute | solution.py:800
  301.5 15.9 %collective-permute-start.16 = (bf16[320,960]{1,0:T(8,128)(2,1)}, bf16[320,960]{1,0:T(8,128)(2,1)S(1)}, u32[]{:S(2)}, u32[]{:S(2)}) collective-permute-start(bf16[320,960]{1,0:T(8,128)(2,1)} %fusion), channel_id=1, source_target_pairs={{0,1},{3,2},{4,5},{7,6},{8,9},{11,10},{12,13},{15,14},{16,17},{19,... | collective-permute-start | bytes 1843208 | tf_op jit(solution)/shard_map/ppermute | solution.py:800
  302.8 25.9 %collective-permute-start.21 = (bf16[160,3840]{1,0:T(8,128)(2,1)}, bf16[160,3840]{1,0:T(8,128)(2,1)}, u32[]{:S(2)}, u32[]{:S(2)}) collective-permute-start(bf16[160,3840]{1,0:T(8,128)(2,1)} %add_convert_fusion.2), channel_id=1, source_target_pairs={{1,2},{2,1},{5,6},{6,5},{9,10},{10,9},{13,14},{14,13},{17,18},{18,... | collective-permute-start | bytes 3686408 | tf_op jit(solution)/shard_map/ppermute | solution.py:800
  304.6 12.5 %collective-permute-start.19 = (f32[48,128]{1,0:T(8,128)S(1)}, f32[48,128]{1,0:T(8,128)S(1)}, u32[]{:S(2)}, u32[]{:S(2)}) collective-permute-start(f32[48,128]{1,0:T(8,128)S(1)} %fusion.12), channel_id=1, source_target_pairs={{0,16},{1,17},{2,18},{3,19},{4,20},{5,21},{6,22},{7,23},{8,24},{9,... | collective-permute-start | bytes 73736 | tf_op jit(solution)/shard_map/ppermute | solution.py:800
  318.6 6.8 %copy-start.2 = (f32[512,1280]{1,0:T(8,128)S(1)}, f32[512,1280]{1,0:T(8,128)}, u32[]{:S(2)}) copy-start(f32[512,1280]{1,0:T(8,128)} %get-tuple-element.170) | copy-start | bytes 7864324
  318.6 6.8 %copy-start.4 = (bf16[512,1280]{1,0:T(8,128)(2,1)S(1)}, bf16[512,1280]{1,0:T(8,128)(2,1)}, u32[]{:S(2)}) copy-start(bf16[512,1280]{1,0:T(8,128)(2,1)} %get-tuple-element.152) | copy-start | bytes 3932164
  321.1 9.5 %collective-permute-start.20 = (bf16[320,960]{1,0:T(8,128)(2,1)S(1)}, bf16[320,960]{1,0:T(8,128)(2,1)S(1)}, u32[]{:S(2)}, u32[]{:S(2)}) collective-permute-start(bf16[320,960]{1,0:T(8,128)(2,1)S(1)} %add_convert_fusion.6), channel_id=1, source_target_pairs={{1,2},{2,1},{5,6},{6,5},{9,10},{10,9},{13,14},{14,13},{17,18},{18,... | collective-permute-start | bytes 1843208 | tf_op jit(solution)/shard_map/ppermute | solution.py:800
  321.8 17.9 %collective-permute-start.22 = (bf16[320,960]{1,0:T(8,128)(2,1)}, bf16[320,960]{1,0:T(8,128)(2,1)S(1)}, u32[]{:S(2)}, u32[]{:S(2)}) collective-permute-start(bf16[320,960]{1,0:T(8,128)(2,1)} %get-tuple-element.175), channel_id=1, source_target_pairs={{0,8},{1,9},{2,10},{3,11},{4,12},{5,13},{6,14},{7,15},{8,0},{9,1},... | collective-permute-start | bytes 1843208 | tf_op jit(solution)/shard_map/ppermute | solution.py:800
  323.2 29.9 %collective-permute-start.23 = (bf16[320,960]{1,0:T(8,128)(2,1)}, bf16[320,960]{1,0:T(8,128)(2,1)S(1)}, u32[]{:S(2)}, u32[]{:S(2)}) collective-permute-start(bf16[320,960]{1,0:T(8,128)(2,1)} %get-tuple-element.176), channel_id=1, source_target_pairs={{0,16},{1,17},{2,18},{3,19},{4,20},{5,21},{6,22},{7,23},{8,24},{9,... | collective-permute-start | bytes 1843208 | tf_op jit(solution)/shard_map/ppermute | solution.py:800
  323.9 29.2 %collective-permute-start.24 = (bf16[320,960]{1,0:T(8,128)(2,1)}, bf16[320,960]{1,0:T(8,128)(2,1)S(1)}, u32[]{:S(2)}, u32[]{:S(2)}) collective-permute-start(bf16[320,960]{1,0:T(8,128)(2,1)} %get-tuple-element.177), channel_id=1, source_target_pairs={{0,24},{1,25},{2,26},{3,27},{4,28},{5,29},{6,30},{7,31},{8,16},{9,... | collective-permute-start | bytes 1843208 | tf_op jit(solution)/shard_map/ppermute | solution.py:800
  328.7 24.7 %copy-start.13 = (bf16[320,960]{1,0:T(8,128)(2,1)S(1)}, bf16[320,960]{1,0:T(8,128)(2,1)}, u32[]{:S(2)}) copy-start(bf16[320,960]{1,0:T(8,128)(2,1)} %get-tuple-element.172) | copy-start | bytes 1843204
  328.7 59.6 %collective-permute-start.28 = (bf16[512,1280]{1,0:T(8,128)(2,1)}, bf16[512,1280]{1,0:T(8,128)(2,1)}, u32[]{:S(2)}, u32[]{:S(2)}) collective-permute-start(bf16[512,1280]{1,0:T(8,128)(2,1)} %fusion.2), channel_id=1, source_target_pairs={{2,5},{3,4},{4,3},{5,2},{10,13},{11,12},{12,11},{13,10},{18,21},{1... | collective-permute-start | bytes 3932168 | tf_op jit(solution)/shard_map/ppermute | solution.py:800
  353.9 28.9 %collective-permute-start.25 = (bf16[320,960]{1,0:T(8,128)(2,1)S(1)}, bf16[320,960]{1,0:T(8,128)(2,1)S(1)}, u32[]{:S(2)}, u32[]{:S(2)}) collective-permute-start(bf16[320,960]{1,0:T(8,128)(2,1)S(1)} %fusion.1), channel_id=1, source_target_pairs={{0,1},{3,2},{4,5},{7,6},{8,9},{11,10},{12,13},{15,14},{16,17},{19,... | collective-permute-start | bytes 1843208 | tf_op jit(solution)/shard_map/ppermute | solution.py:800
  363.2 19.6 %collective-permute-start.26 = (bf16[320,960]{1,0:T(8,128)(2,1)S(1)}, bf16[320,960]{1,0:T(8,128)(2,1)S(1)}, u32[]{:S(2)}, u32[]{:S(2)}) collective-permute-start(bf16[320,960]{1,0:T(8,128)(2,1)S(1)} %add_convert_fusion.5), channel_id=1, source_target_pairs={{1,0},{2,3},{5,4},{6,7},{9,8},{10,11},{13,12},{14,15},{17,16},{18,... | collective-permute-start | bytes 1843208 | tf_op jit(solution)/shard_map/ppermute | solution.py:800
  367.5 41.7 %collective-permute-start.31 = (bf16[160,3840]{1,0:T(8,128)(2,1)}, bf16[160,3840]{1,0:T(8,128)(2,1)}, u32[]{:S(2)}, u32[]{:S(2)}) collective-permute-start(bf16[160,3840]{1,0:T(8,128)(2,1)} %add_convert_fusion.1), channel_id=1, source_target_pairs={{1,0},{2,3},{5,4},{6,7},{9,8},{10,11},{13,12},{14,15},{17,16},{18,... | collective-permute-start | bytes 3686408 | tf_op jit(solution)/shard_map/ppermute | solution.py:800
  384.3 4.0 collective-permute-start.27
  388.4 26.4 %collective-permute-start.29 = (bf16[160,960]{1,0:T(8,128)(2,1)S(1)}, bf16[160,960]{1,0:T(8,128)(2,1)S(1)}, u32[]{:S(2)}, u32[]{:S(2)}) collective-permute-start(bf16[160,960]{1,0:T(8,128)(2,1)S(1)} %constant_dynamic-slice_fusion.1), channel_id=1, source_target_pairs={{0,4},{1,5},{2,6},{3,7},{4,0},{5,1},{6,2},{7,3},{8,12},{9,13},{10,... | collective-permute-start | bytes 921608 | tf_op jit(solution)/shard_map/ppermute | solution.py:800
  390.0 20.7 %copy-start.5 = (bf16[512,1280]{1,0:T(8,128)(2,1)S(1)}, bf16[512,1280]{1,0:T(8,128)(2,1)}, u32[]{:S(2)}) copy-start(bf16[512,1280]{1,0:T(8,128)(2,1)} %get-tuple-element.152) | copy-start | bytes 3932164
  390.0 20.7 %copy-start.7 = (bf16[512,1280]{1,0:T(8,128)(2,1)S(1)}, bf16[512,1280]{1,0:T(8,128)(2,1)}, u32[]{:S(2)}) copy-start(bf16[512,1280]{1,0:T(8,128)(2,1)} %copy-done.6) | copy-start | bytes 3932164
  390.0 31.0 %collective-permute-start.30 = (bf16[320,960]{1,0:T(8,128)(2,1)S(1)}, bf16[320,960]{1,0:T(8,128)(2,1)S(1)}, u32[]{:S(2)}, u32[]{:S(2)}) collective-permute-start(bf16[320,960]{1,0:T(8,128)(2,1)S(1)} %add_convert_fusion.3), channel_id=1, source_target_pairs={{1,0},{2,3},{5,4},{6,7},{9,8},{10,11},{13,12},{14,15},{17,16},{18,... | collective-permute-start | bytes 1843208 | tf_op jit(solution)/shard_map/ppermute | solution.py:800
  414.7 6.5 %collective-permute-start.32 = (f32[48,128]{1,0:T(8,128)S(1)}, f32[48,128]{1,0:T(8,128)S(1)}, u32[]{:S(2)}, u32[]{:S(2)}) collective-permute-start(f32[48,128]{1,0:T(8,128)S(1)} %add.109), channel_id=1, source_target_pairs={{0,1},{1,0},{2,3},{3,2},{4,5},{5,4},{6,7},{7,6},{8,9},{9,8},{10,11... | collective-permute-start | bytes 73736 | tf_op jit(solution)/shard_map/ppermute | solution.py:800
  421.2 4.7 %collective-permute-start.34 = (f32[48,128]{1,0:T(8,128)S(1)}, f32[48,128]{1,0:T(8,128)S(1)}, u32[]{:S(2)}, u32[]{:S(2)}) collective-permute-start(f32[48,128]{1,0:T(8,128)S(1)} %add.124), channel_id=1, source_target_pairs={{0,2},{1,3},{2,0},{3,1},{4,6},{5,7},{6,4},{7,5},{8,10},{9,11},{10,... | collective-permute-start | bytes 73736 | tf_op jit(solution)/shard_map/ppermute | solution.py:800
  421.7 5.4 %collective-permute-start.33 = (bf16[160,960]{1,0:T(8,128)(2,1)S(1)}, bf16[160,960]{1,0:T(8,128)(2,1)S(1)}, u32[]{:S(2)}, u32[]{:S(2)}) collective-permute-start(bf16[160,960]{1,0:T(8,128)(2,1)S(1)} %constant_dynamic-slice_fusion), channel_id=1, source_target_pairs={{0,4},{1,5},{2,6},{3,7},{4,0},{5,1},{6,2},{7,3},{8,12},{9,13},{10,... | collective-permute-start | bytes 921608 | tf_op jit(solution)/shard_map/ppermute | solution.py:800
  (11 other events, 13.1 us)
Sparse Core Ops, SparseCore 0:
  9.9 63.1 all-gather.2
  75.0 60.5 all-gather.4
  168.8 78.2 reduce-scatter.1

commit v4 on v3

--- a/solution.py
+++ b/solution.py
@@ -660,7 +660,7 @@
     part = dkvs[0].shape[0]
     n = len(slots)
     rows, width = slots[0].shape
-    tile = 256
+    tile = rows
     per_slot = rows // tile
     once = pl.Buffered(1)
     dkv = pl.BlockSpec((part, tile), lambda i, c: (0, i))

time: 446 us -> 446 us (level)
  no operation moved by 1% of the time
where the time goes in v4:
time: 446 us; the launch traced here: 439 us
  Pallas kernels  174 us (39%)
  waiting for transfers between devices  128 us (29%)
  starting transfers between devices  69.1 us (15%)
  other arithmetic  37.2 us (8%)
  local copies, waits for them, and re-layouts  15.2 us (3%)
  between operations  14.8 us (3%)
    ppermute x35, waiting for transfers between devices, send(): return lax.ppermute(value, AXES, pairs)  111 us
    ppermute x35, starting transfers between devices, send(): return lax.ppermute(value, AXES, pairs)  69 us
    pallas_call x2, Pallas kernels, attention_backward(): pl.pallas_call(functools.partial(backward_kernel, hd, tile, base, count,...  49.5 us
    pallas_call x2, Pallas kernels, input_gradient(): pl.pallas_call(functools.partial(dx_kernel, part, bool(dqs), n), grid_spe...  27.8 us
    pallas_call x1, Pallas kernels, attention_forward(): pl.pallas_call(functools.partial(forward_kernel, hd, tile), grid=(heads /...  24.2 us
    pallas_call x2, Pallas kernels, weight_gradient(): pl.pallas_call(functools.partial(weight_kernel, size, nq), grid_spec=pltp...  22.2 us
    pallas_call x1, Pallas kernels, mlp(): pl.pallas_call(functools.partial(mlp_kernel, part), grid_spec=pltpu.Prefe...  20.7 us
    pallas_call x1, Pallas kernels, project(): pl.pallas_call(functools.partial(project_kernel, part, query_slots, n), g...  18.8 us
  transfers between devices with their start and end apart: 38, of which 14 were waited for; matrix products, arithmetic and copies ran while one was open for 10% of the time, Pallas kernels for 35%

profile of v4, /device:TPU:0, one launch (start us, length us, event | category | flops | bytes accessed | tf_op | source)
XLA Modules:
  0.0 438.7 jit_solution(2711266796827117550)
XLA Ops:
  8.4 1.1 pad_maximum_fusion
  9.6 3.1 collective-permute-start.1
  12.7 27.7 %collective-permute-done.1 = bf16[512,1280]{1,0:T(8,128)(2,1)S(1)} collective-permute-done((bf16[512,1280]{1,0:T(8,128)(2,1)S(1)}, bf16[512,1280]{1,0:T(8,128)(2,1)S(1)}, u32[]{:S(2)}, u32[]{:S(2)}) %collective-permute-start.1) | collective-permute-done | bytes 1310752 | tf_op jit(solution)/shard_map/ppermute | solution.py:800
  40.4 1.9 broadcast_select_fusion.2.refs_0_.x_ref.refs_5_
  42.4 0.9 collective-permute-start.3
  43.3 1.9 broadcast_select_fusion.1.refs_2_.refs_5_
  45.2 19.5 %collective-permute-start.4 = (bf16[512,1280]{1,0:T(8,128)(2,1)S(1)}, bf16[512,1280]{1,0:T(8,128)(2,1)}, u32[]{:S(2)}, u32[]{:S(2)}) collective-permute-start(bf16[512,1280]{1,0:T(8,128)(2,1)S(1)} %broadcast_select_fusion.1.refs_2_.refs_5_), channel_id=1, source_target_pairs={{0,4},{1,5},{2,6},{3,7},{4,0},{5,1},{6,2},{7,3},{8,12},{9,13},{10,... | collective-permute-start | bytes 3932168 | tf_op jit(solution)/shard_map/ppermute | solution.py:800
  66.2 1.3 fusion.3.place_ref.refs_1_
  68.1 1.4 copy.31.col_ref.refs_3_
  69.5 1.7 collective-permute-start.5
  71.2 2.0 all-gather.3.cloned.1.call-done.refs_4_.refs_5_.refs_6_.refs_2_.refs_3_.refs_8_
  73.2 18.8 %project.1 = (bf16[640,1024]{1,0:T(8,128)(2,1)}, bf16[640,2048]{1,0:T(8,128)(2,1)}, bf16[640,2048]{1,0:T(8,128)(2,1)}, bf16[1280,2048]{1,0:T(8,128)(2,1)}) custom-call(s32[1]{0:T(128)} %bitcast.core_ref, f32[1,1280]{1,0:T(1,128)} %reshape.111.gain_ref.refs_4_, f32[640,1]{1,0:T(8,128)} %broadcast_multiply_fusion.scale_ref, bf16[512,1280]{1,0:T(8,128)(2,1)} %copy-done, ...), custom_call_target="tpu_custom_call" | custom-call | flops 8388608000 | bytes 65536 | tf_op jit(solution)/shard_map/project/pallas_call | solution.py:75
  92.0 24.2 %attention_forward.1 = (bf16[640,512]{1,0:T(8,128)(2,1)}, bf16[640,512]{1,0:T(8,128)(2,1)}, f32[8,1,1024]{2,1,0:T(1,128)}) custom-call(s32[2048]{0:T(1024)} %copy-done.24, s32[24]{0:T(128)} %fusion.3.place_ref.refs_1_, s32[1,2048]{1,0:T(1,128)} %bitcast.37, s32[2048,1]{1,0:T(8,128)} %copy.31.col_ref.refs_3_, ...), custom_call_target="tpu_custom_call" | custom-call | flops 10307921920 | bytes 65536 | tf_op jit(solution)/shard_map/attention_forward/pallas_call | solution.py:495
  116.2 2.2 collective-permute-start.6
  120.1 1.2 broadcast_select_fusion.cot_ref
  121.3 14.3 %all-gather.5.cloned.1.call-done.w_ref = bf16[1280,3840]{1,0:T(8,128)(2,1)} async-done(((bf16[160,3840]{1,0:T(8,128)(2,1)}), bf16[1280,3840]{1,0:T(8,128)(2,1)}) %all-gather.5.cloned.1.call-update) | async-done | bytes 9830416 | tf_op jit(solution)/shard_map/all_gather | solution.py:878
  135.6 0.8 copy-done.35
  136.4 20.7 %mlp.1 = (bf16[512,1280]{1,0:T(8,128)(2,1)}, bf16[640,512]{1,0:T(8,128)(2,1)}, bf16[640,512]{1,0:T(8,128)(2,1)}, f32[512,1280]{1,0:T(8,128)}, bf16[1280,512]{1,0...) custom-call(s32[1]{0:T(128)} %bitcast.core_ref, ...), custom_call_target="tpu_custom_call" | custom-call | flops 10066329600 | bytes 65536 | tf_op jit(solution)/shard_map/mlp/pallas_call | solution.py:185
  157.4 11.2 %mlp_weights.1 = bf16[1280,3840]{1,0:T(8,128)(2,1)} custom-call(s32[1]{0:T(128)} %bitcast.core_ref, bf16[640,512]{1,0:T(8,128)(2,1)} %get-tuple-element.108.near_ref.refs_9_, bf16[640,512]{1,0:T(8,128)(2,1)} %copy-done.35, bf16[1280,512]{1,0:T(8,128)(2,1)} %get-tuple-element.112.ht_ref, bf16[1280,512]{1,0:T(8,128)(2,1)} %get-tuple-element.113.nt_ref, ...), custom_call_target="tpu_custom_call" | custom-call | flops 5033164800 | bytes 20971520 | tf_op jit(solution)/shard_map/mlp_weights/pallas_call | solution.py:258
  171.0 22.8 %attention_backward.2 = (f32[640,1024]{1,0:T(8,128)}, bf16[640,1024]{1,0:T(8,128)(2,1)}, bf16[640,1024]{1,0:T(8,128)(2,1)}) custom-call(s32[2048]{0:T(1024)} %copy-done.24, s32[24]{0:T(128)} %fusion.3.place_ref.refs_1_, s32[1,2048]{1,0:T(1,128)} %bitcast.38, s32[2048,1]{1,0:T(8,128)} %copy.31.col_ref.refs_3_, ...), custom_call_target="tpu_custom_call" | custom-call | flops 12884901888 | bytes 16777216 | tf_op jit(solution)/shard_map/attention_backward/pallas_call | solution.py:537
  193.7 12.9 %input_gradient.2 = (bf16[512,1280]{1,0:T(8,128)(2,1)}, bf16[512,1280]{1,0:T(8,128)(2,1)}, f32[1,1280]{1,0:T(1,128)}) custom-call(s32[1]{0:T(128)} %bitcast.core_ref, bf16[640,1024]{1,0:T(8,128)(2,1)} %get-tuple-element.122.refs_0_.dkb_ref, bf16[640,1024]{1,0:T(8,128)(2,1)} %get-tuple-element.123.refs_1_.dvb_ref, ...), custom_call_target="tpu_custom_call" | custom-call | flops 3355443200 | bytes 65536 | tf_op jit(solution)/shard_map/input_gradient/pallas_call | solution.py:681
  206.6 5.6 %collective-permute-start.9 = (bf16[512,1280]{1,0:T(8,128)(2,1)}, bf16[512,1280]{1,0:T(8,128)(2,1)S(1)}, u32[]{:S(2)}, u32[]{:S(2)}) collective-permute-start(bf16[512,1280]{1,0:T(8,128)(2,1)} %get-tuple-element.128), channel_id=1, source_target_pairs={{0,4},{1,5},{2,6},{3,7},{4,0},{5,1},{6,2},{7,3},{8,12},{9,13},{10,... | collective-permute-start | bytes 3932168 | tf_op jit(solution)/shard_map/ppermute | solution.py:800
  212.2 2.9 collective-permute-done.9
  215.1 1.7 add_convert_fusion
  216.8 26.7 %attention_backward.3 = (bf16[640,1024]{1,0:T(8,128)(2,1)}, bf16[640,1024]{1,0:T(8,128)(2,1)}, bf16[640,1024]{1,0:T(8,128)(2,1)}, f32[640,1]{1,0:T(8,128)}) custom-call(s32[2048]{0:T(1024)} %copy-done.24, s32[24]{0:T(128)} %fusion.3.place_ref.refs_1_, s32[1,2048]{1,0:T(1,128)} %bitcast.39, s32[2048,1]{1,0:T(8,128)} %copy.31.col_ref.refs_3_, ...), custom_call_target="tpu_custom_call" | custom-call | flops 12884901888 | bytes 16777216 | tf_op jit(solution)/shard_map/attention_backward/pallas_call | solution.py:537
  243.6 4.4 %collective-permute-done.10 = bf16[512,1280]{1,0:T(8,128)(2,1)} collective-permute-done((bf16[512,1280]{1,0:T(8,128)(2,1)S(1)}, bf16[512,1280]{1,0:T(8,128)(2,1)}, u32[]{:S(2)}, u32[]{:S(2)}) %collective-permute-start.10) | collective-permute-done | bytes 1310752 | tf_op jit(solution)/shard_map/ppermute | solution.py:800
  248.0 3.6 collective-permute-start.11
  252.2 11.2 %weight_gradient.2 = (bf16[320,960]{1,0:T(8,128)(2,1)}, bf16[320,960]{1,0:T(8,128)(2,1)}, bf16[320,960]{1,0:T(8,128)(2,1)}, bf16[320,960]{1,0:T(8,128)(2,1)}) custom-call(s32[4]{0:T(128)} %pad_add_fusion.at_ref, bf16[1280,2048]{1,0:T(8,128)(2,1)} %get-tuple-element.139.xt_ref, bf16[640,1024]{1,0:T(8,128)(2,1)} %get-tuple-element.164.dqt_ref.refs_7_, ...), custom_call_target="tpu_custom_call" | custom-call | flops 4194304000 | bytes 12582912 | tf_op jit(solution)/shard_map/weight_gradient/pallas_call | solution.py:590
  263.4 1.4 collective-permute-start.12
  265.4 1.5 collective-permute-start.14
  267.3 14.9 %input_gradient.3 = (bf16[512,1280]{1,0:T(8,128)(2,1)}, bf16[512,1280]{1,0:T(8,128)(2,1)}, f32[1,1280]{1,0:T(1,128)}) custom-call(s32[1]{0:T(128)} %bitcast.core_ref, bf16[640,1024]{1,0:T(8,128)(2,1)} %get-tuple-element.136.dka_ref.refs_0_, bf16[640,1024]{1,0:T(8,128)(2,1)} %get-tuple-element.137.dva_ref.refs_1_, ...), custom_call_target="tpu_custom_call" | custom-call | flops 5033164800 | bytes 65536 | tf_op jit(solution)/shard_map/input_gradient/pallas_call | solution.py:681
  282.3 12.7 %collective-permute-done.13 = bf16[320,960]{1,0:T(8,128)(2,1)S(1)} collective-permute-done((bf16[320,960]{1,0:T(8,128)(2,1)}, bf16[320,960]{1,0:T(8,128)(2,1)S(1)}, u32[]{:S(2)}, u32[]{:S(2)}) %collective-permute-start.13) | collective-permute-done | bytes 614432 | tf_op jit(solution)/shard_map/ppermute | solution.py:800
  296.4 3.0 add_convert_fusion.2
  300.1 1.3 fusion
  301.4 1.3 collective-permute-start.16
  302.8 1.7 collective-permute-start.21
  304.5 1.4 collective-permute-start.19
  306.0 11.1 %weight_gradient.3 = (bf16[320,960]{1,0:T(8,128)(2,1)}, bf16[320,960]{1,0:T(8,128)(2,1)}, bf16[320,960]{1,0:T(8,128)(2,1)}, bf16[320,960]{1,0:T(8,128)(2,1)}) custom-call(s32[4]{0:T(128)} %pad_add_fusion.at_ref, bf16[1280,2048]{1,0:T(8,128)(2,1)} %get-tuple-element.139.xt_ref, bf16[640,1024]{1,0:T(8,128)(2,1)} %get-tuple-element.164.dqt_ref.refs_7_, ...), custom_call_target="tpu_custom_call" | custom-call | flops 4194304000 | bytes 12582912 | tf_op jit(solution)/shard_map/weight_gradient/pallas_call | solution.py:590
  317.3 0.8 copy-done.19
  318.6 2.5 add_convert_fusion.6
  321.8 1.4 collective-permute-start.22
  323.9 1.5 collective-permute-start.24
  325.3 3.3 fusion.2
  328.7 1.9 collective-permute-start.28
  330.6 9.2 %collective-permute-done.22 = bf16[320,960]{1,0:T(8,128)(2,1)S(1)} collective-permute-done((bf16[320,960]{1,0:T(8,128)(2,1)}, bf16[320,960]{1,0:T(8,128)(2,1)S(1)}, u32[]{:S(2)}, u32[]{:S(2)}) %collective-permute-start.22) | collective-permute-done | bytes 614432 | tf_op jit(solution)/shard_map/ppermute | solution.py:800
  339.7 13.4 %collective-permute-done.23 = bf16[320,960]{1,0:T(8,128)(2,1)S(1)} collective-permute-done((bf16[320,960]{1,0:T(8,128)(2,1)}, bf16[320,960]{1,0:T(8,128)(2,1)S(1)}, u32[]{:S(2)}, u32[]{:S(2)}) %collective-permute-start.23) | collective-permute-done | bytes 614432 | tf_op jit(solution)/shard_map/ppermute | solution.py:800
  353.9 9.3 %collective-permute-start.25 = (bf16[320,960]{1,0:T(8,128)(2,1)S(1)}, bf16[320,960]{1,0:T(8,128)(2,1)S(1)}, u32[]{:S(2)}, u32[]{:S(2)}) collective-permute-start(bf16[320,960]{1,0:T(8,128)(2,1)S(1)} %fusion.1), channel_id=1, source_target_pairs={{0,1},{3,2},{4,5},{7,6},{8,9},{11,10},{12,13},{15,14},{16,17},{19,... | collective-permute-start | bytes 1843208 | tf_op jit(solution)/shard_map/ppermute | solution.py:800
  363.2 1.3 collective-permute-start.26
  364.5 3.0 add_convert_fusion.1
  367.4 1.3 collective-permute-start.31
  368.7 14.0 %collective-permute-done.26 = bf16[320,960]{1,0:T(8,128)(2,1)S(1)} collective-permute-done((bf16[320,960]{1,0:T(8,128)(2,1)S(1)}, bf16[320,960]{1,0:T(8,128)(2,1)S(1)}, u32[]{:S(2)}, u32[]{:S(2)}) %collective-permute-start.26) | collective-permute-done | bytes 614432 | tf_op jit(solution)/shard_map/ppermute | solution.py:800
  382.8 1.5 add_convert_fusion.4
  384.3 1.5 collective-permute-start.27
  385.8 2.5 select_bitcast_fusion.1
  388.4 1.5 add_convert_fusion.3
  390.0 1.4 collective-permute-start.30
  391.4 17.8 %collective-permute-done.31 = bf16[160,3840]{1,0:T(8,128)(2,1)} collective-permute-done((bf16[160,3840]{1,0:T(8,128)(2,1)}, bf16[160,3840]{1,0:T(8,128)(2,1)}, u32[]{:S(2)}, u32[]{:S(2)}) %collective-permute-start.31) | collective-permute-done | bytes 1228832 | tf_op jit(solution)/shard_map/ppermute | solution.py:800
  409.2 1.4 broadcast_select_fusion.3
  410.6 4.1 select_bitcast_fusion
  415.0 5.9 %collective-permute-done.30 = bf16[320,960]{1,0:T(8,128)(2,1)S(1)} collective-permute-done((bf16[320,960]{1,0:T(8,128)(2,1)S(1)}, bf16[320,960]{1,0:T(8,128)(2,1)S(1)}, u32[]{:S(2)}, u32[]{:S(2)}) %collective-permute-start.30) | collective-permute-done | bytes 614432 | tf_op jit(solution)/shard_map/ppermute | solution.py:800
  421.8 1.5 fusion.7
  423.3 2.7 collective-permute-done.34
  427.4 2.7 concatenate.14
  430.1 1.6 concatenate.15
  (160 shorter events, 17.3 us)
Async XLA Ops:
  7.2 65.9 %all-gather.3.cloned.1.call-start = ((), (), s32[]{:S(2)}) async-start(), calls=%async_computation.1 | async-start | bytes 11059200 | tf_op jit(solution)/shard_map/all_gather | solution.py:863
  8.0 127.6 %all-gather.5.cloned.1.call-start = ((), (), s32[]{:S(2)}) async-start(), calls=%async_computation.2 | async-start | bytes 11059200 | tf_op jit(solution)/shard_map/all_gather | solution.py:878
  9.6 238.4 %reduce-scatter.2.cloned.1.call-start = ((), (), s32[]{:S(2)}) async-start(), calls=%async_computation.3 | async-start | bytes 11059200 | tf_op jit(solution)/shard_map/reduce_scatter | solution.py:901
  9.6 30.7 %collective-permute-start.1 = (bf16[512,1280]{1,0:T(8,128)(2,1)S(1)}, bf16[512,1280]{1,0:T(8,128)(2,1)S(1)}, u32[]{:S(2)}, u32[]{:S(2)}) collective-permute-start(bf16[512,1280]{1,0:T(8,128)(2,1)S(1)} %bitcast.33), channel_id=1, source_target_pairs={{0,1},{1,0},{2,5},{3,4},{4,3},{5,2},{6,7},{7,6},{8,9},{9,8},{10,13... | collective-permute-start | bytes 3932168 | tf_op jit(solution)/shard_map/ppermute | solution.py:800
  42.3 22.4 %copy-start = (bf16[512,1280]{1,0:T(8,128)(2,1)}, bf16[512,1280]{1,0:T(8,128)(2,1)S(1)}, u32[]{:S(2)}) copy-start(bf16[512,1280]{1,0:T(8,128)(2,1)S(1)} %broadcast_select_fusion.2.refs_0_.x_ref.refs_5_) | copy-start | bytes 3932164
  42.3 22.4 %copy-start.25 = (s32[1,2048]{1,0:T(1,128)S(1)}, s32[1,2048]{1,0:T(1,128)}, u32[]{:S(2)}) copy-start(s32[1,2048]{1,0:T(1,128)} %param.14) | copy-start | bytes 24580
  42.3 22.9 %copy-start.36 = (bf16[80]{0:T(256)(128)(2,1)S(1)}, bf16[80]{0:T(256)(128)(2,1)}, u32[]{:S(2)}) copy-start(bf16[80]{0:T(256)(128)(2,1)} %param.23) | copy-start | bytes 484
  42.4 25.1 %copy-start.30 = (bf16[1280]{0:T(1024)(128)(2,1)S(1)}, bf16[1280]{0:T(1024)(128)(2,1)}, u32[]{:S(2)}) copy-start(bf16[1280]{0:T(1024)(128)(2,1)} %param.19) | copy-start | bytes 7684
  42.4 0.9 collective-permute-start.3
  45.2 28.0 %copy-start.1 = (bf16[512,1280]{1,0:T(8,128)(2,1)}, bf16[512,1280]{1,0:T(8,128)(2,1)S(1)}, u32[]{:S(2)}) copy-start(bf16[512,1280]{1,0:T(8,128)(2,1)S(1)} %broadcast_select_fusion.1.refs_2_.refs_5_) | copy-start | bytes 3932164
  45.2 24.3 %collective-permute-start.4 = (bf16[512,1280]{1,0:T(8,128)(2,1)S(1)}, bf16[512,1280]{1,0:T(8,128)(2,1)}, u32[]{:S(2)}, u32[]{:S(2)}) collective-permute-start(bf16[512,1280]{1,0:T(8,128)(2,1)S(1)} %broadcast_select_fusion.1.refs_2_.refs_5_), channel_id=1, source_target_pairs={{0,4},{1,5},{2,6},{3,7},{4,0},{5,1},{6,2},{7,3},{8,12},{9,13},{10,... | collective-permute-start | bytes 3932168 | tf_op jit(solution)/shard_map/ppermute | solution.py:800
  64.7 6.5 %collective-permute-start.2 = (bf16[512,1280]{1,0:T(8,128)(2,1)S(1)}, bf16[512,1280]{1,0:T(8,128)(2,1)}, u32[]{:S(2)}, u32[]{:S(2)}) collective-permute-start(bf16[512,1280]{1,0:T(8,128)(2,1)S(1)} %broadcast_select_fusion.2.refs_0_.x_ref.refs_5_), channel_id=1, source_target_pairs={{0,4},{1,5},{2,6},{3,7},{4,0},{5,1},{6,2},{7,3},{8,12},{9,13},{10,... | collective-permute-start | bytes 3932168 | tf_op jit(solution)/shard_map/ppermute | solution.py:800
  64.8 3.3 collective-permute-start
  65.4 26.5 %copy-start.18 = (f32[640,1]{1,0:T(8,128)}, f32[640,1]{1,0:T(8,128)S(1)}, u32[]{:S(2)}) copy-start(f32[640,1]{1,0:T(8,128)S(1)} %broadcast_in_dim_tile.4.refs_13_) | copy-start | bytes 7684
  68.1 23.8 %copy-start.24 = (s32[2048]{0:T(1024)}, s32[2048]{0:T(1024)S(1)}, u32[]{:S(2)}) copy-start(s32[2048]{0:T(1024)S(1)} %broadcast_select_fusion.10.ids_ref.refs_0_) | copy-start | bytes 24580
  69.5 46.7 %collective-permute-start.5 = (bf16[512,1280]{1,0:T(8,128)(2,1)}, bf16[512,1280]{1,0:T(8,128)(2,1)}, u32[]{:S(2)}, u32[]{:S(2)}) collective-permute-start(bf16[512,1280]{1,0:T(8,128)(2,1)} %bitcast.34), channel_id=1, source_target_pairs={{2,5},{3,4},{4,3},{5,2},{10,13},{11,12},{12,11},{13,10},{18,21},{1... | collective-permute-start | bytes 3932168 | tf_op jit(solution)/shard_map/ppermute | solution.py:800
  91.9 26.4 %copy-start.31 = (bf16[1280]{0:T(1024)(128)(2,1)S(1)}, bf16[1280]{0:T(1024)(128)(2,1)}, u32[]{:S(2)}) copy-start(bf16[1280]{0:T(1024)(128)(2,1)} %param.20) | copy-start | bytes 7684
  91.9 27.0 %copy-start.32 = (bf16[1280]{0:T(1024)(128)(2,1)S(1)}, bf16[1280]{0:T(1024)(128)(2,1)}, u32[]{:S(2)}) copy-start(bf16[1280]{0:T(1024)(128)(2,1)} %param.21) | copy-start | bytes 7684
  91.9 27.6 %copy-start.33 = (bf16[1280]{0:T(1024)(128)(2,1)S(1)}, bf16[1280]{0:T(1024)(128)(2,1)}, u32[]{:S(2)}) copy-start(bf16[1280]{0:T(1024)(128)(2,1)} %param.22) | copy-start | bytes 7684
  91.9 28.2 %copy-start.15 = (bf16[1,512,1280]{2,1,0:T(8,128)(2,1)S(1)}, bf16[1,512,1280]{2,1,0:T(8,128)(2,1)}, u32[]{:S(2)}) copy-start(bf16[1,512,1280]{2,1,0:T(8,128)(2,1)} %param.24) | copy-start | bytes 3932164
  116.2 19.4 %collective-permute-start.6 = (bf16[640,512]{1,0:T(8,128)(2,1)}, bf16[640,512]{1,0:T(8,128)(2,1)S(1)}, u32[]{:S(2)}, u32[]{:S(2)}) collective-permute-start(bf16[640,512]{1,0:T(8,128)(2,1)} %get-tuple-element.109.refs_10_), channel_id=1, source_target_pairs={{0,4},{1,5},{2,6},{3,7},{4,0},{5,1},{6,2},{7,3},{8,12},{9,13},{10,... | collective-permute-start | bytes 1966088 | tf_op jit(solution)/shard_map/ppermute | solution.py:800
  157.1 11.6 %collective-permute-start.7 = (bf16[640,512]{1,0:T(8,128)(2,1)}, bf16[640,512]{1,0:T(8,128)(2,1)S(1)}, u32[]{:S(2)}, u32[]{:S(2)}) collective-permute-start(bf16[640,512]{1,0:T(8,128)(2,1)} %get-tuple-element.116), channel_id=1, source_target_pairs={{0,4},{1,5},{2,6},{3,7},{4,0},{5,1},{6,2},{7,3},{8,12},{9,13},{10,... | collective-permute-start | bytes 1966088 | tf_op jit(solution)/shard_map/ppermute | solution.py:800
  170.2 36.4 %collective-permute-start.8 = (bf16[512,1280]{1,0:T(8,128)(2,1)S(1)}, bf16[512,1280]{1,0:T(8,128)(2,1)S(1)}, u32[]{:S(2)}, u32[]{:S(2)}) collective-permute-start(bf16[512,1280]{1,0:T(8,128)(2,1)S(1)} %copy-done.16), channel_id=1, source_target_pairs={{2,5},{3,4},{4,3},{5,2},{10,13},{11,12},{12,11},{13,10},{18,21},{1... | collective-permute-start | bytes 3932168 | tf_op jit(solution)/shard_map/ppermute | solution.py:800
  206.6 10.1 %copy-start.17 = (bf16[512,1280]{1,0:T(8,128)(2,1)}, bf16[512,1280]{1,0:T(8,128)(2,1)S(1)}, u32[]{:S(2)}) copy-start(bf16[512,1280]{1,0:T(8,128)(2,1)S(1)} %collective-permute-done.8) | copy-start | bytes 3932164
  206.6 8.4 %collective-permute-start.9 = (bf16[512,1280]{1,0:T(8,128)(2,1)}, bf16[512,1280]{1,0:T(8,128)(2,1)S(1)}, u32[]{:S(2)}, u32[]{:S(2)}) collective-permute-start(bf16[512,1280]{1,0:T(8,128)(2,1)} %get-tuple-element.128), channel_id=1, source_target_pairs={{0,4},{1,5},{2,6},{3,7},{4,0},{5,1},{6,2},{7,3},{8,12},{9,13},{10,... | collective-permute-start | bytes 3932168 | tf_op jit(solution)/shard_map/ppermute | solution.py:800
  216.8 31.2 %collective-permute-start.10 = (bf16[512,1280]{1,0:T(8,128)(2,1)S(1)}, bf16[512,1280]{1,0:T(8,128)(2,1)}, u32[]{:S(2)}, u32[]{:S(2)}) collective-permute-start(bf16[512,1280]{1,0:T(8,128)(2,1)S(1)} %add_convert_fusion), channel_id=1, source_target_pairs={{0,1},{1,0},{2,3},{3,2},{4,5},{5,4},{6,7},{7,6},{8,9},{9,8},{10,11... | collective-permute-start | bytes 3932168 | tf_op jit(solution)/shard_map/ppermute | solution.py:800
  248.0 47.0 %collective-permute-start.11 = (bf16[160,3840]{1,0:T(8,128)(2,1)}, bf16[160,3840]{1,0:T(8,128)(2,1)}, u32[]{:S(2)}, u32[]{:S(2)}) collective-permute-start(bf16[160,3840]{1,0:T(8,128)(2,1)} %reduce-scatter.2.cloned.1.call-done), channel_id=1, source_target_pairs={{0,1},{3,2},{4,5},{7,6},{8,9},{11,10},{12,13},{15,14},{16,17},{19,... | collective-permute-start | bytes 3686408 | tf_op jit(solution)/shard_map/ppermute | solution.py:800
  252.2 14.7 %copy-start.28 = (f32[1,1280]{1,0:T(1,128)S(1)}, f32[1,1280]{1,0:T(1,128)}, u32[]{:S(2)}) copy-start(f32[1,1280]{1,0:T(1,128)} %get-tuple-element.160) | copy-start | bytes 15364
  252.2 14.7 %copy-start.27 = (f32[1,1280]{1,0:T(1,128)S(1)}, f32[1,1280]{1,0:T(1,128)}, u32[]{:S(2)}) copy-start(f32[1,1280]{1,0:T(1,128)} %get-tuple-element.161) | copy-start | bytes 15364
  252.2 14.7 %copy-start.26 = (f32[1,1280]{1,0:T(1,128)S(1)}, f32[1,1280]{1,0:T(1,128)}, u32[]{:S(2)}) copy-start(f32[1,1280]{1,0:T(1,128)} %get-tuple-element.162) | copy-start | bytes 15364
  252.2 14.8 %copy-start.23 = (f32[640,1]{1,0:T(8,128)S(1)}, f32[640,1]{1,0:T(8,128)}, u32[]{:S(2)}) copy-start(f32[640,1]{1,0:T(8,128)} %get-tuple-element.163) | copy-start | bytes 7684
  263.4 18.8 %collective-permute-start.12 = (bf16[320,960]{1,0:T(8,128)(2,1)}, bf16[320,960]{1,0:T(8,128)(2,1)S(1)}, u32[]{:S(2)}, u32[]{:S(2)}) collective-permute-start(bf16[320,960]{1,0:T(8,128)(2,1)} %get-tuple-element.149), channel_id=1, source_target_pairs={{0,8},{1,9},{2,10},{3,11},{4,12},{5,13},{6,14},{7,15},{8,0},{9,1},... | collective-permute-start | bytes 1843208 | tf_op jit(solution)/shard_map/ppermute | solution.py:800
  264.8 30.2 %collective-permute-start.13 = (bf16[320,960]{1,0:T(8,128)(2,1)}, bf16[320,960]{1,0:T(8,128)(2,1)S(1)}, u32[]{:S(2)}, u32[]{:S(2)}) collective-permute-start(bf16[320,960]{1,0:T(8,128)(2,1)} %get-tuple-element.150), channel_id=1, source_target_pairs={{0,16},{1,17},{2,18},{3,19},{4,20},{5,21},{6,22},{7,23},{8,24},{9,... | collective-permute-start | bytes 1843208 | tf_op jit(solution)/shard_map/ppermute | solution.py:800
  265.4 29.5 %collective-permute-start.14 = (bf16[320,960]{1,0:T(8,128)(2,1)}, bf16[320,960]{1,0:T(8,128)(2,1)S(1)}, u32[]{:S(2)}, u32[]{:S(2)}) collective-permute-start(bf16[320,960]{1,0:T(8,128)(2,1)} %get-tuple-element.151), channel_id=1, source_target_pairs={{0,24},{1,25},{2,26},{3,27},{4,28},{5,29},{6,30},{7,31},{8,16},{9,... | collective-permute-start | bytes 1843208 | tf_op jit(solution)/shard_map/ppermute | solution.py:800
  267.3 27.7 %copy-start.29 = (f32[1,1280]{1,0:T(1,128)S(1)}, f32[1,1280]{1,0:T(1,128)}, u32[]{:S(2)}) copy-start(f32[1,1280]{1,0:T(1,128)} %get-tuple-element.158) | copy-start | bytes 15364
  282.2 17.9 %copy-start.9 = (bf16[320,960]{1,0:T(8,128)(2,1)}, bf16[320,960]{1,0:T(8,128)(2,1)S(1)}, u32[]{:S(2)}) copy-start(bf16[320,960]{1,0:T(8,128)(2,1)S(1)} %collective-permute-done.12) | copy-start | bytes 1843204
  294.9 5.2 %copy-start.10 = (bf16[320,960]{1,0:T(8,128)(2,1)}, bf16[320,960]{1,0:T(8,128)(2,1)S(1)}, u32[]{:S(2)}) copy-start(bf16[320,960]{1,0:T(8,128)(2,1)S(1)} %collective-permute-done.13) | copy-start | bytes 1843204
  295.8 4.3 copy-start.8
  295.8 3.5 collective-permute-start.17
  295.9 4.2 copy-start.12
  295.9 21.4 %collective-permute-start.15 = (bf16[512,1280]{1,0:T(8,128)(2,1)}, bf16[512,1280]{1,0:T(8,128)(2,1)S(1)}, u32[]{:S(2)}, u32[]{:S(2)}) collective-permute-start(bf16[512,1280]{1,0:T(8,128)(2,1)} %get-tuple-element.153), channel_id=1, source_target_pairs={{0,4},{1,5},{2,6},{3,7},{4,0},{5,1},{6,2},{7,3},{8,12},{9,13},{10,... | collective-permute-start | bytes 3932168 | tf_op jit(solution)/shard_map/ppermute | solution.py:800
  299.4 5.1 %collective-permute-start.18 = (f32[48,128]{1,0:T(8,128)S(1)}, f32[48,128]{1,0:T(8,128)S(1)}, u32[]{:S(2)}, u32[]{:S(2)}) collective-permute-start(f32[48,128]{1,0:T(8,128)S(1)} %fusion.6), channel_id=1, source_target_pairs={{0,8},{1,9},{2,10},{3,11},{4,12},{5,13},{6,14},{7,15},{8,0},{9,1},... | collective-permute-start | bytes 73736 | tf_op jit(solution)/shard_map/ppermute | solution.py:800
  301.4 15.9 %collective-permute-start.16 = (bf16[320,960]{1,0:T(8,128)(2,1)}, bf16[320,960]{1,0:T(8,128)(2,1)S(1)}, u32[]{:S(2)}, u32[]{:S(2)}) collective-permute-start(bf16[320,960]{1,0:T(8,128)(2,1)} %fusion), channel_id=1, source_target_pairs={{0,1},{3,2},{4,5},{7,6},{8,9},{11,10},{12,13},{15,14},{16,17},{19,... | collective-permute-start | bytes 1843208 | tf_op jit(solution)/shard_map/ppermute | solution.py:800
  302.8 25.9 %collective-permute-start.21 = (bf16[160,3840]{1,0:T(8,128)(2,1)}, bf16[160,3840]{1,0:T(8,128)(2,1)}, u32[]{:S(2)}, u32[]{:S(2)}) collective-permute-start(bf16[160,3840]{1,0:T(8,128)(2,1)} %add_convert_fusion.2), channel_id=1, source_target_pairs={{1,2},{2,1},{5,6},{6,5},{9,10},{10,9},{13,14},{14,13},{17,18},{18,... | collective-permute-start | bytes 3686408 | tf_op jit(solution)/shard_map/ppermute | solution.py:800
  304.5 12.5 %collective-permute-start.19 = (f32[48,128]{1,0:T(8,128)S(1)}, f32[48,128]{1,0:T(8,128)S(1)}, u32[]{:S(2)}, u32[]{:S(2)}) collective-permute-start(f32[48,128]{1,0:T(8,128)S(1)} %fusion.12), channel_id=1, source_target_pairs={{0,16},{1,17},{2,18},{3,19},{4,20},{5,21},{6,22},{7,23},{8,24},{9,... | collective-permute-start | bytes 73736 | tf_op jit(solution)/shard_map/ppermute | solution.py:800
  318.6 6.8 %copy-start.2 = (f32[512,1280]{1,0:T(8,128)S(1)}, f32[512,1280]{1,0:T(8,128)}, u32[]{:S(2)}) copy-start(f32[512,1280]{1,0:T(8,128)} %get-tuple-element.170) | copy-start | bytes 7864324
  318.6 6.8 %copy-start.4 = (bf16[512,1280]{1,0:T(8,128)(2,1)S(1)}, bf16[512,1280]{1,0:T(8,128)(2,1)}, u32[]{:S(2)}) copy-start(bf16[512,1280]{1,0:T(8,128)(2,1)} %get-tuple-element.152) | copy-start | bytes 3932164
  321.1 9.5 %collective-permute-start.20 = (bf16[320,960]{1,0:T(8,128)(2,1)S(1)}, bf16[320,960]{1,0:T(8,128)(2,1)S(1)}, u32[]{:S(2)}, u32[]{:S(2)}) collective-permute-start(bf16[320,960]{1,0:T(8,128)(2,1)S(1)} %add_convert_fusion.6), channel_id=1, source_target_pairs={{1,2},{2,1},{5,6},{6,5},{9,10},{10,9},{13,14},{14,13},{17,18},{18,... | collective-permute-start | bytes 1843208 | tf_op jit(solution)/shard_map/ppermute | solution.py:800
  321.8 17.9 %collective-permute-start.22 = (bf16[320,960]{1,0:T(8,128)(2,1)}, bf16[320,960]{1,0:T(8,128)(2,1)S(1)}, u32[]{:S(2)}, u32[]{:S(2)}) collective-permute-start(bf16[320,960]{1,0:T(8,128)(2,1)} %get-tuple-element.175), channel_id=1, source_target_pairs={{0,8},{1,9},{2,10},{3,11},{4,12},{5,13},{6,14},{7,15},{8,0},{9,1},... | collective-permute-start | bytes 1843208 | tf_op jit(solution)/shard_map/ppermute | solution.py:800
  323.2 29.9 %collective-permute-start.23 = (bf16[320,960]{1,0:T(8,128)(2,1)}, bf16[320,960]{1,0:T(8,128)(2,1)S(1)}, u32[]{:S(2)}, u32[]{:S(2)}) collective-permute-start(bf16[320,960]{1,0:T(8,128)(2,1)} %get-tuple-element.176), channel_id=1, source_target_pairs={{0,16},{1,17},{2,18},{3,19},{4,20},{5,21},{6,22},{7,23},{8,24},{9,... | collective-permute-start | bytes 1843208 | tf_op jit(solution)/shard_map/ppermute | solution.py:800
  323.9 29.2 %collective-permute-start.24 = (bf16[320,960]{1,0:T(8,128)(2,1)}, bf16[320,960]{1,0:T(8,128)(2,1)S(1)}, u32[]{:S(2)}, u32[]{:S(2)}) collective-permute-start(bf16[320,960]{1,0:T(8,128)(2,1)} %get-tuple-element.177), channel_id=1, source_target_pairs={{0,24},{1,25},{2,26},{3,27},{4,28},{5,29},{6,30},{7,31},{8,16},{9,... | collective-permute-start | bytes 1843208 | tf_op jit(solution)/shard_map/ppermute | solution.py:800
  328.7 24.7 %copy-start.13 = (bf16[320,960]{1,0:T(8,128)(2,1)S(1)}, bf16[320,960]{1,0:T(8,128)(2,1)}, u32[]{:S(2)}) copy-start(bf16[320,960]{1,0:T(8,128)(2,1)} %get-tuple-element.172) | copy-start | bytes 1843204
  328.7 59.6 %collective-permute-start.28 = (bf16[512,1280]{1,0:T(8,128)(2,1)}, bf16[512,1280]{1,0:T(8,128)(2,1)}, u32[]{:S(2)}, u32[]{:S(2)}) collective-permute-start(bf16[512,1280]{1,0:T(8,128)(2,1)} %fusion.2), channel_id=1, source_target_pairs={{2,5},{3,4},{4,3},{5,2},{10,13},{11,12},{12,11},{13,10},{18,21},{1... | collective-permute-start | bytes 3932168 | tf_op jit(solution)/shard_map/ppermute | solution.py:800
  353.9 29.0 %collective-permute-start.25 = (bf16[320,960]{1,0:T(8,128)(2,1)S(1)}, bf16[320,960]{1,0:T(8,128)(2,1)S(1)}, u32[]{:S(2)}, u32[]{:S(2)}) collective-permute-start(bf16[320,960]{1,0:T(8,128)(2,1)S(1)} %fusion.1), channel_id=1, source_target_pairs={{0,1},{3,2},{4,5},{7,6},{8,9},{11,10},{12,13},{15,14},{16,17},{19,... | collective-permute-start | bytes 1843208 | tf_op jit(solution)/shard_map/ppermute | solution.py:800
  363.2 19.6 %collective-permute-start.26 = (bf16[320,960]{1,0:T(8,128)(2,1)S(1)}, bf16[320,960]{1,0:T(8,128)(2,1)S(1)}, u32[]{:S(2)}, u32[]{:S(2)}) collective-permute-start(bf16[320,960]{1,0:T(8,128)(2,1)S(1)} %add_convert_fusion.5), channel_id=1, source_target_pairs={{1,0},{2,3},{5,4},{6,7},{9,8},{10,11},{13,12},{14,15},{17,16},{18,... | collective-permute-start | bytes 1843208 | tf_op jit(solution)/shard_map/ppermute | solution.py:800
  367.4 41.7 %collective-permute-start.31 = (bf16[160,3840]{1,0:T(8,128)(2,1)}, bf16[160,3840]{1,0:T(8,128)(2,1)}, u32[]{:S(2)}, u32[]{:S(2)}) collective-permute-start(bf16[160,3840]{1,0:T(8,128)(2,1)} %add_convert_fusion.1), channel_id=1, source_target_pairs={{1,0},{2,3},{5,4},{6,7},{9,8},{10,11},{13,12},{14,15},{17,16},{18,... | collective-permute-start | bytes 3686408 | tf_op jit(solution)/shard_map/ppermute | solution.py:800
  384.3 4.0 collective-permute-start.27
  388.3 26.4 %collective-permute-start.29 = (bf16[160,960]{1,0:T(8,128)(2,1)S(1)}, bf16[160,960]{1,0:T(8,128)(2,1)S(1)}, u32[]{:S(2)}, u32[]{:S(2)}) collective-permute-start(bf16[160,960]{1,0:T(8,128)(2,1)S(1)} %constant_dynamic-slice_fusion.1), channel_id=1, source_target_pairs={{0,4},{1,5},{2,6},{3,7},{4,0},{5,1},{6,2},{7,3},{8,12},{9,13},{10,... | collective-permute-start | bytes 921608 | tf_op jit(solution)/shard_map/ppermute | solution.py:800
  389.9 20.7 %copy-start.5 = (bf16[512,1280]{1,0:T(8,128)(2,1)S(1)}, bf16[512,1280]{1,0:T(8,128)(2,1)}, u32[]{:S(2)}) copy-start(bf16[512,1280]{1,0:T(8,128)(2,1)} %get-tuple-element.152) | copy-start | bytes 3932164
  390.0 20.7 %copy-start.7 = (bf16[512,1280]{1,0:T(8,128)(2,1)S(1)}, bf16[512,1280]{1,0:T(8,128)(2,1)}, u32[]{:S(2)}) copy-start(bf16[512,1280]{1,0:T(8,128)(2,1)} %copy-done.6) | copy-start | bytes 3932164
  390.0 30.9 %collective-permute-start.30 = (bf16[320,960]{1,0:T(8,128)(2,1)S(1)}, bf16[320,960]{1,0:T(8,128)(2,1)S(1)}, u32[]{:S(2)}, u32[]{:S(2)}) collective-permute-start(bf16[320,960]{1,0:T(8,128)(2,1)S(1)} %add_convert_fusion.3), channel_id=1, source_target_pairs={{1,0},{2,3},{5,4},{6,7},{9,8},{10,11},{13,12},{14,15},{17,16},{18,... | collective-permute-start | bytes 1843208 | tf_op jit(solution)/shard_map/ppermute | solution.py:800
  414.7 6.5 %collective-permute-start.32 = (f32[48,128]{1,0:T(8,128)S(1)}, f32[48,128]{1,0:T(8,128)S(1)}, u32[]{:S(2)}, u32[]{:S(2)}) collective-permute-start(f32[48,128]{1,0:T(8,128)S(1)} %add.109), channel_id=1, source_target_pairs={{0,1},{1,0},{2,3},{3,2},{4,5},{5,4},{6,7},{7,6},{8,9},{9,8},{10,11... | collective-permute-start | bytes 73736 | tf_op jit(solution)/shard_map/ppermute | solution.py:800
  421.2 4.7 %collective-permute-start.34 = (f32[48,128]{1,0:T(8,128)S(1)}, f32[48,128]{1,0:T(8,128)S(1)}, u32[]{:S(2)}, u32[]{:S(2)}) collective-permute-start(f32[48,128]{1,0:T(8,128)S(1)} %add.124), channel_id=1, source_target_pairs={{0,2},{1,3},{2,0},{3,1},{4,6},{5,7},{6,4},{7,5},{8,10},{9,11},{10,... | collective-permute-start | bytes 73736 | tf_op jit(solution)/shard_map/ppermute | solution.py:800
  421.7 5.4 %collective-permute-start.33 = (bf16[160,960]{1,0:T(8,128)(2,1)S(1)}, bf16[160,960]{1,0:T(8,128)(2,1)S(1)}, u32[]{:S(2)}, u32[]{:S(2)}) collective-permute-start(bf16[160,960]{1,0:T(8,128)(2,1)S(1)} %constant_dynamic-slice_fusion), channel_id=1, source_target_pairs={{0,4},{1,5},{2,6},{3,7},{4,0},{5,1},{6,2},{7,3},{8,12},{9,13},{10,... | collective-permute-start | bytes 921608 | tf_op jit(solution)/shard_map/ppermute | solution.py:800
  (11 other events, 13.1 us)
Sparse Core Ops, SparseCore 0:
  9.9 63.1 all-gather.2
  75.0 60.5 all-gather.4
  168.8 78.2 reduce-scatter.1
